TPU v7x, 32 devices: a whole 2x2x4 slice. The times are simulated.
32 devices in a mesh: grp: 2 (over x), pre: 2 (over core), head: 8 (over z, y).
Axes of the slice: x: 2, y: 2, z: 4, core: 2. Of those that a mesh axis runs over, the one named last changes fastest.
Arguments:
- hidden: bfloat16 [1024, 14336], P(('grp', 'pre'), 'head'), parts along dimension 0, may hold values from -6 to 6
- slot_tokens: int32 [1024], P('grp'), parts along dimension 0, may hold values from 0 to 511, each once
- lengths: int32 [4, 16], P(('grp', 'pre')), parts along dimension 0, may hold values from 1 to 64, 256 in all within a row
- decode_rows: bfloat16 [64, 4, 14336], P('grp', None, 'pre'), parts along dimension 0, may hold values from -52 to 52
- query_weight: bfloat16 [14336, 2048], P('pre', 'head'), may hold values from -0.046875 to 0.046875
- key_weight: bfloat16 [14336, 2048], P('pre', 'head'), may hold values from -0.046875 to 0.046875
- value_weight: bfloat16 [14336, 2048], P('pre', 'head'), may hold values from -0.046875 to 0.046875
Outputs:
- attended: bfloat16 [64, 4, 2048], P(('grp', 'pre'), None, 'head'), parts along dimension 0
There are 2 independent parts, one for each index of `grp`. A program takes and returns all parts, laid end to end along the dimension named above; an argument that names none is the same for every part. Nothing has to cross between parts.
Inputs may be any that keep to these rules, and one draw needn't show every extreme that they name: `slot_tokens`: each prompt token stands in exactly one cache slot. The lengths of one owner's requests add up to 256; in each row the longest is 64.
All inputs are finite; a program needn't handle non-finite values.
Results may differ from a plain program's by a relative error of at most 0.012.
The roundings to bfloat16 on the way count: a program that leaves them out, or rounds other values in their place, can miss the bound.
Values may be sent and summed in bfloat16 or wider, within the bound.
No kernel may reach another device: no remote copies, remote signals or barrier semaphores. Data moves between devices by JAX's collectives and lax.ppermute only.
A program may use at most 128 MiB of HBM per device.

v0:
```python
import jax
import jax.numpy as jnp
from jax import lax
from jax.sharding import PartitionSpec as P

HS = 128


def on_device(hidden, slot_tokens, lengths, decode_rows, query_weight, key_weight, value_weight):
    group = lax.axis_index("head")
    own_tok = hidden.shape[0]
    half = key_weight.shape[0]
    cols = key_weight.shape[1]
    heads_dev = cols // HS
    full_rows = lax.all_gather(hidden, "head", axis=1, tiled=True)
    halves = lax.all_to_all(full_rows, "pre", split_axis=1, concat_axis=0, tiled=True)
    rows = halves[slot_tokens]
    cache = lax.psum_scatter(
        jnp.concatenate(
            [
                jnp.dot(rows, key_weight, preferred_element_type=jnp.float32),
                jnp.dot(rows, value_weight, preferred_element_type=jnp.float32),
            ],
            axis=1,
        ),
        "pre",
        scatter_dimension=0,
        tiled=True,
    ).astype(jnp.bfloat16)
    key_cache = cache[:, :cols].reshape(own_tok, heads_dev, HS)
    value_cache = cache[:, cols:].reshape(own_tok, heads_dev, HS)
    req_dev = lengths.shape[1]
    steps = decode_rows.shape[1]
    rows = decode_rows.reshape(req_dev * lax.axis_size("pre") * steps, half)
    parts = [
        jnp.dot(rows, query_weight, preferred_element_type=jnp.float32),
        jnp.dot(rows, key_weight, preferred_element_type=jnp.float32),
        jnp.dot(rows, value_weight, preferred_element_type=jnp.float32),
    ]
    fresh = lax.psum_scatter(
        jnp.concatenate(parts, axis=1).reshape(req_dev * lax.axis_size("pre"), steps, 3 * cols),
        "pre",
        scatter_dimension=0,
        tiled=True,
    ).astype(jnp.bfloat16)
    query = fresh[:, :, :cols].reshape(req_dev, steps, heads_dev, HS)
    fresh_key = fresh[:, :, cols : 2 * cols].reshape(req_dev, steps, heads_dev, HS)
    fresh_value = fresh[:, :, 2 * cols :].reshape(req_dev, steps, heads_dev, HS)
    lens = lengths[0]
    starts = jnp.cumsum(lens) - lens
    heads_all = heads_dev * lax.axis_size("head")
    heads_index = (group * heads_dev + jnp.arange(heads_dev)).astype(jnp.float32)
    slope = jnp.exp2(-8.0 * (heads_index + 1.0) / heads_all)
    scale = 1.0 / HS**0.5
    step_index = jnp.arange(steps, dtype=jnp.int32)
    slot_index = jnp.arange(own_tok, dtype=jnp.int32)
    rel = slot_index[None, :] - starts[:, None]
    valid = (rel >= 0) & (rel < lens[:, None])
    dist = (lens[:, None, None] + step_index[None, :, None] - rel[:, None, :]).astype(jnp.float32)
    ctx = jnp.einsum("rshd,jhd->rshj", query, key_cache, preferred_element_type=jnp.float32) * scale
    ctx = ctx - slope[None, None, :, None] * dist[:, :, None, :]
    ctx = jnp.where(valid[:, None, None, :], ctx, -1e30)
    near = (
        jnp.einsum("rshd,rthd->rsht", query, fresh_key, preferred_element_type=jnp.float32) * scale
    )
    tdist = (step_index[:, None] - step_index[None, :]).astype(jnp.float32)
    near = near - slope[None, None, :, None] * tdist[None, :, None, :]
    near = jnp.where((step_index[None, :] <= step_index[:, None])[None, :, None, :], near, -1e30)
    top = jnp.maximum(jnp.max(ctx, axis=-1), jnp.max(near, axis=-1))
    part_ctx = jnp.exp(ctx - top[..., None])
    part_near = jnp.exp(near - top[..., None])
    total = jnp.sum(part_ctx, axis=-1) + jnp.sum(part_near, axis=-1)
    weight_ctx = (part_ctx / total[..., None]).astype(jnp.bfloat16)
    weight_near = (part_near / total[..., None]).astype(jnp.bfloat16)
    out = jnp.einsum("rshj,jhd->rshd", weight_ctx, value_cache, preferred_element_type=jnp.float32)
    out = out + jnp.einsum(
        "rsht,rthd->rshd", weight_near, fresh_value, preferred_element_type=jnp.float32
    )
    return out.reshape(req_dev, steps, cols).astype(jnp.bfloat16)


def solution(mesh):
    in_specs = (
        P(("grp", "pre"), "head"),
        P("grp"),
        P(("grp", "pre"), None),
        P("grp", None, "pre"),
        P("pre", "head"),
        P("pre", "head"),
        P("pre", "head"),
    )
    out_specs = P(("grp", "pre"), None, "head")
    return jax.shard_map(
        on_device, mesh=mesh, in_specs=in_specs, out_specs=out_specs, check_vma=False
    )
```

profile of v0, /device:TPU:0, one launch (start us, length us, event | category | flops | bytes accessed | tf_op | source)
XLA Modules:
  0.0 185.7 jit_solution(2308804484889503451)
XLA Ops:
  7.4 0.0 all-gather.2.cloned.1.call-start
  7.4 0.7 all-gather.2.cloned.1.call-update
  8.1 0.0 reduce-scatter.5.cloned.1.call-start
  8.1 2.9 %reshape.184 = bf16[128,7168]{1,0:T(8,128)(2,1)S(1)} reshape(bf16[32,4,7168]{2,1,0:T(4,128)(2,1)} %param.10) | data formatting | bytes 3670016 | tf_op jit(solution)/shard_map/reshape | solution.py:34
  11.1 0.0 copy-start.2
  11.1 2.8 %fusion.27 = f32[128,256]{1,0:T(8,128)S(1)} fusion(bf16[128,7168]{1,0:T(8,128)(2,1)S(1)} %reshape.184, bf16[7168,256]{1,0:T(8,128)(2,1)} %param.13), kind=kOutput, calls=%fused_computation.50 | convolution fusion | flops 469762048 | bytes 5636096 | tf_op jit(solution)/shard_map/dot_general | solution.py:38
  13.9 0.3 copy-done.2
  14.2 0.0 copy-start.1
  14.2 0.7 fusion.26
  14.9 1.3 copy-done.1
  16.3 0.0 copy-start.5
  16.3 0.0 copy-start.4
  16.3 0.7 fusion.25
  17.0 0.1 reshape.185
  17.1 0.8 copy.62
  18.0 0.0 reduce-scatter.5.cloned.1.call-update
  18.0 0.0 reduce-scatter.3.cloned.1.call-start
  18.1 0.0 copy-done.5
  18.1 0.0 copy-done.4
  18.1 0.1 copy.61
  18.2 0.1 reduce
  18.3 107.3 %all-gather.2.cloned.1.call-done = bf16[256,14336]{1,0:T(8,128)(2,1)} async-done(((bf16[256,1792]{1,0:T(8,128)(2,1)}), bf16[256,14336]{1,0:T(8,128)(2,1)}) %all-gather.2.cloned.1.call-update) | async-done | bytes 7340048 | tf_op jit(solution)/shard_map/all_gather | solution.py:15
  125.6 3.6 %copy.106 = bf16[32,2,8,7168]{3,2,0,1:T(8,128)(2,1)S(1)} copy(bf16[32,2,8,7168]{3,2,1,0:T(8,128)(2,1)} %bitcast.67) | data formatting | bytes 14680064 | tf_op jit(solution)/shard_map/all_to_all | solution.py:16
  129.3 10.9 %all_to_all.19 = bf16[256,2,7168]{2,0,1:T(8,128)(2,1)} all-to-all(bf16[256,2,7168]{2,0,1:T(8,128)(2,1)S(1)} %bitcast.66), channel_id=1, replica_groups=mesh['grp'=2,'pre'=2,'head'=8] {'pre'}, dimensions={1} | all-to-all | bytes 14680064 | tf_op jit(solution)/shard_map/all_to_all | solution.py:16
  140.1 17.9 %gather_fusion = bf16[512,7168]{1,0:T(8,128)(2,1)} fusion(bf16[512,7168]{1,0:T(8,128)(2,1)} %bitcast.65, s32[1024]{0:T(1024)S(1)} %pad_clamp_fusion), kind=kCustom, calls=%fused_computation | custom fusion | bytes 14682112 | tf_op jit(solution)/shard_map/gather | solution.py:17
  158.0 0.0 copy-start
  158.0 0.0 copy-start.3
  158.1 6.4 %fusion.24 = f32[512,256]{0,1:T(8,128)S(1)} fusion(bf16[512,7168]{1,0:T(8,128)(2,1)} %gather_fusion, bf16[7168,256]{1,0:T(8,128)(2,1)} %param.13), kind=kOutput, calls=%fused_computation.47 | convolution fusion | flops 1879048192 | bytes 11534336 | tf_op jit(solution)/shard_map/dot_general | solution.py:22
  164.4 0.0 copy-done
  164.4 0.9 copy-done.3
  165.3 2.1 %fusion.23 = f32[512,256]{0,1:T(8,128)S(1)} fusion(bf16[512,7168]{1,0:T(8,128)(2,1)S(1)} %copy-done, bf16[7168,256]{1,0:T(8,128)(2,1)S(1)} %copy-done.3), kind=kOutput, calls=%fused_computation.46 | convolution fusion | flops 1879048192 | bytes 11534336 | tf_op jit(solution)/shard_map/dot_general | solution.py:21
  167.4 1.1 pad_maximum_fusion
  168.5 0.0 reduce-scatter.3.cloned.1.call-update
  168.6 0.1 compare_and_fusion
  168.6 0.1 broadcast_multiply_fusion
  168.7 0.1 iota_subtract_fusion
  168.8 0.1 subtract_convert_fusion
  168.9 0.0 reduce-scatter.5.cloned.1.call-done
  168.9 0.9 convert_element_type.38
  169.9 0.2 fusion.22
  170.1 0.1 copy.67
  170.2 5.0 %reduce-scatter.3.cloned.1.call-done = f32[256,512]{0,1:T(8,128)} async-done(((f32[512,512]{0,1:T(8,128)}), f32[256,512]{0,1:T(8,128)}) %reduce-scatter.3.cloned.1.call-update) | async-done | bytes 524304 | tf_op jit(solution)/shard_map/reduce_scatter | solution.py:18
  175.2 1.1 convert_element_type.37
  176.3 0.2 fusion.21
  176.6 0.1 copy.68
  176.7 0.2 fusion.8
  176.9 0.1 fusion.11
  177.0 0.1 copy.69
  177.1 0.1 copy.71
  177.2 0.2 fusion.14
  177.4 0.2 fusion.7
  177.7 0.6 reshape.200
  (17 shorter events, 0.2 us)
Async XLA Ops:
  7.4 118.3 %all-gather.2.cloned.1.call-start = ((), (), s32[]{:S(2)}) async-start(), calls=%async_computation.3 | async-start | bytes 8257536 | tf_op jit(solution)/shard_map/all_gather | solution.py:15
  8.1 160.8 %reduce-scatter.5.cloned.1.call-start = ((), (), s32[]{:S(2)}) async-start(), calls=%async_computation.5 | async-start | bytes 589824 | tf_op jit(solution)/shard_map/reduce_scatter | solution.py:40
  11.1 3.1 %copy-start.2 = (bf16[7168,256]{1,0:T(8,128)(2,1)S(1)}, bf16[7168,256]{1,0:T(8,128)(2,1)}, u32[]{:S(2)}) copy-start(bf16[7168,256]{1,0:T(8,128)(2,1)} %param.12) | copy-start | bytes 11010052
  14.2 2.0 %copy-start.1 = (bf16[7168,256]{1,0:T(8,128)(2,1)S(1)}, bf16[7168,256]{1,0:T(8,128)(2,1)}, u32[]{:S(2)}) copy-start(bf16[7168,256]{1,0:T(8,128)(2,1)} %param.11) | copy-start | bytes 11010052
  16.3 1.8 copy-start.5
  16.3 1.8 copy-start.4
  18.0 157.2 %reduce-scatter.3.cloned.1.call-start = ((), (), s32[]{:S(2)}) async-start(), calls=%async_computation.4 | async-start | bytes 1572864 | tf_op jit(solution)/shard_map/reduce_scatter | solution.py:18
  158.0 6.4 %copy-start = (bf16[512,7168]{1,0:T(8,128)(2,1)S(1)}, bf16[512,7168]{1,0:T(8,128)(2,1)}, u32[]{:S(2)}) copy-start(bf16[512,7168]{1,0:T(8,128)(2,1)} %gather_fusion) | copy-start | bytes 22020100
  158.0 7.3 %copy-start.3 = (bf16[7168,256]{1,0:T(8,128)(2,1)S(1)}, bf16[7168,256]{1,0:T(8,128)(2,1)}, u32[]{:S(2)}) copy-start(bf16[7168,256]{1,0:T(8,128)(2,1)} %param.12) | copy-start | bytes 11010052
Sparse Core Ops, SparseCore 0:
  10.7 114.9 all-gather.1
Sparse Core Ops, SparseCore 1:
  18.1 10.4 reduce-scatter.4
  168.6 6.6 reduce-scatter.2
where the time goes:
time: 186 us
  waiting for transfers between devices  113 us (61%)
  local copies, waits for them, and re-layouts  29.2 us (16%)
  between operations  15.1 us (8%)
  matrix products  13.6 us (7%)
  blocking collectives  10.9 us (6%)
  other arithmetic  3.86 us (2%)
    all_gather x1, waiting for transfers between devices, on_device(): full_rows = lax.all_gather(hidden, 'head', axis=1, tiled=True)  107 us
    gather x1, local copies, waits for them, and re-layouts, on_device(): rows = halves[slot_tokens]  17.9 us
    all_to_all x1, blocking collectives, on_device(): lax.all_to_all(full_rows, 'pre', split_axis=1, concat_axis=0, tiled=True)  10.9 us
    dot_general x2, matrix products, on_device(): jnp.dot(rows, value_weight, preferred_element_type=jnp.float32)  9.21 us
    reduce_scatter x1, waiting for transfers between devices, on_device(): lax.psum_scatter(jnp.concatenate([jnp.dot(rows, key_weight, preferred_ele...  5.02 us
  transfers between devices with their start and end apart: 3, of which 2 were waited for; matrix products, arithmetic and copies ran while one was open for 22% of the time, Pallas kernels for 0%

commit v1 on v0

v1 whole, which is shorter than its diff:
```python
import functools

import jax
import jax.numpy as jnp
import numpy as np
from jax import lax
from jax.experimental import pallas as pl
from jax.experimental.pallas import tpu as pltpu
from jax.sharding import PartitionSpec as P

HS = 128


def ring_order(n):
    if n == 8:
        return [0, 2, 4, 6, 7, 5, 3, 1]
    return list(range(n))


def step_kernel(count, first, rows_ref, *refs):
    items = refs[:count]
    acc_ref, wk, wv, wk_far, wv_far = refs[count : count + 5]
    out_ref, held, sems = refs[count + 5 :]
    depth = held.shape[1]
    cols = wk.shape[1]

    def copies(i, keys, values):
        start = pl.multiple_of(rows_ref[2 * (first + i)], 32)
        return [
            pltpu.make_async_copy(
                src.at[pl.ds(start, depth), :], held.at[i, :, pl.ds(part * cols, cols)], sems.at[i, part]
            )
            for part, src in enumerate((keys, values))
        ]

    for i in range(count):

        @pl.when(rows_ref[2 * (first + i) + 1] == 0)
        def _():
            for copy in copies(i, wk, wv):
                copy.start()

        @pl.when(rows_ref[2 * (first + i) + 1] != 0)
        def _():
            for copy in copies(i, wk_far, wv_far):
                copy.start()

    total = acc_ref[...]
    for i in range(count):
        for copy in copies(i, wk, wv):
            copy.wait()
        term = jnp.dot(items[i][...], held[i], preferred_element_type=jnp.float32)
        total = total + term
    out_ref[...] = total.astype(out_ref.dtype)


def step(items, acc, rows, first, weights, dtype=jnp.float32):
    count = len(items)
    tok, depth = items[0].shape
    cols = weights[0].shape[1]
    vmem = pl.BlockSpec(memory_space=pltpu.VMEM)
    return pl.pallas_call(
        functools.partial(step_kernel, count, first),
        out_shape=jax.ShapeDtypeStruct((tok, 2 * cols), dtype),
        in_specs=[pl.BlockSpec(memory_space=pltpu.SMEM)]
        + [vmem] * (count + 1)
        + [pl.BlockSpec(memory_space=pl.ANY)] * 4,
        out_specs=vmem,
        scratch_shapes=[
            pltpu.VMEM((count, depth, 2 * cols), jnp.bfloat16),
            pltpu.SemaphoreType.DMA((count, 2)),
        ],
        compiler_params=pltpu.CompilerParams(vmem_limit_bytes=24 * 1024 * 1024),
        cost_estimate=pl.CostEstimate(
            flops=2 * count * tok * depth * 2 * cols,
            bytes_accessed=count * (tok * depth * 2 + depth * cols * 4) + tok * cols * 16,
            transcendentals=0,
        ),
    )(rows, *items, acc, *weights)


def attend_kernel(steps, slope_ref, fresh_ref, own_ref, far_ref, place_ref, span_ref, out_ref):
    rows = fresh_ref.shape[0]
    cols = fresh_ref.shape[1] // 3
    tok = own_ref.shape[0]
    scale = 1.0 / HS**0.5
    start = span_ref[:, 0:1]
    length = span_ref[:, 1:2]
    row = lax.broadcasted_iota(jnp.int32, (rows, 1), 0)
    step_of = row % steps
    rel = place_ref[...] - start
    valid = (rel >= 0) & (rel < length)
    dist = (length + step_of - rel).astype(jnp.float32)
    col = lax.broadcasted_iota(jnp.int32, (1, rows), 1)
    near_ok = (row // steps == col // steps) & (col <= row)
    near_dist = (row - col).astype(jnp.float32)
    nt = (((1,), (1,)), ((), ()))
    for head in range(cols // HS):
        slope = slope_ref[head]
        query = fresh_ref[:, head * HS : (head + 1) * HS]
        fresh_key = fresh_ref[:, cols + head * HS : cols + (head + 1) * HS]
        fresh_value = fresh_ref[:, 2 * cols + head * HS : 2 * cols + (head + 1) * HS]
        scores = []
        for part, ref in enumerate((own_ref, far_ref)):
            key = ref[:, head * HS : (head + 1) * HS]
            ctx = lax.dot_general(query, key, nt, preferred_element_type=jnp.float32) * scale
            ctx = ctx - slope * dist[:, part * tok : (part + 1) * tok]
            scores.append(jnp.where(valid[:, part * tok : (part + 1) * tok], ctx, -1e30))
        near = lax.dot_general(query, fresh_key, nt, preferred_element_type=jnp.float32) * scale
        scores.append(jnp.where(near_ok, near - slope * near_dist, -1e30))
        top = functools.reduce(jnp.maximum, [jnp.max(s, axis=1, keepdims=True) for s in scores])
        exps = [jnp.exp(s - top) for s in scores]
        total = sum(jnp.sum(e, axis=1, keepdims=True) for e in exps)
        weights = [(e / total).astype(jnp.bfloat16) for e in exps]
        values = [ref[:, cols + head * HS : cols + (head + 1) * HS] for ref in (own_ref, far_ref)]
        values.append(fresh_value)
        out = sum(
            jnp.dot(w, v, preferred_element_type=jnp.float32) for w, v in zip(weights, values)
        )
        out_ref[:, head * HS : (head + 1) * HS] = out.astype(out_ref.dtype)


def on_device(hidden, slot_tokens, lengths, decode_rows, query_weight, key_weight, value_weight):
    group = lax.axis_index("head")
    owner = lax.axis_index("pre")
    n = lax.axis_size("head")
    own_tok, width = hidden.shape
    depth = key_weight.shape[0]
    cols = key_weight.shape[1]
    heads_dev = cols // HS
    swap = [(0, 1), (1, 0)]

    order = ring_order(n)
    up = [(order[i], order[(i + 1) % n]) for i in range(n)]
    down = [(order[i], order[(i - 1) % n]) for i in range(n)]
    place = [0] * n
    for i, g in enumerate(order):
        place[g] = i
    half = width // 2

    own = [hidden[:, :half], hidden[:, half:]]
    ups, downs = list(own), list(own)
    arrivals = []
    for s in range(1, n // 2 + 1):
        last = s == n // 2
        for i in range(2):
            if not last or i == 0:
                ups[i] = lax.ppermute(ups[i], "head", up)
                downs[1 - i] = lax.ppermute(downs[1 - i], "head", down)
                arrivals.append(((ups[i], -s, i), (downs[1 - i], s, 1 - i)))

    seen = [(0, 0), (0, 1)] + [(d, part) for pair in arrivals for _, d, part in pair]
    table = np.zeros((2 * n, 2 * len(seen)), np.int32)
    for g in range(n):
        for k, (distance, part) in enumerate(seen):
            row = order[(place[g] + distance) % n] * width + part * half
            for p in range(2):
                table[2 * g + p, 2 * k : 2 * k + 2] = row % depth, row // depth != p
    rows_of = lax.dynamic_slice_in_dim(jnp.asarray(table), 2 * group + owner, 1, 0)[0]

    weights = (
        key_weight,
        value_weight,
        lax.ppermute(key_weight, "pre", swap),
        lax.ppermute(value_weight, "pre", swap),
    )

    req_dev, steps = lengths.shape[1], decode_rows.shape[1]
    rows_dev = req_dev * steps
    rows = decode_rows.reshape(2 * rows_dev, depth)
    sums = jnp.concatenate(
        [jnp.dot(rows, w, preferred_element_type=jnp.float32) for w in (query_weight, key_weight, value_weight)],
        axis=1,
    )
    keep = lax.dynamic_slice_in_dim(sums, owner * rows_dev, rows_dev, 0)
    give = lax.dynamic_slice_in_dim(sums, (1 - owner) * rows_dev, rows_dev, 0)
    fresh = (keep + lax.ppermute(give, "pre", swap)).astype(jnp.bfloat16)

    mine = lax.dynamic_slice_in_dim(slot_tokens, owner * own_tok, own_tok)
    lane = jnp.arange(2 * own_tok, dtype=jnp.int32)
    token = (lane + owner * own_tok) % (2 * own_tok)
    slot = jnp.arange(1, own_tok + 1, dtype=jnp.int32)
    where = jnp.sum(jnp.where(mine[:, None] == token[None, :], slot[:, None], 0), axis=0, keepdims=True)
    lens = lengths[0]
    starts = jnp.cumsum(lens) - lens
    where = jnp.where(where == 0, -(1 << 20), where - 1)
    span = jnp.repeat(jnp.stack([starts, lens], axis=1), steps, axis=0)
    heads_index = (group * heads_dev + jnp.arange(heads_dev)).astype(jnp.float32)
    slope = jnp.exp2(-8.0 * (heads_index + 1.0) / (heads_dev * n))

    acc = step(own, jnp.zeros((own_tok, 2 * cols), jnp.float32), rows_of, 0, weights)
    for k, pair in enumerate(arrivals):
        final = k == len(arrivals) - 1
        acc = step(
            [item for item, _, _ in pair],
            acc,
            rows_of,
            2 * k + 2,
            weights,
            jnp.bfloat16 if final else jnp.float32,
        )
    far = lax.ppermute(acc, "pre", swap)
    vmem = pl.BlockSpec(memory_space=pltpu.VMEM)
    out = pl.pallas_call(
        functools.partial(attend_kernel, steps),
        out_shape=jax.ShapeDtypeStruct((rows_dev, cols), jnp.bfloat16),
        in_specs=[pl.BlockSpec(memory_space=pltpu.SMEM)] + [vmem] * 5,
        out_specs=vmem,
        compiler_params=pltpu.CompilerParams(vmem_limit_bytes=16 * 1024 * 1024),
    )(slope, fresh, acc, far, where, span)
    return out.reshape(req_dev, steps, cols)


def solution(mesh):
    in_specs = (
        P(("grp", "pre"), "head"),
        P("grp"),
        P(("grp", "pre"), None),
        P("grp", None, "pre"),
        P("pre", "head"),
        P("pre", "head"),
        P("pre", "head"),
    )
    out_specs = P(("grp", "pre"), None, "head")
    return jax.shard_map(
        on_device, mesh=mesh, in_specs=in_specs, out_specs=out_specs, check_vma=False
    )
```

time: 186 us -> 95.3 us (0.51)
  the two profiles are of different devices: /device:TPU:0 before, /device:TPU:17 now
where the time goes in v1:
time: 95.3 us; the launch traced here: 94.7 us
  waiting for transfers between devices  34.5 us (36%)
  Pallas kernels  23 us (24%)
  starting transfers between devices  15.9 us (17%)
  local copies, waits for them, and re-layouts  14.3 us (15%)
  matrix products  4.67 us (5%)
  other arithmetic  1.97 us (2%)
    ppermute x7, waiting for transfers between devices, on_device(): ups[i] = lax.ppermute(ups[i], 'head', up)  24.4 us
    pallas_call x8, Pallas kernels, step(): pl.pallas_call(functools.partial(step_kernel, count, first), out_shape=ja...  21.6 us
    ppermute x7, waiting for transfers between devices, on_device(): downs[1 - i] = lax.ppermute(downs[1 - i], 'head', down)  9.66 us
    ppermute x7, starting transfers between devices, on_device(): ups[i] = lax.ppermute(ups[i], 'head', up)  8.28 us
    unnamed x25, local copies, waits for them, and re-layouts  6.58 us
    ppermute x1, starting transfers between devices, on_device(): fresh = (keep + lax.ppermute(give, 'pre', swap)).astype(jnp.bfloat16)  5.6 us
    dot_general x3, matrix products, on_device(): jnp.dot(rows, w, preferred_element_type=jnp.float32)  4.67 us
    reshape x1, local copies, waits for them, and re-layouts, on_device(): rows = decode_rows.reshape(2 * rows_dev, depth)  3.99 us
  transfers between devices with their start and end apart: 18, of which 7 were waited for; matrix products, arithmetic and copies ran while one was open for 15% of the time, Pallas kernels for 23%

profile of v1, /device:TPU:17, one launch (start us, length us, event | category | flops | bytes accessed | tf_op | source)
XLA Modules:
  0.0 94.7 jit_solution(8802365458099594187)
XLA Ops:
  0.0 0.7 collective-permute-start.15
  0.7 0.1 collective-permute-start.16
  0.8 1.2 %fusion.2 = (bf16[256,896]{1,0:T(8,128)(2,1)S(1)}, bf16[256,896]{1,0:T(8,128)(2,1)S(1)}) fusion(bf16[256,1792]{1,0:T(8,128)(2,1)} %param.8), kind=kLoop, calls=%fused_computation.14 | loop fusion | bytes 1835008 | tf_op jit(solution)/shard_map/slice | solution.py:141
  2.0 1.3 %collective-permute-start.1 = (bf16[256,896]{1,0:T(8,128)(2,1)S(1)}, bf16[256,896]{1,0:T(8,128)(2,1)S(1)}, u32[]{:S(2)}, u32[]{:S(2)}) collective-permute-start(bf16[256,896]{1,0:T(8,128)(2,1)S(1)} %get-tuple-element.6.refs_0_), channel_id=1, source_target_pairs={{0,2},{2,4},{4,6},{6,7},{7,5},{5,3},{3,1},{1,0},{8,10},{10,12},{12... | collective-permute-start | bytes 1376264 | tf_op jit(solution)/shard_map/ppermute | solution.py:148
  3.3 0.2 collective-permute-start.12
  3.5 0.2 collective-permute-start.5
  3.7 4.0 %reshape.69 = bf16[128,7168]{1,0:T(8,128)(2,1)} reshape(bf16[32,4,7168]{2,1,0:T(4,128)(2,1)} %param.11) | data formatting | bytes 3670016 | tf_op jit(solution)/shard_map/reshape | solution.py:170
  7.7 0.1 copy.23
  7.8 0.1 copy.25
  7.9 0.1 dynamic_slice.15
  8.0 3.4 %fusion.4 = f32[128,256]{1,0:T(8,128)S(1)} fusion(bf16[128,7168]{1,0:T(8,128)(2,1)} %reshape.69, bf16[7168,256]{1,0:T(8,128)(2,1)} %refs_3_.15), kind=kOutput, calls=%fused_computation.16 | convolution fusion | flops 469762048 | bytes 5636096 | tf_op jit(solution)/shard_map/dot_general | solution.py:172
  11.4 0.0 copy-start.8
  11.4 2.3 %collective-permute-done.1.refs_0_ = bf16[256,896]{1,0:T(8,128)(2,1)S(1)} collective-permute-done((bf16[256,896]{1,0:T(8,128)(2,1)S(1)}, bf16[256,896]{1,0:T(8,128)(2,1)S(1)}, u32[]{:S(2)}, u32[]{:S(2)}) %collective-permute-start.1) | collective-permute-done | bytes 458784 | tf_op jit(solution)/shard_map/ppermute | solution.py:148
  13.7 1.3 %collective-permute-start.9 = (bf16[256,896]{1,0:T(8,128)(2,1)S(1)}, bf16[256,896]{1,0:T(8,128)(2,1)S(1)}, u32[]{:S(2)}, u32[]{:S(2)}) collective-permute-start(bf16[256,896]{1,0:T(8,128)(2,1)S(1)} %get-tuple-element.5.refs_1_), channel_id=1, source_target_pairs={{0,2},{2,4},{4,6},{6,7},{7,5},{5,3},{3,1},{1,0},{8,10},{10,12},{12... | collective-permute-start | bytes 1376264 | tf_op jit(solution)/shard_map/ppermute | solution.py:148
  15.0 0.6 fusion.5
  15.7 8.8 %collective-permute-done.5.refs_1_ = bf16[256,896]{1,0:T(8,128)(2,1)S(1)} collective-permute-done((bf16[256,896]{1,0:T(8,128)(2,1)S(1)}, bf16[256,896]{1,0:T(8,128)(2,1)S(1)}, u32[]{:S(2)}, u32[]{:S(2)}) %collective-permute-start.5) | collective-permute-done | bytes 458784 | tf_op jit(solution)/shard_map/ppermute | solution.py:149
  24.5 1.2 %collective-permute-start.2 = (bf16[256,896]{1,0:T(8,128)(2,1)S(1)}, bf16[256,896]{1,0:T(8,128)(2,1)S(1)}, u32[]{:S(2)}, u32[]{:S(2)}) collective-permute-start(bf16[256,896]{1,0:T(8,128)(2,1)S(1)} %collective-permute-done.1.refs_0_), channel_id=1, source_target_pairs={{0,2},{2,4},{4,6},{6,7},{7,5},{5,3},{3,1},{1,0},{8,10},{10,12},{12... | collective-permute-start | bytes 1376264 | tf_op jit(solution)/shard_map/ppermute | solution.py:148
  25.8 0.0 collective-permute-done.12.refs_1_
  25.8 0.2 collective-permute-start.6
  26.0 0.0 collective-permute-done.9.refs_0_
  26.0 1.2 %collective-permute-start.10 = (bf16[256,896]{1,0:T(8,128)(2,1)S(1)}, bf16[256,896]{1,0:T(8,128)(2,1)}, u32[]{:S(2)}, u32[]{:S(2)}) collective-permute-start(bf16[256,896]{1,0:T(8,128)(2,1)S(1)} %collective-permute-done.9.refs_0_), channel_id=1, source_target_pairs={{0,2},{2,4},{4,6},{6,7},{7,5},{5,3},{3,1},{1,0},{8,10},{10,12},{12... | collective-permute-start | bytes 1376264 | tf_op jit(solution)/shard_map/ppermute | solution.py:148
  27.2 0.6 fusion.3
  27.9 0.8 pad_maximum_fusion
  28.7 6.2 %collective-permute-done.2.refs_0_ = bf16[256,896]{1,0:T(8,128)(2,1)S(1)} collective-permute-done((bf16[256,896]{1,0:T(8,128)(2,1)S(1)}, bf16[256,896]{1,0:T(8,128)(2,1)S(1)}, u32[]{:S(2)}, u32[]{:S(2)}) %collective-permute-start.2) | collective-permute-done | bytes 458784 | tf_op jit(solution)/shard_map/ppermute | solution.py:148
  34.9 0.2 collective-permute-start.13
  35.1 0.8 collective-permute-done.6.refs_1_
  35.9 0.5 collective-permute-start.3
  36.4 8.5 %collective-permute-done.10.refs_0_ = bf16[256,896]{1,0:T(8,128)(2,1)} collective-permute-done((bf16[256,896]{1,0:T(8,128)(2,1)S(1)}, bf16[256,896]{1,0:T(8,128)(2,1)}, u32[]{:S(2)}, u32[]{:S(2)}) %collective-permute-start.10) | collective-permute-done | bytes 458784 | tf_op jit(solution)/shard_map/ppermute | solution.py:148
  44.8 0.2 collective-permute-start.7
  45.0 0.8 copy-done.5
  45.8 0.1 select_reduce_fusion
  45.9 0.0 collective-permute-done.13.refs_1_
  46.0 1.3 %collective-permute-start.11 = (bf16[256,896]{1,0:T(8,128)(2,1)}, bf16[256,896]{1,0:T(8,128)(2,1)}, u32[]{:S(2)}, u32[]{:S(2)}) collective-permute-start(bf16[256,896]{1,0:T(8,128)(2,1)} %collective-permute-done.10.refs_0_), channel_id=1, source_target_pairs={{0,2},{2,4},{4,6},{6,7},{7,5},{5,3},{3,1},{1,0},{8,10},{10,12},{12... | collective-permute-start | bytes 1376264 | tf_op jit(solution)/shard_map/ppermute | solution.py:148
  47.3 7.4 %collective-permute-done.3.refs_0_ = bf16[256,896]{1,0:T(8,128)(2,1)} collective-permute-done((bf16[256,896]{1,0:T(8,128)(2,1)S(1)}, bf16[256,896]{1,0:T(8,128)(2,1)}, u32[]{:S(2)}, u32[]{:S(2)}) %collective-permute-start.3) | collective-permute-done | bytes 458784 | tf_op jit(solution)/shard_map/ppermute | solution.py:148
  54.7 0.2 collective-permute-start.14
  54.8 0.0 collective-permute-done.7.refs_1_
  54.8 1.3 %collective-permute-start.4 = (bf16[256,896]{1,0:T(8,128)(2,1)}, bf16[256,896]{1,0:T(8,128)(2,1)}, u32[]{:S(2)}, u32[]{:S(2)}) collective-permute-start(bf16[256,896]{1,0:T(8,128)(2,1)} %collective-permute-done.3.refs_0_), channel_id=1, source_target_pairs={{0,2},{2,4},{4,6},{6,7},{7,5},{5,3},{3,1},{1,0},{8,10},{10,12},{12... | collective-permute-start | bytes 1376264 | tf_op jit(solution)/shard_map/ppermute | solution.py:148
  56.1 0.0 collective-permute-done.15.refs_5_
  56.1 0.2 collective-permute-start.8
  56.3 0.7 fusion.1.rows_ref
  57.0 0.9 constant_dynamic-slice_fusion.1
  58.0 0.0 collective-permute-done.16.refs_6_
  58.0 5.6 %collective-permute-start = (f32[64,768]{1,0:T(8,128)S(1)}, f32[64,768]{1,0:T(8,128)}, u32[]{:S(2)}, u32[]{:S(2)}) collective-permute-start(f32[64,768]{1,0:T(8,128)S(1)} %constant_dynamic-slice_fusion.1), channel_id=1, source_target_pairs={{0,8},{8,0},{1,9},{9,1},{2,10},{10,2},{3,11},{11,3},{4,12},{12,4},... | collective-permute-start | bytes 589832 | tf_op jit(solution)/shard_map/ppermute | solution.py:177
  63.6 0.0 copy-start.1
  63.6 2.0 %copy-done.1 = bf16[7168,256]{1,0:T(8,128)(2,1)S(1)} copy-done((bf16[7168,256]{1,0:T(8,128)(2,1)S(1)}, bf16[7168,256]{1,0:T(8,128)(2,1)}, u32[]{:S(2)}) %copy-start.1) | copy-done | bytes 3670040
  65.7 2.0 %copy-done.3 = bf16[7168,256]{1,0:T(8,128)(2,1)S(1)} copy-done((bf16[7168,256]{1,0:T(8,128)(2,1)S(1)}, bf16[7168,256]{1,0:T(8,128)(2,1)}, u32[]{:S(2)}) %copy-start.3) | copy-done | bytes 3670040
  67.7 1.5 %shard_map.82.refs_2_ = f32[256,512]{1,0:T(8,128)S(1)} custom-call(s32[32]{0:T(128)S(1)} %fusion.1.rows_ref, bf16[256,896]{1,0:T(8,128)(2,1)S(1)} %get-tuple-element.6.refs_0_, bf16[256,896]{1,0:T(8,128)(2,1)S(1)} %get-tuple-element.5.refs_1_, f32[256,512]{1,0:T(8,128)S(1)} %broadcast_in_dim.26.refs_2_, bf16[7168,256]{1,0:T(8,128)(2,1)S(1)} %copy-done.3, ...), custom_call_target="tpu_custom_call" | custom-call | flops 469762048 | bytes 3801088 | tf_op jit(solution)/shard_map/pallas_call | solution.py:62
  69.2 0.5 copy-done.2
  69.7 1.1 %copy-done.4 = bf16[7168,256]{1,0:T(8,128)(2,1)S(1)} copy-done((bf16[7168,256]{1,0:T(8,128)(2,1)S(1)}, bf16[7168,256]{1,0:T(8,128)(2,1)}, u32[]{:S(2)}) %copy-start.4) | copy-done | bytes 3670040
  70.9 2.5 %shard_map.83.refs_2_ = f32[256,512]{1,0:T(8,128)S(1)} custom-call(s32[32]{0:T(128)S(1)} %fusion.1.rows_ref, bf16[256,896]{1,0:T(8,128)(2,1)S(1)} %collective-permute-done.1.refs_0_, bf16[256,896]{1,0:T(8,128)(2,1)S(1)} %collective-permute-done.5.refs_1_, f32[256,512]{1,0:T(8,128)S(1)} %shard_map.82.refs_2_, bf16[7168,256]{1,0:T(8,128)(2,1)S(1)} %copy-done.4, ...), custom_call_target="tpu_custom_call" | custom-call | flops 469762048 | bytes 3801088 | tf_op jit(solution)/shard_map/pallas_call | solution.py:62
  73.4 2.5 %shard_map.84.refs_2_ = f32[256,512]{1,0:T(8,128)S(1)} custom-call(s32[32]{0:T(128)S(1)} %fusion.1.rows_ref, bf16[256,896]{1,0:T(8,128)(2,1)S(1)} %collective-permute-done.9.refs_0_, bf16[256,896]{1,0:T(8,128)(2,1)S(1)} %collective-permute-done.12.refs_1_, f32[256,512]{1,0:T(8,128)S(1)} %shard_map.83.refs_2_, bf16[7168,256]{1,0:T(8,128)(2,1)S(1)} %copy-done.4, ...), custom_call_target="tpu_custom_call" | custom-call | flops 469762048 | bytes 3801088 | tf_op jit(solution)/shard_map/pallas_call | solution.py:62
  75.9 2.5 %shard_map.85.refs_2_ = f32[256,512]{1,0:T(8,128)S(1)} custom-call(s32[32]{0:T(128)S(1)} %fusion.1.rows_ref, bf16[256,896]{1,0:T(8,128)(2,1)S(1)} %collective-permute-done.2.refs_0_, bf16[256,896]{1,0:T(8,128)(2,1)S(1)} %copy-done.6, f32[256,512]{1,0:T(8,128)S(1)} %shard_map.84.refs_2_, bf16[7168,256]{1,0:T(8,128)(2,1)S(1)} %copy-done.4, ...), custom_call_target="tpu_custom_call" | custom-call | flops 469762048 | bytes 3801088 | tf_op jit(solution)/shard_map/pallas_call | solution.py:62
  78.4 3.1 %shard_map.86.refs_2_ = f32[256,512]{1,0:T(8,128)S(1)} custom-call(s32[32]{0:T(128)S(1)} %fusion.1.rows_ref, bf16[256,896]{1,0:T(8,128)(2,1)} %collective-permute-done.10.refs_0_, bf16[256,896]{1,0:T(8,128)(2,1)} %collective-permute-done.13.refs_1_, f32[256,512]{1,0:T(8,128)S(1)} %shard_map.85.refs_2_, bf16[7168,256]{1,0:T(8,128)(2,1)S(1)} %copy-done.4, ...), custom_call_target="tpu_custom_call" | custom-call | flops 469762048 | bytes 3801088 | tf_op jit(solution)/shard_map/pallas_call | solution.py:62
  81.6 3.1 %shard_map.87.refs_2_ = f32[256,512]{1,0:T(8,128)S(1)} custom-call(s32[32]{0:T(128)S(1)} %fusion.1.rows_ref, bf16[256,896]{1,0:T(8,128)(2,1)} %collective-permute-done.3.refs_0_, bf16[256,896]{1,0:T(8,128)(2,1)} %collective-permute-done.7.refs_1_, f32[256,512]{1,0:T(8,128)S(1)} %shard_map.86.refs_2_, bf16[7168,256]{1,0:T(8,128)(2,1)S(1)} %copy-done.4, ...), custom_call_target="tpu_custom_call" | custom-call | flops 469762048 | bytes 3801088 | tf_op jit(solution)/shard_map/pallas_call | solution.py:62
  84.7 0.0 collective-permute-done.11.refs_0_
  84.7 3.1 %shard_map.88.refs_2_ = f32[256,512]{1,0:T(8,128)S(1)} custom-call(s32[32]{0:T(128)S(1)} %fusion.1.rows_ref, bf16[256,896]{1,0:T(8,128)(2,1)} %collective-permute-done.11.refs_0_, bf16[256,896]{1,0:T(8,128)(2,1)} %collective-permute-done.14.refs_1_, f32[256,512]{1,0:T(8,128)S(1)} %shard_map.87.refs_2_, bf16[7168,256]{1,0:T(8,128)(2,1)S(1)} %copy-done.4, ...), custom_call_target="tpu_custom_call" | custom-call | flops 469762048 | bytes 3801088 | tf_op jit(solution)/shard_map/pallas_call | solution.py:62
  87.9 0.0 collective-permute-done.8.refs_1_
  87.9 3.2 %shard_map.89.own_ref = bf16[256,512]{1,0:T(8,128)(2,1)S(1)} custom-call(s32[32]{0:T(128)S(1)} %fusion.1.rows_ref, bf16[256,896]{1,0:T(8,128)(2,1)} %collective-permute-done.4.refs_0_, bf16[256,896]{1,0:T(8,128)(2,1)} %collective-permute-done.8.refs_1_, f32[256,512]{1,0:T(8,128)S(1)} %shard_map.88.refs_2_, bf16[7168,256]{1,0:T(8,128)(2,1)S(1)} %copy-done.4, ...), custom_call_target="tpu_custom_call" | custom-call | flops 469762048 | bytes 3801088 | tf_op jit(solution)/shard_map/pallas_call | solution.py:62
  91.1 0.1 collective-permute-start.17
  91.2 0.1 copy.28
  91.3 0.9 %add_convert_fusion.fresh_ref = bf16[64,768]{1,0:T(8,128)(2,1)S(1)} fusion(f32[64,768]{1,0:T(8,128)} %collective-permute-done, f32[128,768]{1,0:T(8,128)S(1)} %copy-done.9, s32[]{:T(128)S(6)} %select_n.33), kind=kLoop, calls=%fused_computation.2 | loop fusion | flops 98304 | bytes 491524 | tf_op jit(solution)/shard_map/convert_element_type | solution.py:177
  92.2 0.5 collective-permute-done.17.far_ref
  92.7 1.4 %shard_map.90 = bf16[64,256]{1,0:T(8,128)(2,1)S(1)} custom-call(f32[2]{0:T(128)S(1)} %multiply_exponential_fusion.slope_ref, bf16[64,768]{1,0:T(8,128)(2,1)S(1)} %add_convert_fusion.fresh_ref, bf16[256,512]{1,0:T(8,128)(2,1)S(1)} %shard_map.89.own_ref, bf16[256,512]{1,0:T(8,128)(2,1)S(1)} %collective-permute-done.17.far_ref, s32[1,512]{1,0:T(1,128)S(1)} %bitcast.12, ...), custom_call_target="tpu_custom_call" | custom-call | tf_op jit(solution)/shard_map/pallas_call | solution.py:204
  94.1 0.6 reshape.72
  (29 shorter events, 0.2 us)
Async XLA Ops:
  0.0 7.7 %copy-start.10 = (s32[1,16]{1,0:T(1,128)S(1)}, s32[1,16]{1,0:T(1,128)}, u32[]{:S(2)}) copy-start(s32[1,16]{1,0:T(1,128)} %param.10) | copy-start | bytes 196
  0.0 7.9 %copy-start.11 = (s32[512]{0:T(512)S(1)}, s32[512]{0:T(512)}, u32[]{:S(2)}) copy-start(s32[512]{0:T(512)} %param.9) | copy-start | bytes 6148
  0.0 56.1 %collective-permute-start.15 = (bf16[7168,256]{1,0:T(8,128)(2,1)}, bf16[7168,256]{1,0:T(8,128)(2,1)}, u32[]{:S(2)}, u32[]{:S(2)}) collective-permute-start(bf16[7168,256]{1,0:T(8,128)(2,1)} %refs_3_.15), channel_id=1, source_target_pairs={{0,8},{8,0},{1,9},{9,1},{2,10},{10,2},{3,11},{11,3},{4,12},{12,4},... | collective-permute-start | bytes 11010056 | tf_op jit(solution)/shard_map/ppermute | solution.py:164
  0.7 57.3 %collective-permute-start.16 = (bf16[7168,256]{1,0:T(8,128)(2,1)}, bf16[7168,256]{1,0:T(8,128)(2,1)}, u32[]{:S(2)}, u32[]{:S(2)}) collective-permute-start(bf16[7168,256]{1,0:T(8,128)(2,1)} %refs_4_.15), channel_id=1, source_target_pairs={{0,8},{8,0},{1,9},{9,1},{2,10},{10,2},{3,11},{11,3},{4,12},{12,4},... | collective-permute-start | bytes 11010056 | tf_op jit(solution)/shard_map/ppermute | solution.py:165
  2.0 11.7 %collective-permute-start.1 = (bf16[256,896]{1,0:T(8,128)(2,1)S(1)}, bf16[256,896]{1,0:T(8,128)(2,1)S(1)}, u32[]{:S(2)}, u32[]{:S(2)}) collective-permute-start(bf16[256,896]{1,0:T(8,128)(2,1)S(1)} %get-tuple-element.6.refs_0_), channel_id=1, source_target_pairs={{0,2},{2,4},{4,6},{6,7},{7,5},{5,3},{3,1},{1,0},{8,10},{10,12},{12... | collective-permute-start | bytes 1376264 | tf_op jit(solution)/shard_map/ppermute | solution.py:148
  3.3 22.4 %collective-permute-start.12 = (bf16[256,896]{1,0:T(8,128)(2,1)S(1)}, bf16[256,896]{1,0:T(8,128)(2,1)S(1)}, u32[]{:S(2)}, u32[]{:S(2)}) collective-permute-start(bf16[256,896]{1,0:T(8,128)(2,1)S(1)} %get-tuple-element.6.refs_0_), channel_id=1, source_target_pairs={{0,1},{2,0},{4,2},{6,4},{7,6},{5,7},{3,5},{1,3},{8,9},{10,8},{12,1... | collective-permute-start | bytes 1376264 | tf_op jit(solution)/shard_map/ppermute | solution.py:149
  3.5 21.0 %collective-permute-start.5 = (bf16[256,896]{1,0:T(8,128)(2,1)S(1)}, bf16[256,896]{1,0:T(8,128)(2,1)S(1)}, u32[]{:S(2)}, u32[]{:S(2)}) collective-permute-start(bf16[256,896]{1,0:T(8,128)(2,1)S(1)} %get-tuple-element.5.refs_1_), channel_id=1, source_target_pairs={{0,1},{2,0},{4,2},{6,4},{7,6},{5,7},{3,5},{1,3},{8,9},{10,8},{12,1... | collective-permute-start | bytes 1376264 | tf_op jit(solution)/shard_map/ppermute | solution.py:149
  7.9 7.1 %copy-start = (bf16[7168,256]{1,0:T(8,128)(2,1)S(1)}, bf16[7168,256]{1,0:T(8,128)(2,1)}, u32[]{:S(2)}) copy-start(bf16[7168,256]{1,0:T(8,128)(2,1)} %refs_4_.15) | copy-start | bytes 11010052
  7.9 7.1 %copy-start.7 = (bf16[128,7168]{1,0:T(8,128)(2,1)S(1)}, bf16[128,7168]{1,0:T(8,128)(2,1)}, u32[]{:S(2)}) copy-start(bf16[128,7168]{1,0:T(8,128)(2,1)} %reshape.69) | copy-start | bytes 5505028
  11.4 15.9 %copy-start.8 = (bf16[7168,256]{1,0:T(8,128)(2,1)S(1)}, bf16[7168,256]{1,0:T(8,128)(2,1)}, u32[]{:S(2)}) copy-start(bf16[7168,256]{1,0:T(8,128)(2,1)} %param.12) | copy-start | bytes 11010052
  13.7 12.3 %collective-permute-start.9 = (bf16[256,896]{1,0:T(8,128)(2,1)S(1)}, bf16[256,896]{1,0:T(8,128)(2,1)S(1)}, u32[]{:S(2)}, u32[]{:S(2)}) collective-permute-start(bf16[256,896]{1,0:T(8,128)(2,1)S(1)} %get-tuple-element.5.refs_1_), channel_id=1, source_target_pairs={{0,2},{2,4},{4,6},{6,7},{7,5},{5,3},{3,1},{1,0},{8,10},{10,12},{12... | collective-permute-start | bytes 1376264 | tf_op jit(solution)/shard_map/ppermute | solution.py:148
  24.5 10.4 %collective-permute-start.2 = (bf16[256,896]{1,0:T(8,128)(2,1)S(1)}, bf16[256,896]{1,0:T(8,128)(2,1)S(1)}, u32[]{:S(2)}, u32[]{:S(2)}) collective-permute-start(bf16[256,896]{1,0:T(8,128)(2,1)S(1)} %collective-permute-done.1.refs_0_), channel_id=1, source_target_pairs={{0,2},{2,4},{4,6},{6,7},{7,5},{5,3},{3,1},{1,0},{8,10},{10,12},{12... | collective-permute-start | bytes 1376264 | tf_op jit(solution)/shard_map/ppermute | solution.py:148
  25.8 10.1 %collective-permute-start.6 = (bf16[256,896]{1,0:T(8,128)(2,1)S(1)}, bf16[256,896]{1,0:T(8,128)(2,1)S(1)}, u32[]{:S(2)}, u32[]{:S(2)}) collective-permute-start(bf16[256,896]{1,0:T(8,128)(2,1)S(1)} %collective-permute-done.5.refs_1_), channel_id=1, source_target_pairs={{0,1},{2,0},{4,2},{6,4},{7,6},{5,7},{3,5},{1,3},{8,9},{10,8},{12,1... | collective-permute-start | bytes 1376264 | tf_op jit(solution)/shard_map/ppermute | solution.py:149
  26.0 18.9 %collective-permute-start.10 = (bf16[256,896]{1,0:T(8,128)(2,1)S(1)}, bf16[256,896]{1,0:T(8,128)(2,1)}, u32[]{:S(2)}, u32[]{:S(2)}) collective-permute-start(bf16[256,896]{1,0:T(8,128)(2,1)S(1)} %collective-permute-done.9.refs_0_), channel_id=1, source_target_pairs={{0,2},{2,4},{4,6},{6,7},{7,5},{5,3},{3,1},{1,0},{8,10},{10,12},{12... | collective-permute-start | bytes 1376264 | tf_op jit(solution)/shard_map/ppermute | solution.py:148
  34.9 11.0 %collective-permute-start.13 = (bf16[256,896]{1,0:T(8,128)(2,1)S(1)}, bf16[256,896]{1,0:T(8,128)(2,1)}, u32[]{:S(2)}, u32[]{:S(2)}) collective-permute-start(bf16[256,896]{1,0:T(8,128)(2,1)S(1)} %collective-permute-done.12.refs_1_), channel_id=1, source_target_pairs={{0,1},{2,0},{4,2},{6,4},{7,6},{5,7},{3,5},{1,3},{8,9},{10,8},{12,1... | collective-permute-start | bytes 1376264 | tf_op jit(solution)/shard_map/ppermute | solution.py:149
  35.9 18.8 %collective-permute-start.3 = (bf16[256,896]{1,0:T(8,128)(2,1)S(1)}, bf16[256,896]{1,0:T(8,128)(2,1)}, u32[]{:S(2)}, u32[]{:S(2)}) collective-permute-start(bf16[256,896]{1,0:T(8,128)(2,1)S(1)} %collective-permute-done.2.refs_0_), channel_id=1, source_target_pairs={{0,2},{2,4},{4,6},{6,7},{7,5},{5,3},{3,1},{1,0},{8,10},{10,12},{12... | collective-permute-start | bytes 1376264 | tf_op jit(solution)/shard_map/ppermute | solution.py:148
  44.8 10.0 %collective-permute-start.7 = (bf16[256,896]{1,0:T(8,128)(2,1)S(1)}, bf16[256,896]{1,0:T(8,128)(2,1)}, u32[]{:S(2)}, u32[]{:S(2)}) collective-permute-start(bf16[256,896]{1,0:T(8,128)(2,1)S(1)} %collective-permute-done.6.refs_1_), channel_id=1, source_target_pairs={{0,1},{2,0},{4,2},{6,4},{7,6},{5,7},{3,5},{1,3},{8,9},{10,8},{12,1... | collective-permute-start | bytes 1376264 | tf_op jit(solution)/shard_map/ppermute | solution.py:149
  45.0 0.8 copy-start.5
  46.0 38.7 %collective-permute-start.11 = (bf16[256,896]{1,0:T(8,128)(2,1)}, bf16[256,896]{1,0:T(8,128)(2,1)}, u32[]{:S(2)}, u32[]{:S(2)}) collective-permute-start(bf16[256,896]{1,0:T(8,128)(2,1)} %collective-permute-done.10.refs_0_), channel_id=1, source_target_pairs={{0,2},{2,4},{4,6},{6,7},{7,5},{5,3},{3,1},{1,0},{8,10},{10,12},{12... | collective-permute-start | bytes 1376264 | tf_op jit(solution)/shard_map/ppermute | solution.py:148
  54.7 30.0 %collective-permute-start.14 = (bf16[256,896]{1,0:T(8,128)(2,1)}, bf16[256,896]{1,0:T(8,128)(2,1)}, u32[]{:S(2)}, u32[]{:S(2)}) collective-permute-start(bf16[256,896]{1,0:T(8,128)(2,1)} %collective-permute-done.13.refs_1_), channel_id=1, source_target_pairs={{0,1},{2,0},{4,2},{6,4},{7,6},{5,7},{3,5},{1,3},{8,9},{10,8},{12,1... | collective-permute-start | bytes 1376264 | tf_op jit(solution)/shard_map/ppermute | solution.py:149
  54.8 33.0 %collective-permute-start.4 = (bf16[256,896]{1,0:T(8,128)(2,1)}, bf16[256,896]{1,0:T(8,128)(2,1)}, u32[]{:S(2)}, u32[]{:S(2)}) collective-permute-start(bf16[256,896]{1,0:T(8,128)(2,1)} %collective-permute-done.3.refs_0_), channel_id=1, source_target_pairs={{0,2},{2,4},{4,6},{6,7},{7,5},{5,3},{3,1},{1,0},{8,10},{10,12},{12... | collective-permute-start | bytes 1376264 | tf_op jit(solution)/shard_map/ppermute | solution.py:148
  56.1 31.7 %collective-permute-start.8 = (bf16[256,896]{1,0:T(8,128)(2,1)}, bf16[256,896]{1,0:T(8,128)(2,1)}, u32[]{:S(2)}, u32[]{:S(2)}) collective-permute-start(bf16[256,896]{1,0:T(8,128)(2,1)} %collective-permute-done.7.refs_1_), channel_id=1, source_target_pairs={{0,1},{2,0},{4,2},{6,4},{7,6},{5,7},{3,5},{1,3},{8,9},{10,8},{12,1... | collective-permute-start | bytes 1376264 | tf_op jit(solution)/shard_map/ppermute | solution.py:149
  58.0 33.3 %collective-permute-start = (f32[64,768]{1,0:T(8,128)S(1)}, f32[64,768]{1,0:T(8,128)}, u32[]{:S(2)}, u32[]{:S(2)}) collective-permute-start(f32[64,768]{1,0:T(8,128)S(1)} %constant_dynamic-slice_fusion.1), channel_id=1, source_target_pairs={{0,8},{8,0},{1,9},{9,1},{2,10},{10,2},{3,11},{11,3},{4,12},{12,4},... | collective-permute-start | bytes 589832 | tf_op jit(solution)/shard_map/ppermute | solution.py:177
  63.6 2.0 %copy-start.1 = (bf16[7168,256]{1,0:T(8,128)(2,1)S(1)}, bf16[7168,256]{1,0:T(8,128)(2,1)}, u32[]{:S(2)}) copy-start(bf16[7168,256]{1,0:T(8,128)(2,1)} %refs_4_.15) | copy-start | bytes 11010052
  65.7 2.0 %copy-start.3 = (bf16[7168,256]{1,0:T(8,128)(2,1)S(1)}, bf16[7168,256]{1,0:T(8,128)(2,1)}, u32[]{:S(2)}) copy-start(bf16[7168,256]{1,0:T(8,128)(2,1)} %refs_3_.15) | copy-start | bytes 11010052
  67.7 2.0 %copy-start.2 = (bf16[7168,256]{1,0:T(8,128)(2,1)S(1)}, bf16[7168,256]{1,0:T(8,128)(2,1)}, u32[]{:S(2)}) copy-start(bf16[7168,256]{1,0:T(8,128)(2,1)} %refs_4_.15) | copy-start | bytes 11010052
  67.7 3.2 %copy-start.4 = (bf16[7168,256]{1,0:T(8,128)(2,1)S(1)}, bf16[7168,256]{1,0:T(8,128)(2,1)}, u32[]{:S(2)}) copy-start(bf16[7168,256]{1,0:T(8,128)(2,1)} %refs_3_.15) | copy-start | bytes 11010052
  73.4 2.5 %copy-start.6 = (bf16[256,896]{1,0:T(8,128)(2,1)S(1)}, bf16[256,896]{1,0:T(8,128)(2,1)}, u32[]{:S(2)}) copy-start(bf16[256,896]{1,0:T(8,128)(2,1)} %copy-done.5) | copy-start | bytes 1376260
  87.9 3.4 %copy-start.9 = (f32[128,768]{1,0:T(8,128)S(1)}, f32[128,768]{1,0:T(8,128)}, u32[]{:S(2)}) copy-start(f32[128,768]{1,0:T(8,128)} %pad_maximum_fusion) | copy-start | bytes 1179652
  91.1 1.6 %collective-permute-start.17 = (bf16[256,512]{1,0:T(8,128)(2,1)S(1)}, bf16[256,512]{1,0:T(8,128)(2,1)S(1)}, u32[]{:S(2)}, u32[]{:S(2)}) collective-permute-start(bf16[256,512]{1,0:T(8,128)(2,1)S(1)} %shard_map.89.own_ref), channel_id=1, source_target_pairs={{0,8},{8,0},{1,9},{9,1},{2,10},{10,2},{3,11},{11,3},{4,12},{12,4},... | collective-permute-start | bytes 786440 | tf_op jit(solution)/shard_map/ppermute | solution.py:202

commit v2 on v1

v2 whole, which is shorter than its diff:
```python
import functools

import jax
import jax.numpy as jnp
import numpy as np
from jax import lax
from jax.experimental import pallas as pl
from jax.experimental.pallas import tpu as pltpu
from jax.sharding import PartitionSpec as P

HS = 128


def ring_order(n):
    if n == 8:
        return [0, 2, 4, 6, 7, 5, 3, 1]
    return list(range(n))


def step_kernel(count, first, rows_ref, *refs):
    more = first >= 0
    items, refs = refs[:count], refs[count:]
    if count:
        acc_ref, now_ref, refs = refs[0], refs[1], refs[2:]
    if more:
        near, far = refs[:2], refs[2:4]
        next_ref, sems = refs[-2:]
        depth = next_ref.shape[1]
        cols = near[0].shape[1]

        def copies(i, sources):
            start = pl.multiple_of(rows_ref[2 * (first + i)], 32)
            return [
                pltpu.make_async_copy(
                    src.at[pl.ds(start, depth), :],
                    next_ref.at[i, :, pl.ds(part * cols, cols)],
                    sems.at[i, part],
                )
                for part, src in enumerate(sources)
            ]

        for i in range(2):

            @pl.when(rows_ref[2 * (first + i) + 1] == 0)
            def _():
                for copy in copies(i, near):
                    copy.start()

            @pl.when(rows_ref[2 * (first + i) + 1] != 0)
            def _():
                for copy in copies(i, far):
                    copy.start()

    if count:
        out_ref = refs[4] if more else refs[0]
        total = acc_ref[...] if acc_ref.shape[0] == items[0].shape[0] else 0.0
        for i in range(count):
            total = total + jnp.dot(items[i][...], now_ref[i], preferred_element_type=jnp.float32)
        out_ref[...] = total.astype(out_ref.dtype)
    if more:
        for i in range(2):
            for copy in copies(i, near):
                copy.wait()


def step(items, acc, now, rows, first, weights, depth, dtype=jnp.float32):
    count, more = len(items), first >= 0
    cols = 2 * weights[0].shape[1]
    vmem = pl.BlockSpec(memory_space=pltpu.VMEM)
    operands, specs = [rows, *items], [pl.BlockSpec(memory_space=pltpu.SMEM)] + [vmem] * count
    shapes = []
    if count:
        tok = items[0].shape[0]
        operands += [acc, now]
        specs += [vmem] * 2
        shapes.append(jax.ShapeDtypeStruct((tok, cols), dtype))
    if more:
        operands += weights
        specs += [pl.BlockSpec(memory_space=pl.ANY)] * 4
        shapes.append(jax.ShapeDtypeStruct((2, depth, cols), jnp.bfloat16))
    return pl.pallas_call(
        functools.partial(step_kernel, count, first),
        out_shape=shapes,
        in_specs=specs,
        out_specs=[vmem] * len(shapes),
        scratch_shapes=[pltpu.SemaphoreType.DMA((2, 2))] if more else [],
        compiler_params=pltpu.CompilerParams(vmem_limit_bytes=40 * 1024 * 1024),
        cost_estimate=pl.CostEstimate(flops=0, bytes_accessed=0, transcendentals=0),
    )(*operands)


def decode_kernel(rows_ref, wq_ref, wk_ref, wv_ref, out_ref, flat):
    count, steps, _ = rows_ref.shape
    cols = wq_ref.shape[1]
    for r in range(count):
        flat[r * steps : (r + 1) * steps] = rows_ref[r].astype(jnp.float32)
    rows = flat[...].astype(jnp.bfloat16)
    for part, ref in enumerate((wq_ref, wk_ref, wv_ref)):
        term = jnp.dot(rows, ref[...], preferred_element_type=jnp.float32)
        at = slice(part * cols, (part + 1) * cols)

        @pl.when(pl.program_id(0) == 0)
        def _():
            out_ref[:, at] = term

        @pl.when(pl.program_id(0) != 0)
        def _():
            out_ref[:, at] += term


def decode(rows, weights, block):
    count, steps, depth = rows.shape
    cols = weights[0].shape[1]
    return pl.pallas_call(
        decode_kernel,
        out_shape=jax.ShapeDtypeStruct((count * steps, 3 * cols), jnp.float32),
        grid=(depth // block,),
        in_specs=[pl.BlockSpec((count, steps, block), lambda i: (0, 0, i))]
        + [pl.BlockSpec((block, cols), lambda i: (i, 0))] * 3,
        out_specs=pl.BlockSpec((count * steps, 3 * cols), lambda i: (0, 0)),
        scratch_shapes=[pltpu.VMEM((count * steps, block), jnp.float32)],
        compiler_params=pltpu.CompilerParams(vmem_limit_bytes=56 * 1024 * 1024),
        cost_estimate=pl.CostEstimate(flops=0, bytes_accessed=0, transcendentals=0),
    )(rows, *weights)


def attend_kernel(steps, slope_ref, fresh_ref, own_ref, far_ref, place_ref, span_ref, out_ref):
    rows = fresh_ref.shape[0]
    cols = fresh_ref.shape[1] // 3
    tok = own_ref.shape[0]
    scale = 1.0 / HS**0.5
    start = span_ref[:, 0:1]
    length = span_ref[:, 1:2]
    row = lax.broadcasted_iota(jnp.int32, (rows, 1), 0)
    step_of = row % steps
    rel = place_ref[...] - start
    valid = (rel >= 0) & (rel < length)
    dist = (length + step_of - rel).astype(jnp.float32)
    col = lax.broadcasted_iota(jnp.int32, (1, rows), 1)
    near_ok = (row // steps == col // steps) & (col <= row)
    near_dist = (row - col).astype(jnp.float32)
    nt = (((1,), (1,)), ((), ()))
    for head in range(cols // HS):
        slope = slope_ref[head]
        query = fresh_ref[:, head * HS : (head + 1) * HS]
        fresh_key = fresh_ref[:, cols + head * HS : cols + (head + 1) * HS]
        fresh_value = fresh_ref[:, 2 * cols + head * HS : 2 * cols + (head + 1) * HS]
        scores = []
        for part, ref in enumerate((own_ref, far_ref)):
            key = ref[:, head * HS : (head + 1) * HS]
            ctx = lax.dot_general(query, key, nt, preferred_element_type=jnp.float32) * scale
            ctx = ctx - slope * dist[:, part * tok : (part + 1) * tok]
            scores.append(jnp.where(valid[:, part * tok : (part + 1) * tok], ctx, -1e30))
        near = lax.dot_general(query, fresh_key, nt, preferred_element_type=jnp.float32) * scale
        scores.append(jnp.where(near_ok, near - slope * near_dist, -1e30))
        top = functools.reduce(jnp.maximum, [jnp.max(s, axis=1, keepdims=True) for s in scores])
        exps = [jnp.exp(s - top) for s in scores]
        total = sum(jnp.sum(e, axis=1, keepdims=True) for e in exps)
        weights = [(e / total).astype(jnp.bfloat16) for e in exps]
        values = [ref[:, cols + head * HS : cols + (head + 1) * HS] for ref in (own_ref, far_ref)]
        values.append(fresh_value)
        out = sum(
            jnp.dot(w, v, preferred_element_type=jnp.float32) for w, v in zip(weights, values)
        )
        out = out.astype(out_ref.dtype)
        for r in range(rows // steps):
            out_ref[r, :, head * HS : (head + 1) * HS] = out[r * steps : (r + 1) * steps]


def on_device(hidden, slot_tokens, lengths, decode_rows, query_weight, key_weight, value_weight):
    group = lax.axis_index("head")
    owner = lax.axis_index("pre")
    n = lax.axis_size("head")
    own_tok, width = hidden.shape
    depth = key_weight.shape[0]
    cols = key_weight.shape[1]
    heads_dev = cols // HS
    req_dev, steps = lengths.shape[1], decode_rows.shape[1]
    rows_dev = req_dev * steps
    swap = [(0, 1), (1, 0)]

    order = ring_order(n)
    up = [(order[i], order[(i + 1) % n]) for i in range(n)]
    down = [(order[i], order[(i - 1) % n]) for i in range(n)]
    place = [0] * n
    for i, g in enumerate(order):
        place[g] = i
    half = width // 2
    block = 896 if depth % 896 == 0 else depth

    own = [hidden[:, :half], hidden[:, half:]]
    seen = [((0, 0), (0, 1))] + [
        ((-(k // 2 + 1), k % 2), (k // 2 + 1, 1 - k % 2)) for k in range(n - 1)
    ]
    table = np.zeros((2 * n, 4 * len(seen)), np.int32)
    for g in range(n):
        for k, (distance, part) in enumerate(sum(seen, ())):
            row = order[(place[g] + distance) % n] * width + part * half
            for p in range(2):
                table[2 * g + p, 2 * k : 2 * k + 2] = row % depth, row // depth != p
    rows_of = lax.dynamic_slice_in_dim(jnp.asarray(table), 2 * group + owner, 1, 0)[0]

    def send(pair):
        moving.append((lax.ppermute(pair[0], "head", up), lax.ppermute(pair[1], "head", down)))

    tie = lax.optimization_barrier
    moving = []
    for k in range(2):
        send((own[k % 2], own[1 - k % 2]))
    sums = decode(decode_rows, (query_weight, key_weight, value_weight), block)
    key_far = lax.ppermute(key_weight, "pre", swap)
    moving[0], key_far, second, sums, slot_tokens, lengths = tie(
        (moving[0], key_far, value_weight, sums, slot_tokens, lengths)
    )
    send(moving[0])
    weights = (key_weight, value_weight, key_far, lax.ppermute(second, "pre", swap))

    mine = lax.dynamic_slice_in_dim(slot_tokens, owner * own_tok, own_tok)
    lane = jnp.arange(2 * own_tok, dtype=jnp.int32)
    token = (lane + owner * own_tok) % (2 * own_tok)
    slot = jnp.arange(1, own_tok + 1, dtype=jnp.int32)
    where = jnp.sum(jnp.where(mine[:, None] == token[None, :], slot[:, None], 0), axis=0, keepdims=True)
    lens = lengths[0]
    starts = jnp.cumsum(lens) - lens
    where = jnp.where(where == 0, -(1 << 20), where - 1)
    span = jnp.repeat(jnp.stack([starts, lens], axis=1), steps, axis=0)
    heads_index = (group * heads_dev + jnp.arange(heads_dev)).astype(jnp.float32)
    slope = jnp.exp2(-8.0 * (heads_index + 1.0) / (heads_dev * n))

    moving[1], sums, where, span, slope = tie((moving[1], sums, where, span, slope))
    send(moving[1])
    keep = lax.dynamic_slice_in_dim(sums, owner * rows_dev, rows_dev, 0)
    give = lax.dynamic_slice_in_dim(sums, (1 - owner) * rows_dev, rows_dev, 0)

    moving[2], weights, keep, give = tie((moving[2], weights, keep, give))
    fresh = (keep + lax.ppermute(give, "pre", swap)).astype(jnp.bfloat16)
    (now,) = step([], None, None, rows_of, 0, weights, half)
    acc = jnp.zeros((8, 128), jnp.float32)
    waiting, done = [own] + moving[:2], 0
    for k in range(2, n - 1):
        if k > 2:
            moving[k], acc, now, fresh = tie((moving[k], acc, now, fresh))
        if k + 2 < n - 1:
            send(moving[k])
        waiting.append(moving[k])
        for _ in range(2 if len(waiting) > 1 else 1):
            if len(waiting) > 1 or k < n - 2:
                done += 1
                acc, now = step(waiting.pop(0), acc, now, rows_of, 2 * done, weights, half)
    (acc,) = step(waiting[0], acc, now, rows_of, -1, weights, half, jnp.bfloat16)
    far = lax.ppermute(acc, "pre", swap)
    vmem = pl.BlockSpec(memory_space=pltpu.VMEM)
    return pl.pallas_call(
        functools.partial(attend_kernel, steps),
        out_shape=jax.ShapeDtypeStruct((req_dev, steps, cols), jnp.bfloat16),
        in_specs=[pl.BlockSpec(memory_space=pltpu.SMEM)] + [vmem] * 5,
        out_specs=vmem,
        compiler_params=pltpu.CompilerParams(vmem_limit_bytes=16 * 1024 * 1024),
    )(slope, fresh, acc, far, where, span)


def solution(mesh):
    in_specs = (
        P(("grp", "pre"), "head"),
        P("grp"),
        P(("grp", "pre"), None),
        P("grp", None, "pre"),
        P("pre", "head"),
        P("pre", "head"),
        P("pre", "head"),
    )
    out_specs = P(("grp", "pre"), None, "head")
    return jax.shard_map(
        on_device, mesh=mesh, in_specs=in_specs, out_specs=out_specs, check_vma=False
    )
```

time: 95.3 us -> 87.8 us (0.921)
  the two profiles are of different devices: /device:TPU:17 before, /device:TPU:0 now
where the time goes in v2:
time: 87.8 us; the launch traced here: 87.1 us
  Pallas kernels  32.4 us (37%)
  waiting for transfers between devices  27.5 us (31%)
  starting transfers between devices  15.8 us (18%)
  local copies, waits for them, and re-layouts  10 us (11%)
  other arithmetic  1.19 us (1%)
    pallas_call x9, Pallas kernels, step(): pl.pallas_call(functools.partial(step_kernel, count, first), out_shape=sh...  19.4 us
    ppermute x7, waiting for transfers between devices, send(): lax.ppermute(pair[0], 'head', up)  19 us
    ppermute x7, starting transfers between devices, send(): lax.ppermute(pair[0], 'head', up)  13.5 us
    pallas_call x1, Pallas kernels, decode(): pl.pallas_call(decode_kernel, out_shape=jax.ShapeDtypeStruct((count * ste...  10.9 us
    ppermute x7, waiting for transfers between devices, send(): lax.ppermute(pair[1], 'head', down)  7.06 us
    unnamed x10, local copies, waits for them, and re-layouts  5.88 us
    pallas_call x1, Pallas kernels, on_device(): pl.pallas_call(functools.partial(attend_kernel, steps), out_shape=jax.Sha...  2.04 us
    ppermute x7, starting transfers between devices, send(): lax.ppermute(pair[1], 'head', down)  1.83 us
  transfers between devices with their start and end apart: 18, of which 10 were waited for; matrix products, arithmetic and copies ran while one was open for 6% of the time, Pallas kernels for 33%

profile of v2, /device:TPU:0, one launch (start us, length us, event | category | flops | bytes accessed | tf_op | source)
XLA Modules:
  0.0 87.1 jit_solution(602473481628113038)
XLA Ops:
  0.0 0.5 collective-permute-start.4
  0.5 1.2 %fusion.2 = (bf16[256,896]{1,0:T(8,128)(2,1)S(1)}, bf16[256,896]{1,0:T(8,128)(2,1)S(1)}) fusion(bf16[256,1792]{1,0:T(8,128)(2,1)} %param.8), kind=kLoop, calls=%fused_computation.14 | loop fusion | bytes 1835008 | tf_op jit(solution)/shard_map/slice | solution.py:191
  1.7 2.6 %collective-permute-start.2 = (bf16[256,896]{1,0:T(8,128)(2,1)S(1)}, bf16[256,896]{1,0:T(8,128)(2,1)S(1)}, u32[]{:S(2)}, u32[]{:S(2)}) collective-permute-start(bf16[256,896]{1,0:T(8,128)(2,1)S(1)} %get-tuple-element.115.refs_0_), channel_id=1, source_target_pairs={{0,2},{2,4},{4,6},{6,7},{7,5},{5,3},{3,1},{1,0},{8,10},{10,12},{12... | collective-permute-start | bytes 1376264 | tf_op jit(solution)/shard_map/ppermute | solution.py:204
  4.3 0.0 copy-start.4
  4.3 0.0 collective-permute-start.3
  4.3 10.9 %shard_map.82 = f32[128,768]{1,0:T(8,128)} custom-call(bf16[32,4,7168]{2,1,0:T(4,128)(2,1)} %rows_ref.1, bf16[7168,256]{1,0:T(8,128)(2,1)} %wq_ref.1, bf16[7168,256]{1,0:T(8,128)(2,1)} %refs_4_.6, bf16[7168,256]{1,0:T(8,128)(2,1)} %refs_5_.6), custom_call_target="tpu_custom_call" | custom-call | tf_op jit(solution)/shard_map/pallas_call | solution.py:114
  15.3 0.2 collective-permute-done.2.refs_0_
  15.4 1.5 %collective-permute-done.3.refs_1_ = bf16[256,896]{1,0:T(8,128)(2,1)S(1)} collective-permute-done((bf16[256,896]{1,0:T(8,128)(2,1)S(1)}, bf16[256,896]{1,0:T(8,128)(2,1)S(1)}, u32[]{:S(2)}, u32[]{:S(2)}) %collective-permute-start.3) | collective-permute-done | bytes 458784 | tf_op jit(solution)/shard_map/ppermute | solution.py:204
  17.0 0.0 collective-permute-done.4.refs_2_.refs_6_
  17.0 1.8 %copy-done.1 = bf16[7168,256]{1,0:T(8,128)(2,1)} copy-done((bf16[7168,256]{1,0:T(8,128)(2,1)}, bf16[7168,256]{1,0:T(8,128)(2,1)S(1)}, u32[]{:S(2)}) %copy-start.1) | copy-done | bytes 3670040
  18.8 0.0 collective-permute-start.7
  18.8 1.6 %collective-permute-start = (bf16[256,896]{1,0:T(8,128)(2,1)S(1)}, bf16[256,896]{1,0:T(8,128)(2,1)S(1)}, u32[]{:S(2)}, u32[]{:S(2)}) collective-permute-start(bf16[256,896]{1,0:T(8,128)(2,1)S(1)} %get-tuple-element.116.refs_1_), channel_id=1, source_target_pairs={{0,2},{2,4},{4,6},{6,7},{7,5},{5,3},{3,1},{1,0},{8,10},{10,12},{12... | collective-permute-start | bytes 1376264 | tf_op jit(solution)/shard_map/ppermute | solution.py:204
  20.3 0.4 collective-permute-start.1
  20.8 0.0 copy-done.3
  20.8 0.1 copy.23
  21.0 0.1 copy.25
  21.1 0.1 broadcast_in_dim.29
  21.1 0.1 reshape.64
  21.2 1.6 %collective-permute-start.5 = (bf16[256,896]{1,0:T(8,128)(2,1)S(1)}, bf16[256,896]{1,0:T(8,128)(2,1)}, u32[]{:S(2)}, u32[]{:S(2)}) collective-permute-start(bf16[256,896]{1,0:T(8,128)(2,1)S(1)} %collective-permute-done.2.refs_0_), channel_id=1, source_target_pairs={{0,2},{2,4},{4,6},{6,7},{7,5},{5,3},{3,1},{1,0},{8,10},{10,12},{12... | collective-permute-start | bytes 1376264 | tf_op jit(solution)/shard_map/ppermute | solution.py:204
  22.9 0.4 collective-permute-start.6
  23.3 0.0 copy-done.4
  23.3 0.1 dynamic_slice.12
  23.4 0.1 select_reduce_fusion
  23.5 8.5 %collective-permute-done.refs_0_ = bf16[256,896]{1,0:T(8,128)(2,1)S(1)} collective-permute-done((bf16[256,896]{1,0:T(8,128)(2,1)S(1)}, bf16[256,896]{1,0:T(8,128)(2,1)S(1)}, u32[]{:S(2)}, u32[]{:S(2)}) %collective-permute-start) | collective-permute-done | bytes 458784 | tf_op jit(solution)/shard_map/ppermute | solution.py:204
  32.1 1.6 %collective-permute-done.1.refs_1_ = bf16[256,896]{1,0:T(8,128)(2,1)S(1)} collective-permute-done((bf16[256,896]{1,0:T(8,128)(2,1)S(1)}, bf16[256,896]{1,0:T(8,128)(2,1)S(1)}, u32[]{:S(2)}, u32[]{:S(2)}) %collective-permute-start.1) | collective-permute-done | bytes 458784 | tf_op jit(solution)/shard_map/ppermute | solution.py:204
  33.7 1.6 %collective-permute-start.10 = (bf16[256,896]{1,0:T(8,128)(2,1)S(1)}, bf16[256,896]{1,0:T(8,128)(2,1)S(1)}, u32[]{:S(2)}, u32[]{:S(2)}) collective-permute-start(bf16[256,896]{1,0:T(8,128)(2,1)S(1)} %collective-permute-done.refs_0_), channel_id=1, source_target_pairs={{0,2},{2,4},{4,6},{6,7},{7,5},{5,3},{3,1},{1,0},{8,10},{10,12},{12... | collective-permute-start | bytes 1376264 | tf_op jit(solution)/shard_map/ppermute | solution.py:204
  35.3 0.4 collective-permute-start.11
  35.7 1.7 %constant_dynamic-slice_fusion.1 = (f32[64,768]{1,0:T(8,128)}, f32[64,768]{1,0:T(8,128)S(1)}) fusion(f32[128,768]{1,0:T(8,128)} %shard_map.82, s32[]{:T(128)S(6)} %select_n.48, s32[]{:T(128)S(6)} %select_n.47), kind=kLoop, calls=%fused_computation.10 | loop fusion | bytes 786440 | tf_op jit(solution)/shard_map/dynamic_slice | solution.py:233
  37.5 4.6 %collective-permute-done.5.refs_0_ = bf16[256,896]{1,0:T(8,128)(2,1)} collective-permute-done((bf16[256,896]{1,0:T(8,128)(2,1)S(1)}, bf16[256,896]{1,0:T(8,128)(2,1)}, u32[]{:S(2)}, u32[]{:S(2)}) %collective-permute-start.5) | collective-permute-done | bytes 458784 | tf_op jit(solution)/shard_map/ppermute | solution.py:204
  42.0 1.6 %collective-permute-done.6.refs_1_ = bf16[256,896]{1,0:T(8,128)(2,1)} collective-permute-done((bf16[256,896]{1,0:T(8,128)(2,1)S(1)}, bf16[256,896]{1,0:T(8,128)(2,1)}, u32[]{:S(2)}, u32[]{:S(2)}) %collective-permute-start.6) | collective-permute-done | bytes 458784 | tf_op jit(solution)/shard_map/ppermute | solution.py:204
  43.6 0.0 collective-permute-done.7.refs_3_.refs_7_
  43.6 1.6 %collective-permute-start.8 = (bf16[256,896]{1,0:T(8,128)(2,1)}, bf16[256,896]{1,0:T(8,128)(2,1)}, u32[]{:S(2)}, u32[]{:S(2)}) collective-permute-start(bf16[256,896]{1,0:T(8,128)(2,1)} %collective-permute-done.5.refs_0_), channel_id=1, source_target_pairs={{0,2},{2,4},{4,6},{6,7},{7,5},{5,3},{3,1},{1,0},{8,10},{10,12},{12... | collective-permute-start | bytes 1376264 | tf_op jit(solution)/shard_map/ppermute | solution.py:204
  45.2 0.4 collective-permute-start.9
  45.7 0.0 collective-permute-start.12
  45.7 0.7 fusion.1.rows_ref
  46.4 2.0 %copy-done = bf16[7168,256]{1,0:T(8,128)(2,1)S(1)} copy-done((bf16[7168,256]{1,0:T(8,128)(2,1)S(1)}, bf16[7168,256]{1,0:T(8,128)(2,1)}, u32[]{:S(2)}) %copy-start) | copy-done | bytes 3670040
  48.4 2.0 %copy-done.2 = bf16[7168,256]{1,0:T(8,128)(2,1)S(1)} copy-done((bf16[7168,256]{1,0:T(8,128)(2,1)S(1)}, bf16[7168,256]{1,0:T(8,128)(2,1)}, u32[]{:S(2)}) %copy-start.2) | copy-done | bytes 3670040
  50.5 1.8 %shard_map.83.refs_3_ = bf16[2,896,512]{2,1,0:T(8,128)(2,1)S(1)} custom-call(s32[32]{0:T(128)S(1)} %fusion.1.rows_ref, bf16[7168,256]{1,0:T(8,128)(2,1)S(1)} %copy-done, bf16[7168,256]{1,0:T(8,128)(2,1)} %refs_5_.6, bf16[7168,256]{1,0:T(8,128)(2,1)S(1)} %copy-done.2, bf16[7168,256]{1,0:T(8,128)(2,1)} %collective-permute-done.7.refs_3_.refs_7_), custom_call_target="tpu_custom_call" | custom-call | tf_op jit(solution)/shard_map/pallas_call | solution.py:81
  52.3 1.8 %shard_map.84 = (f32[256,512]{1,0:T(8,128)S(1)}, bf16[2,896,512]{2,1,0:T(8,128)(2,1)S(1)}) custom-call(s32[32]{0:T(128)S(1)} %fusion.1.rows_ref, bf16[256,896]{1,0:T(8,128)(2,1)S(1)} %get-tuple-element.115.refs_0_, bf16[256,896]{1,0:T(8,128)(2,1)S(1)} %get-tuple-element.116.refs_1_, f32[8,128]{1,0:T(8,128)S(1)} %broadcast_in_dim.30.refs_2_, ...), custom_call_target="tpu_custom_call" | custom-call | tf_op jit(solution)/shard_map/pallas_call | solution.py:81
  54.1 1.8 %shard_map.85 = (f32[256,512]{1,0:T(8,128)S(1)}, bf16[2,896,512]{2,1,0:T(8,128)(2,1)S(1)}) custom-call(s32[32]{0:T(128)S(1)} %fusion.1.rows_ref, bf16[256,896]{1,0:T(8,128)(2,1)S(1)} %collective-permute-done.2.refs_0_, bf16[256,896]{1,0:T(8,128)(2,1)S(1)} %collective-permute-done.3.refs_1_, f32[256,512]{1,0:T(8,128)S(1)} %get-tuple-element.77.refs_2_, ...), custom_call_target="tpu_custom_call" | custom-call | tf_op jit(solution)/shard_map/pallas_call | solution.py:81
  55.9 0.0 collective-permute-done.12
  55.9 1.0 %add_convert_fusion.fresh_ref = bf16[64,768]{1,0:T(8,128)(2,1)S(1)} fusion(f32[64,768]{1,0:T(8,128)S(1)} %get-tuple-element.81, f32[64,768]{1,0:T(8,128)} %collective-permute-done.12), kind=kLoop, calls=%fused_computation.1 | loop fusion | flops 98304 | bytes 491520 | tf_op jit(solution)/shard_map/convert_element_type | solution.py:236
  56.8 0.0 collective-permute-done.10.refs_0_
  56.8 0.0 collective-permute-done.11.refs_1_
  56.8 2.4 %collective-permute-start.15 = (bf16[256,896]{1,0:T(8,128)(2,1)S(1)}, bf16[256,896]{1,0:T(8,128)(2,1)S(1)}, u32[]{:S(2)}, u32[]{:S(2)}) collective-permute-start(bf16[256,896]{1,0:T(8,128)(2,1)S(1)} %collective-permute-done.10.refs_0_), channel_id=1, source_target_pairs={{0,2},{2,4},{4,6},{6,7},{7,5},{5,3},{3,1},{1,0},{8,10},{10,12},{12... | collective-permute-start | bytes 1376264 | tf_op jit(solution)/shard_map/ppermute | solution.py:204
  59.2 0.0 collective-permute-start.16
  59.2 2.1 %shard_map.86 = (f32[256,512]{1,0:T(8,128)S(1)}, bf16[2,896,512]{2,1,0:T(8,128)(2,1)S(1)}) custom-call(s32[32]{0:T(128)S(1)} %fusion.1.rows_ref, bf16[256,896]{1,0:T(8,128)(2,1)S(1)} %collective-permute-done.refs_0_, bf16[256,896]{1,0:T(8,128)(2,1)S(1)} %collective-permute-done.1.refs_1_, f32[256,512]{1,0:T(8,128)S(1)} %get-tuple-element.83.refs_2_, ...), custom_call_target="tpu_custom_call" | custom-call | tf_op jit(solution)/shard_map/pallas_call | solution.py:81
  61.4 2.9 %shard_map.87 = (f32[256,512]{1,0:T(8,128)S(1)}, bf16[2,896,512]{2,1,0:T(8,128)(2,1)S(1)}) custom-call(s32[32]{0:T(128)S(1)} %fusion.1.rows_ref, bf16[256,896]{1,0:T(8,128)(2,1)} %collective-permute-done.5.refs_0_, bf16[256,896]{1,0:T(8,128)(2,1)} %collective-permute-done.6.refs_1_, f32[256,512]{1,0:T(8,128)S(1)} %get-tuple-element.85.refs_2_, ...), custom_call_target="tpu_custom_call" | custom-call | tf_op jit(solution)/shard_map/pallas_call | solution.py:81
  64.3 0.0 collective-permute-done.8.refs_0_
  64.3 0.0 collective-permute-done.9.refs_1_
  64.3 2.1 %collective-permute-start.13 = (bf16[256,896]{1,0:T(8,128)(2,1)}, bf16[256,896]{1,0:T(8,128)(2,1)S(1)}, u32[]{:S(2)}, u32[]{:S(2)}) collective-permute-start(bf16[256,896]{1,0:T(8,128)(2,1)} %collective-permute-done.8.refs_0_), channel_id=1, source_target_pairs={{0,2},{2,4},{4,6},{6,7},{7,5},{5,3},{3,1},{1,0},{8,10},{10,12},{12... | collective-permute-start | bytes 1376264 | tf_op jit(solution)/shard_map/ppermute | solution.py:204
  66.4 0.0 collective-permute-start.14
  66.4 2.7 %shard_map.88 = (f32[256,512]{1,0:T(8,128)S(1)}, bf16[2,896,512]{2,1,0:T(8,128)(2,1)S(1)}) custom-call(s32[32]{0:T(128)S(1)} %fusion.1.rows_ref, bf16[256,896]{1,0:T(8,128)(2,1)S(1)} %collective-permute-done.10.refs_0_, bf16[256,896]{1,0:T(8,128)(2,1)} %collective-permute-done.11.refs_1_, f32[256,512]{1,0:T(8,128)S(1)} %get-tuple-element.94.refs_2_, ...), custom_call_target="tpu_custom_call" | custom-call | tf_op jit(solution)/shard_map/pallas_call | solution.py:81
  69.1 2.9 %shard_map.89 = (f32[256,512]{1,0:T(8,128)S(1)}, bf16[2,896,512]{2,1,0:T(8,128)(2,1)S(1)}) custom-call(s32[32]{0:T(128)S(1)} %fusion.1.rows_ref, bf16[256,896]{1,0:T(8,128)(2,1)} %collective-permute-done.8.refs_0_, bf16[256,896]{1,0:T(8,128)(2,1)} %collective-permute-done.9.refs_1_, f32[256,512]{1,0:T(8,128)S(1)} %get-tuple-element.96.refs_2_, ...), custom_call_target="tpu_custom_call" | custom-call | tf_op jit(solution)/shard_map/pallas_call | solution.py:81
  72.0 0.0 collective-permute-done.15.refs_0_
  72.0 1.0 %collective-permute-done.16.refs_1_ = bf16[256,896]{1,0:T(8,128)(2,1)S(1)} collective-permute-done((bf16[256,896]{1,0:T(8,128)(2,1)}, bf16[256,896]{1,0:T(8,128)(2,1)S(1)}, u32[]{:S(2)}, u32[]{:S(2)}) %collective-permute-start.16) | collective-permute-done | bytes 458784 | tf_op jit(solution)/shard_map/ppermute | solution.py:204
  73.0 2.1 %shard_map.90 = (f32[256,512]{1,0:T(8,128)S(1)}, bf16[2,896,512]{2,1,0:T(8,128)(2,1)S(1)}) custom-call(s32[32]{0:T(128)S(1)} %fusion.1.rows_ref, bf16[256,896]{1,0:T(8,128)(2,1)S(1)} %collective-permute-done.15.refs_0_, bf16[256,896]{1,0:T(8,128)(2,1)S(1)} %collective-permute-done.16.refs_1_, f32[256,512]{1,0:T(8,128)S(1)} %get-tuple-element.103.refs_2_, ...), custom_call_target="tpu_custom_call" | custom-call | tf_op jit(solution)/shard_map/pallas_call | solution.py:81
  75.2 5.7 %collective-permute-done.13.refs_0_ = bf16[256,896]{1,0:T(8,128)(2,1)S(1)} collective-permute-done((bf16[256,896]{1,0:T(8,128)(2,1)}, bf16[256,896]{1,0:T(8,128)(2,1)S(1)}, u32[]{:S(2)}, u32[]{:S(2)}) %collective-permute-start.13) | collective-permute-done | bytes 458784 | tf_op jit(solution)/shard_map/ppermute | solution.py:204
  80.9 1.3 %collective-permute-done.14.refs_1_ = bf16[256,896]{1,0:T(8,128)(2,1)S(1)} collective-permute-done((bf16[256,896]{1,0:T(8,128)(2,1)}, bf16[256,896]{1,0:T(8,128)(2,1)S(1)}, u32[]{:S(2)}, u32[]{:S(2)}) %collective-permute-start.14) | collective-permute-done | bytes 458784 | tf_op jit(solution)/shard_map/ppermute | solution.py:204
  82.2 1.3 %shard_map.91.own_ref = bf16[256,512]{1,0:T(8,128)(2,1)S(1)} custom-call(s32[32]{0:T(128)S(1)} %fusion.1.rows_ref, bf16[256,896]{1,0:T(8,128)(2,1)S(1)} %collective-permute-done.13.refs_0_, bf16[256,896]{1,0:T(8,128)(2,1)S(1)} %collective-permute-done.14.refs_1_, f32[256,512]{1,0:T(8,128)S(1)} %get-tuple-element.111.refs_2_, ...), custom_call_target="tpu_custom_call" | custom-call | tf_op jit(solution)/shard_map/pallas_call | solution.py:81
  83.4 0.1 collective-permute-start.17
  83.5 0.1 copy.26.span_ref
  83.6 1.4 %collective-permute-done.17.far_ref = bf16[256,512]{1,0:T(8,128)(2,1)S(1)} collective-permute-done((bf16[256,512]{1,0:T(8,128)(2,1)S(1)}, bf16[256,512]{1,0:T(8,128)(2,1)S(1)}, u32[]{:S(2)}, u32[]{:S(2)}) %collective-permute-start.17) | collective-permute-done | bytes 262176 | tf_op jit(solution)/shard_map/ppermute | solution.py:251
  85.0 2.0 %shard_map.92 = bf16[16,4,256]{2,1,0:T(4,128)(2,1)} custom-call(f32[2]{0:T(128)S(1)} %multiply_exponential_fusion.slope_ref, bf16[64,768]{1,0:T(8,128)(2,1)S(1)} %add_convert_fusion.fresh_ref, bf16[256,512]{1,0:T(8,128)(2,1)S(1)} %shard_map.91.own_ref, bf16[256,512]{1,0:T(8,128)(2,1)S(1)} %collective-permute-done.17.far_ref, s32[1,512]{1,0:T(1,128)S(1)} %bitcast.6, ...), custom_call_target="tpu_custom_call" | custom-call | tf_op jit(solution)/shard_map/pallas_call | solution.py:253
  (12 shorter events, 0.1 us)
Async XLA Ops:
  0.0 17.0 %collective-permute-start.4 = (bf16[7168,256]{1,0:T(8,128)(2,1)}, bf16[7168,256]{1,0:T(8,128)(2,1)S(1)}, u32[]{:S(2)}, u32[]{:S(2)}) collective-permute-start(bf16[7168,256]{1,0:T(8,128)(2,1)} %refs_4_.6), channel_id=1, source_target_pairs={{0,8},{8,0},{1,9},{9,1},{2,10},{10,2},{3,11},{11,3},{4,12},{12,4},... | collective-permute-start | bytes 11010056 | tf_op jit(solution)/shard_map/ppermute | solution.py:211
  1.7 13.8 %collective-permute-start.2 = (bf16[256,896]{1,0:T(8,128)(2,1)S(1)}, bf16[256,896]{1,0:T(8,128)(2,1)S(1)}, u32[]{:S(2)}, u32[]{:S(2)}) collective-permute-start(bf16[256,896]{1,0:T(8,128)(2,1)S(1)} %get-tuple-element.115.refs_0_), channel_id=1, source_target_pairs={{0,2},{2,4},{4,6},{6,7},{7,5},{5,3},{3,1},{1,0},{8,10},{10,12},{12... | collective-permute-start | bytes 1376264 | tf_op jit(solution)/shard_map/ppermute | solution.py:204
  4.3 16.5 %copy-start.3 = (s32[1,16]{1,0:T(1,128)S(1)}, s32[1,16]{1,0:T(1,128)}, u32[]{:S(2)}) copy-start(s32[1,16]{1,0:T(1,128)} %param.10) | copy-start | bytes 196
  4.3 19.0 %copy-start.4 = (s32[512]{0:T(512)S(1)}, s32[512]{0:T(512)}, u32[]{:S(2)}) copy-start(s32[512]{0:T(512)} %param.9) | copy-start | bytes 6148
  4.3 12.7 %collective-permute-start.3 = (bf16[256,896]{1,0:T(8,128)(2,1)S(1)}, bf16[256,896]{1,0:T(8,128)(2,1)S(1)}, u32[]{:S(2)}, u32[]{:S(2)}) collective-permute-start(bf16[256,896]{1,0:T(8,128)(2,1)S(1)} %get-tuple-element.116.refs_1_), channel_id=1, source_target_pairs={{0,1},{2,0},{4,2},{6,4},{7,6},{5,7},{3,5},{1,3},{8,9},{10,8},{12,1... | collective-permute-start | bytes 1376264 | tf_op jit(solution)/shard_map/ppermute | solution.py:204
  17.0 1.8 %copy-start.1 = (bf16[7168,256]{1,0:T(8,128)(2,1)}, bf16[7168,256]{1,0:T(8,128)(2,1)S(1)}, u32[]{:S(2)}) copy-start(bf16[7168,256]{1,0:T(8,128)(2,1)S(1)} %collective-permute-done.4.refs_2_.refs_6_) | copy-start | bytes 11010052
  18.8 24.9 %collective-permute-start.7 = (bf16[7168,256]{1,0:T(8,128)(2,1)}, bf16[7168,256]{1,0:T(8,128)(2,1)}, u32[]{:S(2)}, u32[]{:S(2)}) collective-permute-start(bf16[7168,256]{1,0:T(8,128)(2,1)} %refs_5_.6), channel_id=1, source_target_pairs={{0,8},{8,0},{1,9},{9,1},{2,10},{10,2},{3,11},{11,3},{4,12},{12,4},... | collective-permute-start | bytes 11010056 | tf_op jit(solution)/shard_map/ppermute | solution.py:216
  18.8 13.3 %collective-permute-start = (bf16[256,896]{1,0:T(8,128)(2,1)S(1)}, bf16[256,896]{1,0:T(8,128)(2,1)S(1)}, u32[]{:S(2)}, u32[]{:S(2)}) collective-permute-start(bf16[256,896]{1,0:T(8,128)(2,1)S(1)} %get-tuple-element.116.refs_1_), channel_id=1, source_target_pairs={{0,2},{2,4},{4,6},{6,7},{7,5},{5,3},{3,1},{1,0},{8,10},{10,12},{12... | collective-permute-start | bytes 1376264 | tf_op jit(solution)/shard_map/ppermute | solution.py:204
  20.3 13.4 %collective-permute-start.1 = (bf16[256,896]{1,0:T(8,128)(2,1)S(1)}, bf16[256,896]{1,0:T(8,128)(2,1)S(1)}, u32[]{:S(2)}, u32[]{:S(2)}) collective-permute-start(bf16[256,896]{1,0:T(8,128)(2,1)S(1)} %get-tuple-element.115.refs_0_), channel_id=1, source_target_pairs={{0,1},{2,0},{4,2},{6,4},{7,6},{5,7},{3,5},{1,3},{8,9},{10,8},{12,1... | collective-permute-start | bytes 1376264 | tf_op jit(solution)/shard_map/ppermute | solution.py:204
  21.2 20.8 %collective-permute-start.5 = (bf16[256,896]{1,0:T(8,128)(2,1)S(1)}, bf16[256,896]{1,0:T(8,128)(2,1)}, u32[]{:S(2)}, u32[]{:S(2)}) collective-permute-start(bf16[256,896]{1,0:T(8,128)(2,1)S(1)} %collective-permute-done.2.refs_0_), channel_id=1, source_target_pairs={{0,2},{2,4},{4,6},{6,7},{7,5},{5,3},{3,1},{1,0},{8,10},{10,12},{12... | collective-permute-start | bytes 1376264 | tf_op jit(solution)/shard_map/ppermute | solution.py:204
  22.9 20.8 %collective-permute-start.6 = (bf16[256,896]{1,0:T(8,128)(2,1)S(1)}, bf16[256,896]{1,0:T(8,128)(2,1)}, u32[]{:S(2)}, u32[]{:S(2)}) collective-permute-start(bf16[256,896]{1,0:T(8,128)(2,1)S(1)} %collective-permute-done.3.refs_1_), channel_id=1, source_target_pairs={{0,1},{2,0},{4,2},{6,4},{7,6},{5,7},{3,5},{1,3},{8,9},{10,8},{12,1... | collective-permute-start | bytes 1376264 | tf_op jit(solution)/shard_map/ppermute | solution.py:204
  33.7 23.1 %collective-permute-start.10 = (bf16[256,896]{1,0:T(8,128)(2,1)S(1)}, bf16[256,896]{1,0:T(8,128)(2,1)S(1)}, u32[]{:S(2)}, u32[]{:S(2)}) collective-permute-start(bf16[256,896]{1,0:T(8,128)(2,1)S(1)} %collective-permute-done.refs_0_), channel_id=1, source_target_pairs={{0,2},{2,4},{4,6},{6,7},{7,5},{5,3},{3,1},{1,0},{8,10},{10,12},{12... | collective-permute-start | bytes 1376264 | tf_op jit(solution)/shard_map/ppermute | solution.py:204
  35.3 21.6 %collective-permute-start.11 = (bf16[256,896]{1,0:T(8,128)(2,1)S(1)}, bf16[256,896]{1,0:T(8,128)(2,1)}, u32[]{:S(2)}, u32[]{:S(2)}) collective-permute-start(bf16[256,896]{1,0:T(8,128)(2,1)S(1)} %collective-permute-done.1.refs_1_), channel_id=1, source_target_pairs={{0,1},{2,0},{4,2},{6,4},{7,6},{5,7},{3,5},{1,3},{8,9},{10,8},{12,1... | collective-permute-start | bytes 1376264 | tf_op jit(solution)/shard_map/ppermute | solution.py:204
  43.6 20.6 %collective-permute-start.8 = (bf16[256,896]{1,0:T(8,128)(2,1)}, bf16[256,896]{1,0:T(8,128)(2,1)}, u32[]{:S(2)}, u32[]{:S(2)}) collective-permute-start(bf16[256,896]{1,0:T(8,128)(2,1)} %collective-permute-done.5.refs_0_), channel_id=1, source_target_pairs={{0,2},{2,4},{4,6},{6,7},{7,5},{5,3},{3,1},{1,0},{8,10},{10,12},{12... | collective-permute-start | bytes 1376264 | tf_op jit(solution)/shard_map/ppermute | solution.py:204
  45.2 19.1 %collective-permute-start.9 = (bf16[256,896]{1,0:T(8,128)(2,1)}, bf16[256,896]{1,0:T(8,128)(2,1)}, u32[]{:S(2)}, u32[]{:S(2)}) collective-permute-start(bf16[256,896]{1,0:T(8,128)(2,1)} %collective-permute-done.6.refs_1_), channel_id=1, source_target_pairs={{0,1},{2,0},{4,2},{6,4},{7,6},{5,7},{3,5},{1,3},{8,9},{10,8},{12,1... | collective-permute-start | bytes 1376264 | tf_op jit(solution)/shard_map/ppermute | solution.py:204
  45.7 10.2 %collective-permute-start.12 = (f32[64,768]{1,0:T(8,128)}, f32[64,768]{1,0:T(8,128)}, u32[]{:S(2)}, u32[]{:S(2)}) collective-permute-start(f32[64,768]{1,0:T(8,128)} %get-tuple-element.82), channel_id=1, source_target_pairs={{0,8},{8,0},{1,9},{9,1},{2,10},{10,2},{3,11},{11,3},{4,12},{12,4},... | collective-permute-start | bytes 589832 | tf_op jit(solution)/shard_map/ppermute | solution.py:236
  46.4 2.0 %copy-start = (bf16[7168,256]{1,0:T(8,128)(2,1)S(1)}, bf16[7168,256]{1,0:T(8,128)(2,1)}, u32[]{:S(2)}) copy-start(bf16[7168,256]{1,0:T(8,128)(2,1)} %refs_4_.6) | copy-start | bytes 11010052
  48.4 2.0 %copy-start.2 = (bf16[7168,256]{1,0:T(8,128)(2,1)S(1)}, bf16[7168,256]{1,0:T(8,128)(2,1)}, u32[]{:S(2)}) copy-start(bf16[7168,256]{1,0:T(8,128)(2,1)} %copy-done.1) | copy-start | bytes 11010052
  56.8 15.2 %collective-permute-start.15 = (bf16[256,896]{1,0:T(8,128)(2,1)S(1)}, bf16[256,896]{1,0:T(8,128)(2,1)S(1)}, u32[]{:S(2)}, u32[]{:S(2)}) collective-permute-start(bf16[256,896]{1,0:T(8,128)(2,1)S(1)} %collective-permute-done.10.refs_0_), channel_id=1, source_target_pairs={{0,2},{2,4},{4,6},{6,7},{7,5},{5,3},{3,1},{1,0},{8,10},{10,12},{12... | collective-permute-start | bytes 1376264 | tf_op jit(solution)/shard_map/ppermute | solution.py:204
  59.2 13.8 %collective-permute-start.16 = (bf16[256,896]{1,0:T(8,128)(2,1)}, bf16[256,896]{1,0:T(8,128)(2,1)S(1)}, u32[]{:S(2)}, u32[]{:S(2)}) collective-permute-start(bf16[256,896]{1,0:T(8,128)(2,1)} %collective-permute-done.11.refs_1_), channel_id=1, source_target_pairs={{0,1},{2,0},{4,2},{6,4},{7,6},{5,7},{3,5},{1,3},{8,9},{10,8},{12,1... | collective-permute-start | bytes 1376264 | tf_op jit(solution)/shard_map/ppermute | solution.py:204
  64.3 16.6 %collective-permute-start.13 = (bf16[256,896]{1,0:T(8,128)(2,1)}, bf16[256,896]{1,0:T(8,128)(2,1)S(1)}, u32[]{:S(2)}, u32[]{:S(2)}) collective-permute-start(bf16[256,896]{1,0:T(8,128)(2,1)} %collective-permute-done.8.refs_0_), channel_id=1, source_target_pairs={{0,2},{2,4},{4,6},{6,7},{7,5},{5,3},{3,1},{1,0},{8,10},{10,12},{12... | collective-permute-start | bytes 1376264 | tf_op jit(solution)/shard_map/ppermute | solution.py:204
  66.4 15.8 %collective-permute-start.14 = (bf16[256,896]{1,0:T(8,128)(2,1)}, bf16[256,896]{1,0:T(8,128)(2,1)S(1)}, u32[]{:S(2)}, u32[]{:S(2)}) collective-permute-start(bf16[256,896]{1,0:T(8,128)(2,1)} %collective-permute-done.9.refs_1_), channel_id=1, source_target_pairs={{0,1},{2,0},{4,2},{6,4},{7,6},{5,7},{3,5},{1,3},{8,9},{10,8},{12,1... | collective-permute-start | bytes 1376264 | tf_op jit(solution)/shard_map/ppermute | solution.py:204
  83.4 1.6 %collective-permute-start.17 = (bf16[256,512]{1,0:T(8,128)(2,1)S(1)}, bf16[256,512]{1,0:T(8,128)(2,1)S(1)}, u32[]{:S(2)}, u32[]{:S(2)}) collective-permute-start(bf16[256,512]{1,0:T(8,128)(2,1)S(1)} %shard_map.91.own_ref), channel_id=1, source_target_pairs={{0,8},{8,0},{1,9},{9,1},{2,10},{10,2},{3,11},{11,3},{4,12},{12,4},... | collective-permute-start | bytes 786440 | tf_op jit(solution)/shard_map/ppermute | solution.py:251

commit v3 on v2

--- a/solution.py
+++ b/solution.py
@@ -124,47 +124,52 @@
     )(rows, *weights)
 
 
-def attend_kernel(steps, slope_ref, fresh_ref, own_ref, far_ref, place_ref, span_ref, out_ref):
-    rows = fresh_ref.shape[0]
-    cols = fresh_ref.shape[1] // 3
-    tok = own_ref.shape[0]
-    scale = 1.0 / HS**0.5
+def plan_kernel(steps, owner_ref, slope_ref, sums_ref, far_ref, place_ref, span_ref, fresh_ref, bias_ref):
+    rows, cols = fresh_ref.shape
+    mine = pl.ds(pl.multiple_of(owner_ref[0] * rows, 8), rows)
+    fresh_ref[...] = (sums_ref[mine, :] + far_ref[mine, :]).astype(fresh_ref.dtype)
     start = span_ref[:, 0:1]
     length = span_ref[:, 1:2]
     row = lax.broadcasted_iota(jnp.int32, (rows, 1), 0)
-    step_of = row % steps
     rel = place_ref[...] - start
     valid = (rel >= 0) & (rel < length)
-    dist = (length + step_of - rel).astype(jnp.float32)
+    dist = (length + row % steps - rel).astype(jnp.float32)
     col = lax.broadcasted_iota(jnp.int32, (1, rows), 1)
     near_ok = (row // steps == col // steps) & (col <= row)
     near_dist = (row - col).astype(jnp.float32)
+    slots = place_ref.shape[1]
+    for head in range(bias_ref.shape[0]):
+        bias_ref[head, :, :slots] = jnp.where(valid, -(slope_ref[head] * dist), -1e30)
+        bias_ref[head, :, slots:] = jnp.where(near_ok, -(slope_ref[head] * near_dist), -1e30)
+
+
+def attend_kernel(steps, fresh_ref, own_ref, far_ref, bias_ref, out_ref):
+    rows = fresh_ref.shape[0]
+    cols = fresh_ref.shape[1] // 3
+    scale = 1.0 / HS**0.5
     nt = (((1,), (1,)), ((), ()))
-    for head in range(cols // HS):
-        slope = slope_ref[head]
+    heads = range(cols // HS)
+    fresh = fresh_ref[:, cols:]
+    scores, out = [], []
+    for head in heads:
         query = fresh_ref[:, head * HS : (head + 1) * HS]
-        fresh_key = fresh_ref[:, cols + head * HS : cols + (head + 1) * HS]
-        fresh_value = fresh_ref[:, 2 * cols + head * HS : 2 * cols + (head + 1) * HS]
-        scores = []
-        for part, ref in enumerate((own_ref, far_ref)):
-            key = ref[:, head * HS : (head + 1) * HS]
-            ctx = lax.dot_general(query, key, nt, preferred_element_type=jnp.float32) * scale
-            ctx = ctx - slope * dist[:, part * tok : (part + 1) * tok]
-            scores.append(jnp.where(valid[:, part * tok : (part + 1) * tok], ctx, -1e30))
-        near = lax.dot_general(query, fresh_key, nt, preferred_element_type=jnp.float32) * scale
-        scores.append(jnp.where(near_ok, near - slope * near_dist, -1e30))
-        top = functools.reduce(jnp.maximum, [jnp.max(s, axis=1, keepdims=True) for s in scores])
-        exps = [jnp.exp(s - top) for s in scores]
-        total = sum(jnp.sum(e, axis=1, keepdims=True) for e in exps)
-        weights = [(e / total).astype(jnp.bfloat16) for e in exps]
-        values = [ref[:, cols + head * HS : cols + (head + 1) * HS] for ref in (own_ref, far_ref)]
-        values.append(fresh_value)
-        out = sum(
-            jnp.dot(w, v, preferred_element_type=jnp.float32) for w, v in zip(weights, values)
-        )
-        out = out.astype(out_ref.dtype)
+        at, here = 0, []
+        for part in (own_ref, far_ref, fresh):
+            key = part[:, head * HS : (head + 1) * HS]
+            score = lax.dot_general(query, key, nt, preferred_element_type=jnp.float32) * scale
+            here.append(score + bias_ref[head, :, at : at + score.shape[1]])
+            at += score.shape[1]
+        scores.append(here)
+    for head in heads:
+        top = functools.reduce(jnp.maximum, [jnp.max(s, axis=1, keepdims=True) for s in scores[head]])
+        exps = [jnp.exp(s - top) for s in scores[head]]
+        total = 1.0 / sum(jnp.sum(e, axis=1, keepdims=True) for e in exps)
+        weights = [(e * total).astype(jnp.bfloat16) for e in exps]
+        values = [part[:, cols + head * HS : cols + (head + 1) * HS] for part in (own_ref, far_ref, fresh)]
+        out.append(sum(jnp.dot(w, v, preferred_element_type=jnp.float32) for w, v in zip(weights, values)))
+    for head in heads:
         for r in range(rows // steps):
-            out_ref[r, :, head * HS : (head + 1) * HS] = out[r * steps : (r + 1) * steps]
+            out_ref[r, :, head * HS : (head + 1) * HS] = out[head][r * steps : (r + 1) * steps].astype(out_ref.dtype)
 
 
 def on_device(hidden, slot_tokens, lengths, decode_rows, query_weight, key_weight, value_weight):
@@ -186,7 +191,7 @@
     for i, g in enumerate(order):
         place[g] = i
     half = width // 2
-    block = 896 if depth % 896 == 0 else depth
+    block = depth // 2
 
     own = [hidden[:, :half], hidden[:, half:]]
     seen = [((0, 0), (0, 1))] + [
@@ -208,12 +213,9 @@
     for k in range(2):
         send((own[k % 2], own[1 - k % 2]))
     sums = decode(decode_rows, (query_weight, key_weight, value_weight), block)
-    key_far = lax.ppermute(key_weight, "pre", swap)
-    moving[0], key_far, second, sums, slot_tokens, lengths = tie(
-        (moving[0], key_far, value_weight, sums, slot_tokens, lengths)
-    )
+    weights = (key_weight, value_weight) + tuple(lax.ppermute(w, "pre", swap) for w in (key_weight, value_weight))
+    moving[0], sums, slot_tokens, lengths = tie((moving[0], sums, slot_tokens, lengths))
     send(moving[0])
-    weights = (key_weight, value_weight, key_far, lax.ppermute(second, "pre", swap))
 
     mine = lax.dynamic_slice_in_dim(slot_tokens, owner * own_tok, own_tok)
     lane = jnp.arange(2 * own_tok, dtype=jnp.int32)
@@ -227,36 +229,47 @@
     heads_index = (group * heads_dev + jnp.arange(heads_dev)).astype(jnp.float32)
     slope = jnp.exp2(-8.0 * (heads_index + 1.0) / (heads_dev * n))
 
-    moving[1], sums, where, span, slope = tie((moving[1], sums, where, span, slope))
+    moving[1], weights, sums, where, span, slope = tie((moving[1], weights, sums, where, span, slope))
     send(moving[1])
-    keep = lax.dynamic_slice_in_dim(sums, owner * rows_dev, rows_dev, 0)
-    give = lax.dynamic_slice_in_dim(sums, (1 - owner) * rows_dev, rows_dev, 0)
-
-    moving[2], weights, keep, give = tie((moving[2], weights, keep, give))
-    fresh = (keep + lax.ppermute(give, "pre", swap)).astype(jnp.bfloat16)
+    sums_far = lax.ppermute(sums, "pre", swap)
     (now,) = step([], None, None, rows_of, 0, weights, half)
     acc = jnp.zeros((8, 128), jnp.float32)
-    waiting, done = [own] + moving[:2], 0
-    for k in range(2, n - 1):
-        if k > 2:
-            moving[k], acc, now, fresh = tie((moving[k], acc, now, fresh))
-        if k + 2 < n - 1:
+    waiting, done = [own, moving[0]], 0
+    vmem = pl.BlockSpec(memory_space=pltpu.VMEM)
+    smem = pl.BlockSpec(memory_space=pltpu.SMEM)
+    for k in range(1, n - 2):
+        if k == 2:
+            moving[k], acc, now, sums_far = tie((moving[k], acc, now, sums_far))
+        elif k > 2:
+            moving[k], acc, now = tie((moving[k], acc, now))
+        if 1 < k < n - 3:
             send(moving[k])
         waiting.append(moving[k])
-        for _ in range(2 if len(waiting) > 1 else 1):
-            if len(waiting) > 1 or k < n - 2:
-                done += 1
-                acc, now = step(waiting.pop(0), acc, now, rows_of, 2 * done, weights, half)
-    (acc,) = step(waiting[0], acc, now, rows_of, -1, weights, half, jnp.bfloat16)
+        for _ in range(min(len(waiting), 1 if k == 1 else 2)):
+            done += 1
+            acc, now = step(waiting.pop(0), acc, now, rows_of, 2 * done, weights, half)
+        if k == 4:
+            fresh, bias = pl.pallas_call(
+                functools.partial(plan_kernel, steps),
+                out_shape=[
+                    jax.ShapeDtypeStruct((rows_dev, 3 * cols), jnp.bfloat16),
+                    jax.ShapeDtypeStruct((heads_dev, rows_dev, 2 * own_tok + rows_dev), jnp.float32),
+                ],
+                in_specs=[smem] * 2 + [vmem] * 4,
+                out_specs=[vmem] * 2,
+                compiler_params=pltpu.CompilerParams(vmem_limit_bytes=16 * 1024 * 1024),
+                cost_estimate=pl.CostEstimate(flops=0, bytes_accessed=0, transcendentals=0),
+            )(owner[None], slope, sums, sums_far, where, span)
+            acc, fresh, bias = tie((acc, fresh, bias))
+    (acc,) = step(moving[n - 2], acc, now, rows_of, -1, weights, half, jnp.bfloat16)
     far = lax.ppermute(acc, "pre", swap)
-    vmem = pl.BlockSpec(memory_space=pltpu.VMEM)
     return pl.pallas_call(
         functools.partial(attend_kernel, steps),
         out_shape=jax.ShapeDtypeStruct((req_dev, steps, cols), jnp.bfloat16),
-        in_specs=[pl.BlockSpec(memory_space=pltpu.SMEM)] + [vmem] * 5,
+        in_specs=[vmem] * 4,
         out_specs=vmem,
         compiler_params=pltpu.CompilerParams(vmem_limit_bytes=16 * 1024 * 1024),
-    )(slope, fresh, acc, far, where, span)
+    )(fresh, acc, far, bias)
 
 
 def solution(mesh):

time: 87.8 us -> 81.8 us (0.932)
  waiting for transfers between devices: 27.5 us -> 23.1 us
  Pallas kernels: 32.4 us -> 28.6 us
  starting transfers between devices: 15.8 us -> 18.4 us
  other arithmetic: 1.19 us -> 0.23 us
    ppermute x7, waiting for transfers between devices: 19 us -> 11.3 us  [send(): lax.ppermute(pair[0], 'head', up)]
    ppermute x7, starting transfers between devices: 1.83 us -> 7.55 us  [send(): lax.ppermute(pair[1], 'head', down)]
    pallas_call x1, Pallas kernels: 10.9 us -> 7.36 us  [decode(): pl.pallas_call(decode_kernel, out_shape=jax.ShapeDtypeStruct((count * ste...]
    ppermute x7, starting transfers between devices: 13.5 us -> 10.2 us  [send(): lax.ppermute(pair[0], 'head', up)]
    ppermute x7, waiting for transfers between devices: 7.06 us -> 10.3 us  [send(): lax.ppermute(pair[1], 'head', down)]
    unnamed x10 -> x14, local copies, waits for them, and re-layouts: 5.88 us -> 8.16 us
    dynamic_slice x1 -> x0, local copies, waits for them, and re-layouts: 1.72 us -> none  [on_device(): give = lax.dynamic_slice_in_dim(sums, (1 - owner) * rows_dev, rows_dev, 0)]
    pallas_call x0 -> x1, Pallas kernels: none -> 1.13 us  [on_device(): pl.pallas_call(functools.partial(plan_kernel, steps), out_shape=[jax.Shap...]
  transfers between devices with their start and end apart: 18 -> 18, of which waited for: 10 -> 9; matrix products, arithmetic and copies ran while one was open for 6% -> 3% of each run, Pallas kernels for 33% -> 32%
where the time goes in v3:
time: 81.8 us; the launch traced here: 81.1 us
  Pallas kernels  28.6 us (35%)
  waiting for transfers between devices  23.1 us (28%)
  starting transfers between devices  18.4 us (22%)
  local copies, waits for them, and re-layouts  10.6 us (13%)
    pallas_call x9, Pallas kernels, step(): pl.pallas_call(functools.partial(step_kernel, count, first), out_shape=sh...  19 us
    ppermute x7, waiting for transfers between devices, send(): lax.ppermute(pair[0], 'head', up)  11.3 us
    ppermute x7, waiting for transfers between devices, send(): lax.ppermute(pair[1], 'head', down)  10.3 us
    ppermute x7, starting transfers between devices, send(): lax.ppermute(pair[0], 'head', up)  10.2 us
    unnamed x14, local copies, waits for them, and re-layouts  8.16 us
    ppermute x7, starting transfers between devices, send(): lax.ppermute(pair[1], 'head', down)  7.55 us
    pallas_call x1, Pallas kernels, decode(): pl.pallas_call(decode_kernel, out_shape=jax.ShapeDtypeStruct((count * ste...  7.36 us
  transfers between devices with their start and end apart: 18, of which 9 were waited for; matrix products, arithmetic and copies ran while one was open for 3% of the time, Pallas kernels for 32%

profile of v3, /device:TPU:0, one launch (start us, length us, event | category | flops | bytes accessed | tf_op | source)
XLA Modules:
  0.0 81.1 jit_solution(18032117622266087497)
XLA Ops:
  0.0 0.5 collective-permute-start.6
  0.5 0.1 collective-permute-start.7
  0.5 1.2 %fusion.1 = (bf16[256,896]{1,0:T(8,128)(2,1)S(1)}, bf16[256,896]{1,0:T(8,128)(2,1)S(1)}) fusion(bf16[256,1792]{1,0:T(8,128)(2,1)} %param.8), kind=kLoop, calls=%fused_computation.10 | loop fusion | bytes 1835008 | tf_op jit(solution)/shard_map/slice | solution.py:196
  1.7 3.1 %collective-permute-start = (bf16[256,896]{1,0:T(8,128)(2,1)S(1)}, bf16[256,896]{1,0:T(8,128)(2,1)S(1)}, u32[]{:S(2)}, u32[]{:S(2)}) collective-permute-start(bf16[256,896]{1,0:T(8,128)(2,1)S(1)} %get-tuple-element.108.refs_0_), channel_id=1, source_target_pairs={{0,2},{2,4},{4,6},{6,7},{7,5},{5,3},{3,1},{1,0},{8,10},{10,12},{12... | collective-permute-start | bytes 1376264 | tf_op jit(solution)/shard_map/ppermute | solution.py:209
  4.8 0.0 collective-permute-start.1
  4.8 2.0 %collective-permute-start.4 = (bf16[256,896]{1,0:T(8,128)(2,1)S(1)}, bf16[256,896]{1,0:T(8,128)(2,1)S(1)}, u32[]{:S(2)}, u32[]{:S(2)}) collective-permute-start(bf16[256,896]{1,0:T(8,128)(2,1)S(1)} %get-tuple-element.107.refs_1_), channel_id=1, source_target_pairs={{0,2},{2,4},{4,6},{6,7},{7,5},{5,3},{3,1},{1,0},{8,10},{10,12},{12... | collective-permute-start | bytes 1376264 | tf_op jit(solution)/shard_map/ppermute | solution.py:209
  6.9 7.4 %shard_map.82.sums_ref = f32[128,768]{1,0:T(8,128)} custom-call(bf16[32,4,7168]{2,1,0:T(4,128)(2,1)} %rows_ref.1, bf16[7168,256]{1,0:T(8,128)(2,1)} %wq_ref.1, bf16[7168,256]{1,0:T(8,128)(2,1)} %refs_4_.6, bf16[7168,256]{1,0:T(8,128)(2,1)} %refs_5_.6), custom_call_target="tpu_custom_call" | custom-call | tf_op jit(solution)/shard_map/pallas_call | solution.py:114
  14.2 1.9 %collective-permute-done.refs_0_ = bf16[256,896]{1,0:T(8,128)(2,1)S(1)} collective-permute-done((bf16[256,896]{1,0:T(8,128)(2,1)S(1)}, bf16[256,896]{1,0:T(8,128)(2,1)S(1)}, u32[]{:S(2)}, u32[]{:S(2)}) %collective-permute-start) | collective-permute-done | bytes 458784 | tf_op jit(solution)/shard_map/ppermute | solution.py:209
  16.1 2.1 %collective-permute-start.5 = (bf16[256,896]{1,0:T(8,128)(2,1)S(1)}, bf16[256,896]{1,0:T(8,128)(2,1)S(1)}, u32[]{:S(2)}, u32[]{:S(2)}) collective-permute-start(bf16[256,896]{1,0:T(8,128)(2,1)S(1)} %get-tuple-element.108.refs_0_), channel_id=1, source_target_pairs={{0,1},{2,0},{4,2},{6,4},{7,6},{5,7},{3,5},{1,3},{8,9},{10,8},{12,1... | collective-permute-start | bytes 1376264 | tf_op jit(solution)/shard_map/ppermute | solution.py:209
  18.2 0.0 collective-permute-done.1.refs_1_
  18.2 0.0 copy-done.5
  18.2 0.1 copy.23
  18.3 0.1 copy.25
  18.4 0.4 collective-permute-start.2
  18.8 0.1 dynamic_slice.7
  18.8 0.1 select_reduce_fusion
  19.0 6.9 %collective-permute-done.4.refs_0_ = bf16[256,896]{1,0:T(8,128)(2,1)S(1)} collective-permute-done((bf16[256,896]{1,0:T(8,128)(2,1)S(1)}, bf16[256,896]{1,0:T(8,128)(2,1)S(1)}, u32[]{:S(2)}, u32[]{:S(2)}) %collective-permute-start.4) | collective-permute-done | bytes 458784 | tf_op jit(solution)/shard_map/ppermute | solution.py:209
  25.9 2.1 %collective-permute-start.3 = (bf16[256,896]{1,0:T(8,128)(2,1)S(1)}, bf16[256,896]{1,0:T(8,128)(2,1)}, u32[]{:S(2)}, u32[]{:S(2)}) collective-permute-start(bf16[256,896]{1,0:T(8,128)(2,1)S(1)} %collective-permute-done.1.refs_1_), channel_id=1, source_target_pairs={{0,1},{2,0},{4,2},{6,4},{7,6},{5,7},{3,5},{1,3},{8,9},{10,8},{12,1... | collective-permute-start | bytes 1376264 | tf_op jit(solution)/shard_map/ppermute | solution.py:209
  28.0 0.1 broadcast_in_dim.33
  28.1 0.1 reshape.64
  28.2 0.0 collective-permute-done.5.refs_1_
  28.2 0.0 collective-permute-done.6.refs_2_.refs_6_
  28.2 0.0 collective-permute-done.7.refs_3_.refs_7_
  28.2 0.1 collective-permute-start.8
  28.3 0.7 dynamic-slice_bitcast_fusion.rows_ref
  29.0 0.6 collective-permute-start.11
  29.5 1.5 %collective-permute-start.12 = (bf16[256,896]{1,0:T(8,128)(2,1)S(1)}, bf16[256,896]{1,0:T(8,128)(2,1)}, u32[]{:S(2)}, u32[]{:S(2)}) collective-permute-start(bf16[256,896]{1,0:T(8,128)(2,1)S(1)} %collective-permute-done.5.refs_1_), channel_id=1, source_target_pairs={{0,1},{2,0},{4,2},{6,4},{7,6},{5,7},{3,5},{1,3},{8,9},{10,8},{12,1... | collective-permute-start | bytes 1376264 | tf_op jit(solution)/shard_map/ppermute | solution.py:209
  31.0 2.0 %copy-done = bf16[7168,256]{1,0:T(8,128)(2,1)S(1)} copy-done((bf16[7168,256]{1,0:T(8,128)(2,1)S(1)}, bf16[7168,256]{1,0:T(8,128)(2,1)}, u32[]{:S(2)}) %copy-start) | copy-done | bytes 3670040
  33.0 2.0 %copy-done.2 = bf16[7168,256]{1,0:T(8,128)(2,1)S(1)} copy-done((bf16[7168,256]{1,0:T(8,128)(2,1)S(1)}, bf16[7168,256]{1,0:T(8,128)(2,1)}, u32[]{:S(2)}) %copy-start.2) | copy-done | bytes 3670040
  35.1 0.7 shard_map.83.refs_3_
  35.8 1.4 %shard_map.84 = (f32[256,512]{1,0:T(8,128)S(1)}, bf16[2,896,512]{2,1,0:T(8,128)(2,1)S(1)}) custom-call(s32[32]{0:T(128)S(1)} %dynamic-slice_bitcast_fusion.rows_ref, bf16[256,896]{1,0:T(8,128)(2,1)S(1)} %get-tuple-element.108.refs_0_, bf16[256,896]{1,0:T(8,128)(2,1)S(1)} %get-tuple-element.107.refs_1_, f32[8,128]{1,0:T(8,128)S(1)} %broadcast_in_dim.29.refs_2_, ...), custom_call_target="tpu_custom_call" | custom-call | tf_op jit(solution)/shard_map/pallas_call | solution.py:81
  37.3 0.0 collective-permute-done.2.refs_0_
  37.3 2.3 %collective-permute-done.3.refs_1_ = bf16[256,896]{1,0:T(8,128)(2,1)} collective-permute-done((bf16[256,896]{1,0:T(8,128)(2,1)S(1)}, bf16[256,896]{1,0:T(8,128)(2,1)}, u32[]{:S(2)}, u32[]{:S(2)}) %collective-permute-start.3) | collective-permute-done | bytes 458784 | tf_op jit(solution)/shard_map/ppermute | solution.py:209
  39.6 0.0 collective-permute-done.8.far_ref
  39.6 2.0 %collective-permute-start.10 = (bf16[256,896]{1,0:T(8,128)(2,1)}, bf16[256,896]{1,0:T(8,128)(2,1)}, u32[]{:S(2)}, u32[]{:S(2)}) collective-permute-start(bf16[256,896]{1,0:T(8,128)(2,1)} %collective-permute-done.3.refs_1_), channel_id=1, source_target_pairs={{0,1},{2,0},{4,2},{6,4},{7,6},{5,7},{3,5},{1,3},{8,9},{10,8},{12,1... | collective-permute-start | bytes 1376264 | tf_op jit(solution)/shard_map/ppermute | solution.py:209
  41.5 0.1 collective-permute-start.9
  41.6 1.5 %shard_map.85 = (f32[256,512]{1,0:T(8,128)S(1)}, bf16[2,896,512]{2,1,0:T(8,128)(2,1)S(1)}) custom-call(s32[32]{0:T(128)S(1)} %dynamic-slice_bitcast_fusion.rows_ref, bf16[256,896]{1,0:T(8,128)(2,1)S(1)} %collective-permute-done.refs_0_, bf16[256,896]{1,0:T(8,128)(2,1)S(1)} %collective-permute-done.1.refs_1_, f32[256,512]{1,0:T(8,128)S(1)} %get-tuple-element.72.refs_2_, ...), custom_call_target="tpu_custom_call" | custom-call | tf_op jit(solution)/shard_map/pallas_call | solution.py:81
  43.1 2.2 %shard_map.86 = (f32[256,512]{1,0:T(8,128)S(1)}, bf16[2,896,512]{2,1,0:T(8,128)(2,1)S(1)}) custom-call(s32[32]{0:T(128)S(1)} %dynamic-slice_bitcast_fusion.rows_ref, bf16[256,896]{1,0:T(8,128)(2,1)S(1)} %collective-permute-done.4.refs_0_, bf16[256,896]{1,0:T(8,128)(2,1)S(1)} %collective-permute-done.5.refs_1_, f32[256,512]{1,0:T(8,128)S(1)} %get-tuple-element.74.refs_2_, ...), custom_call_target="tpu_custom_call" | custom-call | tf_op jit(solution)/shard_map/pallas_call | solution.py:81
  45.2 0.5 collective-permute-done.11.refs_0_
  45.7 3.7 %collective-permute-done.12.refs_1_ = bf16[256,896]{1,0:T(8,128)(2,1)} collective-permute-done((bf16[256,896]{1,0:T(8,128)(2,1)S(1)}, bf16[256,896]{1,0:T(8,128)(2,1)}, u32[]{:S(2)}, u32[]{:S(2)}) %collective-permute-start.12) | collective-permute-done | bytes 458784 | tf_op jit(solution)/shard_map/ppermute | solution.py:209
  49.4 2.0 %collective-permute-start.15 = (bf16[256,896]{1,0:T(8,128)(2,1)}, bf16[256,896]{1,0:T(8,128)(2,1)}, u32[]{:S(2)}, u32[]{:S(2)}) collective-permute-start(bf16[256,896]{1,0:T(8,128)(2,1)} %collective-permute-done.11.refs_0_), channel_id=1, source_target_pairs={{0,2},{2,4},{4,6},{6,7},{7,5},{5,3},{3,1},{1,0},{8,10},{10,12},{12... | collective-permute-start | bytes 1376264 | tf_op jit(solution)/shard_map/ppermute | solution.py:209
  51.4 0.0 collective-permute-start.16
  51.4 2.7 %shard_map.87 = (f32[256,512]{1,0:T(8,128)S(1)}, bf16[2,896,512]{2,1,0:T(8,128)(2,1)S(1)}) custom-call(s32[32]{0:T(128)S(1)} %dynamic-slice_bitcast_fusion.rows_ref, bf16[256,896]{1,0:T(8,128)(2,1)S(1)} %collective-permute-done.2.refs_0_, bf16[256,896]{1,0:T(8,128)(2,1)} %collective-permute-done.3.refs_1_, f32[256,512]{1,0:T(8,128)S(1)} %get-tuple-element.80.refs_2_, ...), custom_call_target="tpu_custom_call" | custom-call | tf_op jit(solution)/shard_map/pallas_call | solution.py:81
  54.2 0.0 copy-start.4
  54.2 2.9 %shard_map.88 = (f32[256,512]{1,0:T(8,128)S(1)}, bf16[2,896,512]{2,1,0:T(8,128)(2,1)S(1)}) custom-call(s32[32]{0:T(128)S(1)} %dynamic-slice_bitcast_fusion.rows_ref, bf16[256,896]{1,0:T(8,128)(2,1)} %collective-permute-done.11.refs_0_, bf16[256,896]{1,0:T(8,128)(2,1)} %collective-permute-done.12.refs_1_, f32[256,512]{1,0:T(8,128)S(1)} %get-tuple-element.82.refs_2_, ...), custom_call_target="tpu_custom_call" | custom-call | tf_op jit(solution)/shard_map/pallas_call | solution.py:81
  57.1 2.1 %collective-permute-done.10.refs_1_ = bf16[256,896]{1,0:T(8,128)(2,1)} collective-permute-done((bf16[256,896]{1,0:T(8,128)(2,1)}, bf16[256,896]{1,0:T(8,128)(2,1)}, u32[]{:S(2)}, u32[]{:S(2)}) %collective-permute-start.10) | collective-permute-done | bytes 458784 | tf_op jit(solution)/shard_map/ppermute | solution.py:209
  59.2 0.0 collective-permute-done.9.refs_0_
  59.2 2.0 %collective-permute-start.13 = (bf16[256,896]{1,0:T(8,128)(2,1)}, bf16[256,896]{1,0:T(8,128)(2,1)S(1)}, u32[]{:S(2)}, u32[]{:S(2)}) collective-permute-start(bf16[256,896]{1,0:T(8,128)(2,1)} %collective-permute-done.9.refs_0_), channel_id=1, source_target_pairs={{0,2},{2,4},{4,6},{6,7},{7,5},{5,3},{3,1},{1,0},{8,10},{10,12},{12... | collective-permute-start | bytes 1376264 | tf_op jit(solution)/shard_map/ppermute | solution.py:209
  61.3 0.0 collective-permute-start.14
  61.3 0.1 copy.26.span_ref
  61.4 1.1 %shard_map.90 = (bf16[64,768]{1,0:T(8,128)(2,1)S(1)}, f32[2,64,576]{2,1,0:T(8,128)S(1)}) custom-call(s32[1]{0:T(128)} %bitcast.3.owner_ref, f32[2]{0:T(128)S(1)} %multiply_exponential_fusion.slope_ref, f32[128,768]{1,0:T(8,128)S(1)} %copy-done.4, f32[128,768]{1,0:T(8,128)} %collective-permute-done.8.far_ref, s32[1,512]{1,0:T(1,128)S(1)} %bitcast.7, ...), custom_call_target="tpu_custom_call" | custom-call | tf_op jit(solution)/shard_map/pallas_call | solution.py:252
  62.5 0.0 copy-start.1
  62.5 2.0 %copy-done.1 = bf16[7168,256]{1,0:T(8,128)(2,1)S(1)} copy-done((bf16[7168,256]{1,0:T(8,128)(2,1)S(1)}, bf16[7168,256]{1,0:T(8,128)(2,1)}, u32[]{:S(2)}) %copy-start.1) | copy-done | bytes 3670040
  64.5 2.0 %copy-done.3 = bf16[7168,256]{1,0:T(8,128)(2,1)S(1)} copy-done((bf16[7168,256]{1,0:T(8,128)(2,1)S(1)}, bf16[7168,256]{1,0:T(8,128)(2,1)}, u32[]{:S(2)}) %copy-start.3) | copy-done | bytes 3670040
  66.6 2.9 %shard_map.89 = (f32[256,512]{1,0:T(8,128)S(1)}, bf16[2,896,512]{2,1,0:T(8,128)(2,1)S(1)}) custom-call(s32[32]{0:T(128)S(1)} %dynamic-slice_bitcast_fusion.rows_ref, bf16[256,896]{1,0:T(8,128)(2,1)} %collective-permute-done.9.refs_0_, bf16[256,896]{1,0:T(8,128)(2,1)} %collective-permute-done.10.refs_1_, f32[256,512]{1,0:T(8,128)S(1)} %get-tuple-element.88.refs_2_, ...), custom_call_target="tpu_custom_call" | custom-call | tf_op jit(solution)/shard_map/pallas_call | solution.py:81
  69.5 0.0 collective-permute-done.15.refs_0_
  69.5 0.0 collective-permute-done.16.refs_1_
  69.5 2.9 %shard_map.91 = (f32[256,512]{1,0:T(8,128)S(1)}, bf16[2,896,512]{2,1,0:T(8,128)(2,1)S(1)}) custom-call(s32[32]{0:T(128)S(1)} %dynamic-slice_bitcast_fusion.rows_ref, bf16[256,896]{1,0:T(8,128)(2,1)} %collective-permute-done.15.refs_0_, bf16[256,896]{1,0:T(8,128)(2,1)} %collective-permute-done.16.refs_1_, f32[256,512]{1,0:T(8,128)S(1)} %get-tuple-element.102.refs_2_, ...), custom_call_target="tpu_custom_call" | custom-call | tf_op jit(solution)/shard_map/pallas_call | solution.py:81
  72.4 2.1 %collective-permute-done.13.refs_0_ = bf16[256,896]{1,0:T(8,128)(2,1)S(1)} collective-permute-done((bf16[256,896]{1,0:T(8,128)(2,1)}, bf16[256,896]{1,0:T(8,128)(2,1)S(1)}, u32[]{:S(2)}, u32[]{:S(2)}) %collective-permute-start.13) | collective-permute-done | bytes 458784 | tf_op jit(solution)/shard_map/ppermute | solution.py:209
  74.4 2.2 %collective-permute-done.14.refs_1_ = bf16[256,896]{1,0:T(8,128)(2,1)} collective-permute-done((bf16[256,896]{1,0:T(8,128)(2,1)}, bf16[256,896]{1,0:T(8,128)(2,1)}, u32[]{:S(2)}, u32[]{:S(2)}) %collective-permute-start.14) | collective-permute-done | bytes 458784 | tf_op jit(solution)/shard_map/ppermute | solution.py:209
  76.6 1.7 %shard_map.92.own_ref = bf16[256,512]{1,0:T(8,128)(2,1)S(1)} custom-call(s32[32]{0:T(128)S(1)} %dynamic-slice_bitcast_fusion.rows_ref, bf16[256,896]{1,0:T(8,128)(2,1)S(1)} %collective-permute-done.13.refs_0_, bf16[256,896]{1,0:T(8,128)(2,1)} %collective-permute-done.14.refs_1_, f32[256,512]{1,0:T(8,128)S(1)} %get-tuple-element.104.refs_2_, ...), custom_call_target="tpu_custom_call" | custom-call | tf_op jit(solution)/shard_map/pallas_call | solution.py:81
  78.4 0.1 collective-permute-start.17
  78.4 1.5 %collective-permute-done.17.far_ref = bf16[256,512]{1,0:T(8,128)(2,1)S(1)} collective-permute-done((bf16[256,512]{1,0:T(8,128)(2,1)S(1)}, bf16[256,512]{1,0:T(8,128)(2,1)S(1)}, u32[]{:S(2)}, u32[]{:S(2)}) %collective-permute-start.17) | collective-permute-done | bytes 262176 | tf_op jit(solution)/shard_map/ppermute | solution.py:265
  80.0 1.2 %shard_map.93 = bf16[16,4,256]{2,1,0:T(4,128)(2,1)} custom-call(bf16[64,768]{1,0:T(8,128)(2,1)S(1)} %get-tuple-element.97.fresh_ref, bf16[256,512]{1,0:T(8,128)(2,1)S(1)} %shard_map.92.own_ref, bf16[256,512]{1,0:T(8,128)(2,1)S(1)} %collective-permute-done.17.far_ref, f32[2,64,576]{2,1,0:T(8,128)S(1)} %get-tuple-element.106.bias_ref), custom_call_target="tpu_custom_call" | custom-call | tf_op jit(solution)/shard_map/pallas_call | solution.py:266
  (15 shorter events, 0.1 us)
Async XLA Ops:
  0.0 28.2 %collective-permute-start.6 = (bf16[7168,256]{1,0:T(8,128)(2,1)}, bf16[7168,256]{1,0:T(8,128)(2,1)}, u32[]{:S(2)}, u32[]{:S(2)}) collective-permute-start(bf16[7168,256]{1,0:T(8,128)(2,1)} %refs_4_.6), channel_id=1, source_target_pairs={{0,8},{8,0},{1,9},{9,1},{2,10},{10,2},{3,11},{11,3},{4,12},{12,4},... | collective-permute-start | bytes 11010056 | tf_op jit(solution)/shard_map/ppermute | solution.py:216
  0.5 27.7 %collective-permute-start.7 = (bf16[7168,256]{1,0:T(8,128)(2,1)}, bf16[7168,256]{1,0:T(8,128)(2,1)}, u32[]{:S(2)}, u32[]{:S(2)}) collective-permute-start(bf16[7168,256]{1,0:T(8,128)(2,1)} %refs_5_.6), channel_id=1, source_target_pairs={{0,8},{8,0},{1,9},{9,1},{2,10},{10,2},{3,11},{11,3},{4,12},{12,4},... | collective-permute-start | bytes 11010056 | tf_op jit(solution)/shard_map/ppermute | solution.py:216
  1.7 14.3 %collective-permute-start = (bf16[256,896]{1,0:T(8,128)(2,1)S(1)}, bf16[256,896]{1,0:T(8,128)(2,1)S(1)}, u32[]{:S(2)}, u32[]{:S(2)}) collective-permute-start(bf16[256,896]{1,0:T(8,128)(2,1)S(1)} %get-tuple-element.108.refs_0_), channel_id=1, source_target_pairs={{0,2},{2,4},{4,6},{6,7},{7,5},{5,3},{3,1},{1,0},{8,10},{10,12},{12... | collective-permute-start | bytes 1376264 | tf_op jit(solution)/shard_map/ppermute | solution.py:209
  4.8 13.3 %collective-permute-start.1 = (bf16[256,896]{1,0:T(8,128)(2,1)S(1)}, bf16[256,896]{1,0:T(8,128)(2,1)S(1)}, u32[]{:S(2)}, u32[]{:S(2)}) collective-permute-start(bf16[256,896]{1,0:T(8,128)(2,1)S(1)} %get-tuple-element.107.refs_1_), channel_id=1, source_target_pairs={{0,1},{2,0},{4,2},{6,4},{7,6},{5,7},{3,5},{1,3},{8,9},{10,8},{12,1... | collective-permute-start | bytes 1376264 | tf_op jit(solution)/shard_map/ppermute | solution.py:209
  4.8 21.1 %collective-permute-start.4 = (bf16[256,896]{1,0:T(8,128)(2,1)S(1)}, bf16[256,896]{1,0:T(8,128)(2,1)S(1)}, u32[]{:S(2)}, u32[]{:S(2)}) collective-permute-start(bf16[256,896]{1,0:T(8,128)(2,1)S(1)} %get-tuple-element.107.refs_1_), channel_id=1, source_target_pairs={{0,2},{2,4},{4,6},{6,7},{7,5},{5,3},{3,1},{1,0},{8,10},{10,12},{12... | collective-permute-start | bytes 1376264 | tf_op jit(solution)/shard_map/ppermute | solution.py:209
  6.8 11.3 %copy-start.5 = (s32[1,16]{1,0:T(1,128)S(1)}, s32[1,16]{1,0:T(1,128)}, u32[]{:S(2)}) copy-start(s32[1,16]{1,0:T(1,128)} %param.10) | copy-start | bytes 196
  6.9 11.9 %copy-start.6 = (s32[512]{0:T(512)S(1)}, s32[512]{0:T(512)}, u32[]{:S(2)}) copy-start(s32[512]{0:T(512)} %param.9) | copy-start | bytes 6148
  16.1 12.1 %collective-permute-start.5 = (bf16[256,896]{1,0:T(8,128)(2,1)S(1)}, bf16[256,896]{1,0:T(8,128)(2,1)S(1)}, u32[]{:S(2)}, u32[]{:S(2)}) collective-permute-start(bf16[256,896]{1,0:T(8,128)(2,1)S(1)} %get-tuple-element.108.refs_0_), channel_id=1, source_target_pairs={{0,1},{2,0},{4,2},{6,4},{7,6},{5,7},{3,5},{1,3},{8,9},{10,8},{12,1... | collective-permute-start | bytes 1376264 | tf_op jit(solution)/shard_map/ppermute | solution.py:209
  18.4 18.9 %collective-permute-start.2 = (bf16[256,896]{1,0:T(8,128)(2,1)S(1)}, bf16[256,896]{1,0:T(8,128)(2,1)S(1)}, u32[]{:S(2)}, u32[]{:S(2)}) collective-permute-start(bf16[256,896]{1,0:T(8,128)(2,1)S(1)} %collective-permute-done.refs_0_), channel_id=1, source_target_pairs={{0,2},{2,4},{4,6},{6,7},{7,5},{5,3},{3,1},{1,0},{8,10},{10,12},{12... | collective-permute-start | bytes 1376264 | tf_op jit(solution)/shard_map/ppermute | solution.py:209
  25.9 13.7 %collective-permute-start.3 = (bf16[256,896]{1,0:T(8,128)(2,1)S(1)}, bf16[256,896]{1,0:T(8,128)(2,1)}, u32[]{:S(2)}, u32[]{:S(2)}) collective-permute-start(bf16[256,896]{1,0:T(8,128)(2,1)S(1)} %collective-permute-done.1.refs_1_), channel_id=1, source_target_pairs={{0,1},{2,0},{4,2},{6,4},{7,6},{5,7},{3,5},{1,3},{8,9},{10,8},{12,1... | collective-permute-start | bytes 1376264 | tf_op jit(solution)/shard_map/ppermute | solution.py:209
  28.2 11.4 %collective-permute-start.8 = (f32[128,768]{1,0:T(8,128)}, f32[128,768]{1,0:T(8,128)}, u32[]{:S(2)}, u32[]{:S(2)}) collective-permute-start(f32[128,768]{1,0:T(8,128)} %shard_map.82.sums_ref), channel_id=1, source_target_pairs={{0,8},{8,0},{1,9},{9,1},{2,10},{10,2},{3,11},{11,3},{4,12},{12,4},... | collective-permute-start | bytes 1179656 | tf_op jit(solution)/shard_map/ppermute | solution.py:234
  29.0 16.7 %collective-permute-start.11 = (bf16[256,896]{1,0:T(8,128)(2,1)S(1)}, bf16[256,896]{1,0:T(8,128)(2,1)}, u32[]{:S(2)}, u32[]{:S(2)}) collective-permute-start(bf16[256,896]{1,0:T(8,128)(2,1)S(1)} %collective-permute-done.4.refs_0_), channel_id=1, source_target_pairs={{0,2},{2,4},{4,6},{6,7},{7,5},{5,3},{3,1},{1,0},{8,10},{10,12},{12... | collective-permute-start | bytes 1376264 | tf_op jit(solution)/shard_map/ppermute | solution.py:209
  29.5 19.9 %collective-permute-start.12 = (bf16[256,896]{1,0:T(8,128)(2,1)S(1)}, bf16[256,896]{1,0:T(8,128)(2,1)}, u32[]{:S(2)}, u32[]{:S(2)}) collective-permute-start(bf16[256,896]{1,0:T(8,128)(2,1)S(1)} %collective-permute-done.5.refs_1_), channel_id=1, source_target_pairs={{0,1},{2,0},{4,2},{6,4},{7,6},{5,7},{3,5},{1,3},{8,9},{10,8},{12,1... | collective-permute-start | bytes 1376264 | tf_op jit(solution)/shard_map/ppermute | solution.py:209
  31.0 2.0 %copy-start = (bf16[7168,256]{1,0:T(8,128)(2,1)S(1)}, bf16[7168,256]{1,0:T(8,128)(2,1)}, u32[]{:S(2)}) copy-start(bf16[7168,256]{1,0:T(8,128)(2,1)} %refs_4_.6) | copy-start | bytes 11010052
  33.0 2.0 %copy-start.2 = (bf16[7168,256]{1,0:T(8,128)(2,1)S(1)}, bf16[7168,256]{1,0:T(8,128)(2,1)}, u32[]{:S(2)}) copy-start(bf16[7168,256]{1,0:T(8,128)(2,1)} %refs_5_.6) | copy-start | bytes 11010052
  39.6 19.7 %collective-permute-start.10 = (bf16[256,896]{1,0:T(8,128)(2,1)}, bf16[256,896]{1,0:T(8,128)(2,1)}, u32[]{:S(2)}, u32[]{:S(2)}) collective-permute-start(bf16[256,896]{1,0:T(8,128)(2,1)} %collective-permute-done.3.refs_1_), channel_id=1, source_target_pairs={{0,1},{2,0},{4,2},{6,4},{7,6},{5,7},{3,5},{1,3},{8,9},{10,8},{12,1... | collective-permute-start | bytes 1376264 | tf_op jit(solution)/shard_map/ppermute | solution.py:209
  41.5 17.7 %collective-permute-start.9 = (bf16[256,896]{1,0:T(8,128)(2,1)S(1)}, bf16[256,896]{1,0:T(8,128)(2,1)}, u32[]{:S(2)}, u32[]{:S(2)}) collective-permute-start(bf16[256,896]{1,0:T(8,128)(2,1)S(1)} %collective-permute-done.2.refs_0_), channel_id=1, source_target_pairs={{0,2},{2,4},{4,6},{6,7},{7,5},{5,3},{3,1},{1,0},{8,10},{10,12},{12... | collective-permute-start | bytes 1376264 | tf_op jit(solution)/shard_map/ppermute | solution.py:209
  49.4 20.1 %collective-permute-start.15 = (bf16[256,896]{1,0:T(8,128)(2,1)}, bf16[256,896]{1,0:T(8,128)(2,1)}, u32[]{:S(2)}, u32[]{:S(2)}) collective-permute-start(bf16[256,896]{1,0:T(8,128)(2,1)} %collective-permute-done.11.refs_0_), channel_id=1, source_target_pairs={{0,2},{2,4},{4,6},{6,7},{7,5},{5,3},{3,1},{1,0},{8,10},{10,12},{12... | collective-permute-start | bytes 1376264 | tf_op jit(solution)/shard_map/ppermute | solution.py:209
  51.4 18.0 %collective-permute-start.16 = (bf16[256,896]{1,0:T(8,128)(2,1)}, bf16[256,896]{1,0:T(8,128)(2,1)}, u32[]{:S(2)}, u32[]{:S(2)}) collective-permute-start(bf16[256,896]{1,0:T(8,128)(2,1)} %collective-permute-done.12.refs_1_), channel_id=1, source_target_pairs={{0,1},{2,0},{4,2},{6,4},{7,6},{5,7},{3,5},{1,3},{8,9},{10,8},{12,1... | collective-permute-start | bytes 1376264 | tf_op jit(solution)/shard_map/ppermute | solution.py:209
  54.2 7.2 %copy-start.4 = (f32[128,768]{1,0:T(8,128)S(1)}, f32[128,768]{1,0:T(8,128)}, u32[]{:S(2)}) copy-start(f32[128,768]{1,0:T(8,128)} %shard_map.82.sums_ref) | copy-start | bytes 1179652
  59.2 15.2 %collective-permute-start.13 = (bf16[256,896]{1,0:T(8,128)(2,1)}, bf16[256,896]{1,0:T(8,128)(2,1)S(1)}, u32[]{:S(2)}, u32[]{:S(2)}) collective-permute-start(bf16[256,896]{1,0:T(8,128)(2,1)} %collective-permute-done.9.refs_0_), channel_id=1, source_target_pairs={{0,2},{2,4},{4,6},{6,7},{7,5},{5,3},{3,1},{1,0},{8,10},{10,12},{12... | collective-permute-start | bytes 1376264 | tf_op jit(solution)/shard_map/ppermute | solution.py:209
  61.3 15.3 %collective-permute-start.14 = (bf16[256,896]{1,0:T(8,128)(2,1)}, bf16[256,896]{1,0:T(8,128)(2,1)}, u32[]{:S(2)}, u32[]{:S(2)}) collective-permute-start(bf16[256,896]{1,0:T(8,128)(2,1)} %collective-permute-done.10.refs_1_), channel_id=1, source_target_pairs={{0,1},{2,0},{4,2},{6,4},{7,6},{5,7},{3,5},{1,3},{8,9},{10,8},{12,1... | collective-permute-start | bytes 1376264 | tf_op jit(solution)/shard_map/ppermute | solution.py:209
  62.5 2.0 %copy-start.1 = (bf16[7168,256]{1,0:T(8,128)(2,1)S(1)}, bf16[7168,256]{1,0:T(8,128)(2,1)}, u32[]{:S(2)}) copy-start(bf16[7168,256]{1,0:T(8,128)(2,1)} %refs_4_.6) | copy-start | bytes 11010052
  64.5 2.0 %copy-start.3 = (bf16[7168,256]{1,0:T(8,128)(2,1)S(1)}, bf16[7168,256]{1,0:T(8,128)(2,1)}, u32[]{:S(2)}) copy-start(bf16[7168,256]{1,0:T(8,128)(2,1)} %refs_5_.6) | copy-start | bytes 11010052
  78.4 1.6 %collective-permute-start.17 = (bf16[256,512]{1,0:T(8,128)(2,1)S(1)}, bf16[256,512]{1,0:T(8,128)(2,1)S(1)}, u32[]{:S(2)}, u32[]{:S(2)}) collective-permute-start(bf16[256,512]{1,0:T(8,128)(2,1)S(1)} %shard_map.92.own_ref), channel_id=1, source_target_pairs={{0,8},{8,0},{1,9},{9,1},{2,10},{10,2},{3,11},{11,3},{4,12},{12,4},... | collective-permute-start | bytes 786440 | tf_op jit(solution)/shard_map/ppermute | solution.py:265

commit v4 on v3

v4 whole, which is shorter than its diff:
```python
import functools

import jax
import jax.numpy as jnp
import numpy as np
from jax import lax
from jax.experimental import pallas as pl
from jax.experimental.pallas import tpu as pltpu
from jax.sharding import PartitionSpec as P

HS = 128


def ring_order(n):
    if n == 8:
        return [0, 2, 4, 6, 7, 5, 3, 1]
    return list(range(n))


def step_kernel(parts, block, rows_ref, *refs):
    items, refs = refs[: len(parts)], refs[len(parts) :]
    if parts:
        acc_ref, now_ref, refs = refs[0], refs[1], refs[2:]
    if block is not None:
        near, far = refs[:2], refs[2:4]
        next_ref, sems = refs[-2:]
        depth = next_ref.shape[0]
        cols = near[0].shape[1]

        def copies(sources):
            start = pl.multiple_of(rows_ref[2 * block], 64)
            return [
                pltpu.make_async_copy(
                    src.at[pl.ds(start, depth), :], next_ref.at[:, pl.ds(part * cols, cols)], sems.at[part]
                )
                for part, src in enumerate(sources)
            ]

        @pl.when(rows_ref[2 * block + 1] == 0)
        def _():
            for copy in copies(near):
                copy.start()

        @pl.when(rows_ref[2 * block + 1] != 0)
        def _():
            for copy in copies(far):
                copy.start()

    if parts:
        out_ref = refs[0] if block is None else refs[4]
        total = acc_ref[...] if acc_ref.shape == out_ref.shape else 0.0
        for item, at in zip(items, parts):
            rows = now_ref[at : at + item.shape[1], :]
            total = total + jnp.dot(item[...], rows, preferred_element_type=jnp.float32)
        out_ref[...] = total.astype(out_ref.dtype)
    if block is not None:
        for copy in copies(near):
            copy.wait()


def step(items, parts, acc, now, rows, block, weights, depth, dtype=jnp.float32, flops=0):
    cols = 2 * weights[0].shape[1]
    vmem = pl.BlockSpec(memory_space=pltpu.VMEM)
    operands, specs = [rows, *items], [pl.BlockSpec(memory_space=pltpu.SMEM)] + [vmem] * len(items)
    shapes, scratch = [], []
    if items:
        operands += [acc, now]
        specs += [vmem] * 2
        shapes.append(jax.ShapeDtypeStruct((items[0].shape[0], cols), dtype))
    if block is not None:
        operands += weights
        specs += [pl.BlockSpec(memory_space=pl.ANY)] * 4
        shapes.append(jax.ShapeDtypeStruct((depth, cols), jnp.bfloat16))
        scratch.append(pltpu.SemaphoreType.DMA((2,)))
    return pl.pallas_call(
        functools.partial(step_kernel, parts, block),
        out_shape=shapes,
        in_specs=specs,
        out_specs=[vmem] * len(shapes),
        scratch_shapes=scratch,
        compiler_params=pltpu.CompilerParams(vmem_limit_bytes=46 * 1024 * 1024),
        cost_estimate=pl.CostEstimate(flops=flops, bytes_accessed=0, transcendentals=0),
    )(*operands)


def decode_kernel(rows_ref, weight_ref, out_ref, flat):
    count, steps, _ = rows_ref.shape
    for r in range(count):
        flat[r * steps : (r + 1) * steps] = rows_ref[r].astype(jnp.float32)
    rows = flat[...].astype(jnp.bfloat16)
    term = jnp.dot(rows, weight_ref[...], preferred_element_type=jnp.float32)

    @pl.when(pl.program_id(0) == 0)
    def _():
        out_ref[...] = term

    @pl.when(pl.program_id(0) != 0)
    def _():
        out_ref[...] += term


def decode(rows, weight, block):
    count, steps, depth = rows.shape
    cols = weight.shape[1]
    return pl.pallas_call(
        decode_kernel,
        out_shape=jax.ShapeDtypeStruct((count * steps, cols), jnp.float32),
        grid=(depth // block,),
        in_specs=[
            pl.BlockSpec((count, steps, block), lambda i: (0, 0, i)),
            pl.BlockSpec((block, cols), lambda i: (i, 0)),
        ],
        out_specs=pl.BlockSpec((count * steps, cols), lambda i: (0, 0)),
        scratch_shapes=[pltpu.VMEM((count * steps, block), jnp.float32)],
        compiler_params=pltpu.CompilerParams(vmem_limit_bytes=52 * 1024 * 1024),
        cost_estimate=pl.CostEstimate(flops=0, bytes_accessed=0, transcendentals=0),
    )(rows, weight)


def plan_kernel(steps, owner_ref, slope_ref, place_ref, span_ref, *refs):
    sums, (fresh_ref, bias_ref) = refs[:-2], refs[-2:]
    rows = fresh_ref.shape[0]
    cols = sums[0].shape[1]
    mine = pl.ds(pl.multiple_of(owner_ref[0] * rows, 8), rows)
    for part in range(3):
        both = sums[part][mine, :] + sums[part + 3][mine, :]
        fresh_ref[:, part * cols : (part + 1) * cols] = both.astype(fresh_ref.dtype)
    start = span_ref[:, 0:1]
    length = span_ref[:, 1:2]
    row = lax.broadcasted_iota(jnp.int32, (rows, 1), 0)
    rel = place_ref[...] - start
    valid = (rel >= 0) & (rel < length)
    dist = (length + row % steps - rel).astype(jnp.float32)
    col = lax.broadcasted_iota(jnp.int32, (1, rows), 1)
    near_ok = (row // steps == col // steps) & (col <= row)
    near_dist = (row - col).astype(jnp.float32)
    slots = place_ref.shape[1]
    for head in range(bias_ref.shape[0]):
        bias_ref[head, :, :slots] = jnp.where(valid, -(slope_ref[head] * dist), -1e30)
        bias_ref[head, :, slots:] = jnp.where(near_ok, -(slope_ref[head] * near_dist), -1e30)


def attend_kernel(steps, fresh_ref, own_ref, far_ref, bias_ref, out_ref):
    rows = fresh_ref.shape[0]
    cols = fresh_ref.shape[1] // 3
    scale = 1.0 / HS**0.5
    nt = (((1,), (1,)), ((), ()))
    heads = range(cols // HS)
    fresh = fresh_ref[:, cols:]
    scores, out = [], []
    for head in heads:
        query = fresh_ref[:, head * HS : (head + 1) * HS]
        at, here = 0, []
        for part in (own_ref, far_ref, fresh):
            key = part[:, head * HS : (head + 1) * HS]
            score = lax.dot_general(query, key, nt, preferred_element_type=jnp.float32) * scale
            here.append(score + bias_ref[head, :, at : at + score.shape[1]])
            at += score.shape[1]
        scores.append(here)
    for head in heads:
        top = functools.reduce(jnp.maximum, [jnp.max(s, axis=1, keepdims=True) for s in scores[head]])
        exps = [jnp.exp(s - top) for s in scores[head]]
        total = 1.0 / sum(jnp.sum(e, axis=1, keepdims=True) for e in exps)
        weights = [(e * total).astype(jnp.bfloat16) for e in exps]
        values = [part[:, cols + head * HS : cols + (head + 1) * HS] for part in (own_ref, far_ref, fresh)]
        out.append(sum(jnp.dot(w, v, preferred_element_type=jnp.float32) for w, v in zip(weights, values)))
    for head in heads:
        for r in range(rows // steps):
            out_ref[r, :, head * HS : (head + 1) * HS] = out[head][r * steps : (r + 1) * steps].astype(out_ref.dtype)


def on_device(hidden, slot_tokens, lengths, decode_rows, query_weight, key_weight, value_weight):
    group = lax.axis_index("head")
    owner = lax.axis_index("pre")
    n = lax.axis_size("head")
    own_tok, width = hidden.shape
    depth = key_weight.shape[0]
    cols = key_weight.shape[1]
    heads_dev = cols // HS
    req_dev, steps = lengths.shape[1], decode_rows.shape[1]
    rows_dev = req_dev * steps
    swap = [(0, 1), (1, 0)]

    order = ring_order(n)
    around = [(order[i], order[(i + 1) % n]) for i in range(n)]
    around += [(n + order[i], n + order[(i - 1) % n]) for i in range(n)]
    table = np.zeros((2 * n, 2 * n), np.int32)
    for g in range(n):
        for p in range(2):
            for hop in range(n):
                row = order[(order.index(g) + (hop if p else -hop)) % n] * width
                table[2 * g + p, 2 * hop : 2 * hop + 2] = row % depth, row // depth != p
    rows_of = lax.dynamic_slice_in_dim(jnp.asarray(table), 2 * group + owner, 1, 0)[0]

    tie = lax.optimization_barrier
    cut = width // 2
    parts = (0, cut)
    own = [hidden[:, :cut], hidden[:, cut:]]

    def send(item):
        return lax.ppermute(item, ("pre", "head"), around)

    moving = [send(own[0]), send(own[1])]
    weights = (key_weight, value_weight) + tuple(lax.ppermute(w, "pre", swap) for w in (key_weight, value_weight))
    sums = [decode(decode_rows, query_weight, depth // 2)]
    moving[0], sums[0], decode_rows, slot_tokens, lengths = tie(
        (moving[0], sums[0], decode_rows, slot_tokens, lengths)
    )
    moving.append(send(moving[0]))
    mine = lax.dynamic_slice_in_dim(slot_tokens, owner * own_tok, own_tok)
    lane = jnp.arange(2 * own_tok, dtype=jnp.int32)
    token = (lane + owner * own_tok) % (2 * own_tok)
    slot = jnp.arange(1, own_tok + 1, dtype=jnp.int32)
    where = jnp.sum(jnp.where(mine[:, None] == token[None, :], slot[:, None], 0), axis=0, keepdims=True)
    lens = lengths[0]
    starts = jnp.cumsum(lens) - lens
    where = jnp.where(where == 0, -(1 << 20), where - 1)
    span = jnp.repeat(jnp.stack([starts, lens], axis=1), steps, axis=0)
    heads_index = (group * heads_dev + jnp.arange(heads_dev)).astype(jnp.float32)
    slope = jnp.exp2(-8.0 * (heads_index + 1.0) / (heads_dev * n))

    moving[1], where, span, slope, rows_of = tie((moving[1], where, span, slope, rows_of))
    moving.append(send(moving[1]))
    sums.append(decode(decode_rows, key_weight, depth // 2))
    moving[2], weights, sums[1] = tie((moving[2], weights, sums[1]))
    moving.append(send(moving[2]))
    (now,) = step([], (), None, None, rows_of, 0, weights, width)
    acc = jnp.zeros((8, 128), jnp.float32)
    vmem = pl.BlockSpec(memory_space=pltpu.VMEM)
    smem = pl.BlockSpec(memory_space=pltpu.SMEM)
    done = 0
    for k in range(3, 2 * n - 2):
        moving[k], acc, now = tie((moving[k], acc, now))
        if k + 2 < 2 * n - 2:
            moving.append(send(moving[k]))
        if k == 3:
            decode_rows, acc = tie((decode_rows, acc))
            sums.append(decode(decode_rows, value_weight, depth // 2))
            acc, now, sums[2] = tie((acc, now, sums[2]))
            sums_far = [lax.ppermute(part, "pre", swap) for part in sums]
            continue
        if done < n - 1 and 2 * done <= k + 1 and k not in (9,):
            items = moving[2 * done - 2 : 2 * done] if done else own
            done += 1
            acc, now = step(items, parts, acc, now, rows_of, done, weights, width)
        if k == 9:
            fresh, bias = pl.pallas_call(
                functools.partial(plan_kernel, steps),
                out_shape=[
                    jax.ShapeDtypeStruct((rows_dev, 3 * cols), jnp.bfloat16),
                    jax.ShapeDtypeStruct((heads_dev, rows_dev, 2 * own_tok + rows_dev), jnp.float32),
                ],
                in_specs=[smem] * 2 + [vmem] * 8,
                out_specs=[vmem] * 2,
                compiler_params=pltpu.CompilerParams(vmem_limit_bytes=8 * 1024 * 1024),
                cost_estimate=pl.CostEstimate(flops=0, bytes_accessed=0, transcendentals=0),
            )(owner[None], slope, where, span, *sums, *sums_far)
            acc, fresh, bias = tie((acc, fresh, bias))
    (acc,) = step(moving[-2:], parts, acc, now, rows_of, None, weights, width, jnp.bfloat16)
    far = lax.ppermute(acc, "pre", swap)
    return pl.pallas_call(
        functools.partial(attend_kernel, steps),
        out_shape=jax.ShapeDtypeStruct((req_dev, steps, cols), jnp.bfloat16),
        in_specs=[vmem] * 4,
        out_specs=vmem,
        compiler_params=pltpu.CompilerParams(vmem_limit_bytes=16 * 1024 * 1024),
    )(fresh, acc, far, bias)


def solution(mesh):
    in_specs = (
        P(("grp", "pre"), "head"),
        P("grp"),
        P(("grp", "pre"), None),
        P("grp", None, "pre"),
        P("pre", "head"),
        P("pre", "head"),
        P("pre", "head"),
    )
    out_specs = P(("grp", "pre"), None, "head")
    return jax.shard_map(
        on_device, mesh=mesh, in_specs=in_specs, out_specs=out_specs, check_vma=False
    )
```

time: 81.8 us -> 79.8 us (0.976)
  starting transfers between devices: 18.4 us -> 30.2 us
  waiting for transfers between devices: 23.1 us -> 13.6 us
  local copies, waits for them, and re-layouts: 10.6 us -> 2.48 us
  Pallas kernels: 28.6 us -> 32.4 us
    ppermute x15 -> x17, starting transfers between devices: 17.8 us -> 29.6 us  [the longest x14 29.1 us: send(): return lax.ppermute(item, ('pre', 'head'), around)]
    ppermute x15 -> x17, waiting for transfers between devices: 21.6 us -> 12.1 us  [the longest x14 10.9 us: send(): return lax.ppermute(item, ('pre', 'head'), around)]
    unnamed x14 -> x12, local copies, waits for them, and re-layouts: 8.16 us -> 0.02 us
    pallas_call x9, Pallas kernels: 19 us -> 22.4 us  [step(): pl.pallas_call(functools.partial(step_kernel, parts, block), out_shape=sh...]
    pallas_call x1 -> x3, Pallas kernels: 7.36 us -> 8.16 us  [decode(): pl.pallas_call(decode_kernel, out_shape=jax.ShapeDtypeStruct((count * ste...]
  transfers between devices with their start and end apart: 18 -> 20, of which waited for: 9 -> 14; matrix products, arithmetic and copies ran while one was open for 3% -> 3% of each run, Pallas kernels for 32% -> 38%
where the time goes in v4:
time: 79.8 us; the launch traced here: 79.2 us
  Pallas kernels  32.4 us (41%)
  starting transfers between devices  30.2 us (38%)
  waiting for transfers between devices  13.6 us (17%)
  local copies, waits for them, and re-layouts  2.48 us (3%)
    ppermute x14, starting transfers between devices, send(): return lax.ppermute(item, ('pre', 'head'), around)  29.1 us
    pallas_call x9, Pallas kernels, step(): pl.pallas_call(functools.partial(step_kernel, parts, block), out_shape=sh...  22.4 us
    ppermute x14, waiting for transfers between devices, send(): return lax.ppermute(item, ('pre', 'head'), around)  10.9 us
    pallas_call x3, Pallas kernels, decode(): pl.pallas_call(decode_kernel, out_shape=jax.ShapeDtypeStruct((count * ste...  8.16 us
  transfers between devices with their start and end apart: 20, of which 14 were waited for; matrix products, arithmetic and copies ran while one was open for 3% of the time, Pallas kernels for 38%

profile of v4, /device:TPU:0, one launch (start us, length us, event | category | flops | bytes accessed | tf_op | source)
XLA Modules:
  0.0 79.2 jit_solution(3951778136859896107)
XLA Ops:
  0.0 0.5 collective-permute-start.4
  0.5 0.1 collective-permute-start.5
  0.5 1.3 %fusion.1 = (bf16[256,896]{1,0:T(8,128)(2,1)S(1)}, bf16[256,896]{1,0:T(8,128)(2,1)S(1)}) fusion(bf16[256,1792]{1,0:T(8,128)(2,1)} %param.8), kind=kLoop, calls=%fused_computation.10 | loop fusion | bytes 1835008 | tf_op jit(solution)/shard_map/slice | solution.py:198
  1.8 3.1 %collective-permute-start.1 = (bf16[256,896]{1,0:T(8,128)(2,1)S(1)}, bf16[256,896]{1,0:T(8,128)(2,1)S(1)}, u32[]{:S(2)}, u32[]{:S(2)}) collective-permute-start(bf16[256,896]{1,0:T(8,128)(2,1)S(1)} %get-tuple-element.151.refs_0_), channel_id=1, source_target_pairs={{0,2},{2,4},{4,6},{6,7},{7,5},{5,3},{3,1},{1,0},{8,9},{10,8},{12,1... | collective-permute-start | bytes 1376264 | tf_op jit(solution)/shard_map/ppermute | solution.py:201
  4.9 1.6 %collective-permute-start = (bf16[256,896]{1,0:T(8,128)(2,1)S(1)}, bf16[256,896]{1,0:T(8,128)(2,1)}, u32[]{:S(2)}, u32[]{:S(2)}) collective-permute-start(bf16[256,896]{1,0:T(8,128)(2,1)S(1)} %get-tuple-element.152.refs_1_), channel_id=1, source_target_pairs={{0,2},{2,4},{4,6},{6,7},{7,5},{5,3},{3,1},{1,0},{8,9},{10,8},{12,1... | collective-permute-start | bytes 1376264 | tf_op jit(solution)/shard_map/ppermute | solution.py:201
  6.4 0.0 copy-done.1
  6.4 2.7 %shard_map.82.refs_0_ = f32[128,256]{1,0:T(8,128)S(1)} custom-call(bf16[32,4,7168]{2,1,0:T(4,128)(2,1)S(1)} %copy-done.1, bf16[7168,256]{1,0:T(8,128)(2,1)} %weight_ref.3), custom_call_target="tpu_custom_call" | custom-call | tf_op jit(solution)/shard_map/pallas_call | solution.py:105
  9.2 0.7 dynamic-slice_bitcast_fusion.rows_ref
  9.9 1.4 %collective-permute-done.1.refs_0_ = bf16[256,896]{1,0:T(8,128)(2,1)S(1)} collective-permute-done((bf16[256,896]{1,0:T(8,128)(2,1)S(1)}, bf16[256,896]{1,0:T(8,128)(2,1)S(1)}, u32[]{:S(2)}, u32[]{:S(2)}) %collective-permute-start.1) | collective-permute-done | bytes 458784 | tf_op jit(solution)/shard_map/ppermute | solution.py:201
  11.3 0.1 copy.23
  11.4 0.1 copy.25
  11.5 2.1 %collective-permute-start.3 = (bf16[256,896]{1,0:T(8,128)(2,1)S(1)}, bf16[256,896]{1,0:T(8,128)(2,1)}, u32[]{:S(2)}, u32[]{:S(2)}) collective-permute-start(bf16[256,896]{1,0:T(8,128)(2,1)S(1)} %collective-permute-done.1.refs_0_), channel_id=1, source_target_pairs={{0,2},{2,4},{4,6},{6,7},{7,5},{5,3},{3,1},{1,0},{8,9},{10,8},{12,1... | collective-permute-start | bytes 1376264 | tf_op jit(solution)/shard_map/ppermute | solution.py:201
  13.6 0.1 dynamic_slice.6
  13.6 0.1 select_reduce_fusion
  13.8 0.1 broadcast_in_dim.32
  13.9 0.1 reshape.64
  14.0 2.3 %collective-permute-done.refs_1_ = bf16[256,896]{1,0:T(8,128)(2,1)} collective-permute-done((bf16[256,896]{1,0:T(8,128)(2,1)S(1)}, bf16[256,896]{1,0:T(8,128)(2,1)}, u32[]{:S(2)}, u32[]{:S(2)}) %collective-permute-start) | collective-permute-done | bytes 458784 | tf_op jit(solution)/shard_map/ppermute | solution.py:201
  16.3 2.1 %collective-permute-start.2 = (bf16[256,896]{1,0:T(8,128)(2,1)}, bf16[256,896]{1,0:T(8,128)(2,1)S(1)}, u32[]{:S(2)}, u32[]{:S(2)}) collective-permute-start(bf16[256,896]{1,0:T(8,128)(2,1)} %collective-permute-done.refs_1_), channel_id=1, source_target_pairs={{0,2},{2,4},{4,6},{6,7},{7,5},{5,3},{3,1},{1,0},{8,9},{10,8},{12,1... | collective-permute-start | bytes 1376264 | tf_op jit(solution)/shard_map/ppermute | solution.py:201
  18.4 2.7 %shard_map.83.refs_1_ = f32[128,256]{1,0:T(8,128)S(1)} custom-call(bf16[32,4,7168]{2,1,0:T(4,128)(2,1)S(1)} %copy-done.1, bf16[7168,256]{1,0:T(8,128)(2,1)} %refs_4_.6), custom_call_target="tpu_custom_call" | custom-call | tf_op jit(solution)/shard_map/pallas_call | solution.py:105
  21.1 0.1 collective-permute-done.3.refs_0_
  21.2 0.0 collective-permute-done.4.refs_2_.refs_6_
  21.2 0.0 collective-permute-done.5.refs_3_.refs_7_
  21.2 2.1 %collective-permute-start.7 = (bf16[256,896]{1,0:T(8,128)(2,1)}, bf16[256,896]{1,0:T(8,128)(2,1)S(1)}, u32[]{:S(2)}, u32[]{:S(2)}) collective-permute-start(bf16[256,896]{1,0:T(8,128)(2,1)} %collective-permute-done.3.refs_0_), channel_id=1, source_target_pairs={{0,2},{2,4},{4,6},{6,7},{7,5},{5,3},{3,1},{1,0},{8,9},{10,8},{12,1... | collective-permute-start | bytes 1376264 | tf_op jit(solution)/shard_map/ppermute | solution.py:201
  23.3 1.8 %shard_map.84.refs_3_ = bf16[1792,512]{1,0:T(8,128)(2,1)S(1)} custom-call(s32[16]{0:T(128)S(1)} %dynamic-slice_bitcast_fusion.rows_ref, bf16[7168,256]{1,0:T(8,128)(2,1)S(1)} %copy-done, bf16[7168,256]{1,0:T(8,128)(2,1)} %refs_5_.6, bf16[7168,256]{1,0:T(8,128)(2,1)} %collective-permute-done.4.refs_2_.refs_6_, ...), custom_call_target="tpu_custom_call" | custom-call | tf_op jit(solution)/shard_map/pallas_call | solution.py:75
  25.1 0.9 %collective-permute-done.2.refs_1_ = bf16[256,896]{1,0:T(8,128)(2,1)S(1)} collective-permute-done((bf16[256,896]{1,0:T(8,128)(2,1)}, bf16[256,896]{1,0:T(8,128)(2,1)S(1)}, u32[]{:S(2)}, u32[]{:S(2)}) %collective-permute-start.2) | collective-permute-done | bytes 458784 | tf_op jit(solution)/shard_map/ppermute | solution.py:201
  26.0 2.1 %collective-permute-start.6 = (bf16[256,896]{1,0:T(8,128)(2,1)S(1)}, bf16[256,896]{1,0:T(8,128)(2,1)S(1)}, u32[]{:S(2)}, u32[]{:S(2)}) collective-permute-start(bf16[256,896]{1,0:T(8,128)(2,1)S(1)} %collective-permute-done.2.refs_1_), channel_id=1, source_target_pairs={{0,2},{2,4},{4,6},{6,7},{7,5},{5,3},{3,1},{1,0},{8,9},{10,8},{12,1... | collective-permute-start | bytes 1376264 | tf_op jit(solution)/shard_map/ppermute | solution.py:201
  28.1 2.7 %shard_map.85.refs_2_ = f32[128,256]{1,0:T(8,128)S(1)} custom-call(bf16[32,4,7168]{2,1,0:T(4,128)(2,1)S(1)} %copy-done.1, bf16[7168,256]{1,0:T(8,128)(2,1)} %refs_5_.6), custom_call_target="tpu_custom_call" | custom-call | tf_op jit(solution)/shard_map/pallas_call | solution.py:105
  30.8 0.1 collective-permute-done.7.refs_0_
  30.9 2.1 %collective-permute-start.9 = (bf16[256,896]{1,0:T(8,128)(2,1)S(1)}, bf16[256,896]{1,0:T(8,128)(2,1)S(1)}, u32[]{:S(2)}, u32[]{:S(2)}) collective-permute-start(bf16[256,896]{1,0:T(8,128)(2,1)S(1)} %collective-permute-done.7.refs_0_), channel_id=1, source_target_pairs={{0,2},{2,4},{4,6},{6,7},{7,5},{5,3},{3,1},{1,0},{8,9},{10,8},{12,1... | collective-permute-start | bytes 1376264 | tf_op jit(solution)/shard_map/ppermute | solution.py:201
  33.0 2.5 %shard_map.86 = (f32[256,512]{1,0:T(8,128)S(1)}, bf16[1792,512]{1,0:T(8,128)(2,1)S(1)}) custom-call(s32[16]{0:T(128)S(1)} %dynamic-slice_bitcast_fusion.rows_ref, bf16[256,896]{1,0:T(8,128)(2,1)S(1)} %get-tuple-element.151.refs_0_, bf16[256,896]{1,0:T(8,128)(2,1)S(1)} %get-tuple-element.152.refs_1_, f32[8,128]{1,0:T(8,128)S(1)} %broadcast_in_dim.33.refs_2_, ...), custom_call_target="tpu_custom_call" | custom-call | tf_op jit(solution)/shard_map/pallas_call | solution.py:75
  35.5 0.3 collective-permute-done.6.refs_1_
  35.8 2.1 %collective-permute-start.8 = (bf16[256,896]{1,0:T(8,128)(2,1)S(1)}, bf16[256,896]{1,0:T(8,128)(2,1)S(1)}, u32[]{:S(2)}, u32[]{:S(2)}) collective-permute-start(bf16[256,896]{1,0:T(8,128)(2,1)S(1)} %collective-permute-done.6.refs_1_), channel_id=1, source_target_pairs={{0,2},{2,4},{4,6},{6,7},{7,5},{5,3},{3,1},{1,0},{8,9},{10,8},{12,1... | collective-permute-start | bytes 1376264 | tf_op jit(solution)/shard_map/ppermute | solution.py:201
  37.9 2.9 %shard_map.87 = (f32[256,512]{1,0:T(8,128)S(1)}, bf16[1792,512]{1,0:T(8,128)(2,1)S(1)}) custom-call(s32[16]{0:T(128)S(1)} %dynamic-slice_bitcast_fusion.rows_ref, bf16[256,896]{1,0:T(8,128)(2,1)S(1)} %copy-done.3, bf16[256,896]{1,0:T(8,128)(2,1)} %collective-permute-done.refs_1_, f32[256,512]{1,0:T(8,128)S(1)} %get-tuple-element.102.refs_2_, ...), custom_call_target="tpu_custom_call" | custom-call | tf_op jit(solution)/shard_map/pallas_call | solution.py:75
  40.9 0.0 collective-permute-done.9.refs_0_
  40.9 2.0 %collective-permute-start.11 = (bf16[256,896]{1,0:T(8,128)(2,1)S(1)}, bf16[256,896]{1,0:T(8,128)(2,1)}, u32[]{:S(2)}, u32[]{:S(2)}) collective-permute-start(bf16[256,896]{1,0:T(8,128)(2,1)S(1)} %collective-permute-done.9.refs_0_), channel_id=1, source_target_pairs={{0,2},{2,4},{4,6},{6,7},{7,5},{5,3},{3,1},{1,0},{8,9},{10,8},{12,1... | collective-permute-start | bytes 1376264 | tf_op jit(solution)/shard_map/ppermute | solution.py:201
  42.8 2.9 %shard_map.88 = (f32[256,512]{1,0:T(8,128)S(1)}, bf16[1792,512]{1,0:T(8,128)(2,1)S(1)}) custom-call(s32[16]{0:T(128)S(1)} %dynamic-slice_bitcast_fusion.rows_ref, bf16[256,896]{1,0:T(8,128)(2,1)} %collective-permute-done.3.refs_0_, bf16[256,896]{1,0:T(8,128)(2,1)S(1)} %collective-permute-done.2.refs_1_, f32[256,512]{1,0:T(8,128)S(1)} %get-tuple-element.106.refs_2_, ...), custom_call_target="tpu_custom_call" | custom-call | tf_op jit(solution)/shard_map/pallas_call | solution.py:75
  45.8 0.0 collective-permute-done.8.refs_1_
  45.8 2.0 %collective-permute-start.10 = (bf16[256,896]{1,0:T(8,128)(2,1)S(1)}, bf16[256,896]{1,0:T(8,128)(2,1)}, u32[]{:S(2)}, u32[]{:S(2)}) collective-permute-start(bf16[256,896]{1,0:T(8,128)(2,1)S(1)} %collective-permute-done.8.refs_1_), channel_id=1, source_target_pairs={{0,2},{2,4},{4,6},{6,7},{7,5},{5,3},{3,1},{1,0},{8,9},{10,8},{12,1... | collective-permute-start | bytes 1376264 | tf_op jit(solution)/shard_map/ppermute | solution.py:201
  47.7 2.4 %shard_map.89 = (f32[256,512]{1,0:T(8,128)S(1)}, bf16[1792,512]{1,0:T(8,128)(2,1)S(1)}) custom-call(s32[16]{0:T(128)S(1)} %dynamic-slice_bitcast_fusion.rows_ref, bf16[256,896]{1,0:T(8,128)(2,1)S(1)} %collective-permute-done.7.refs_0_, bf16[256,896]{1,0:T(8,128)(2,1)S(1)} %collective-permute-done.6.refs_1_, f32[256,512]{1,0:T(8,128)S(1)} %get-tuple-element.112.refs_2_, ...), custom_call_target="tpu_custom_call" | custom-call | tf_op jit(solution)/shard_map/pallas_call | solution.py:75
  50.2 0.5 collective-permute-done.11.refs_0_
  50.7 2.1 %collective-permute-start.15 = (bf16[256,896]{1,0:T(8,128)(2,1)}, bf16[256,896]{1,0:T(8,128)(2,1)}, u32[]{:S(2)}, u32[]{:S(2)}) collective-permute-start(bf16[256,896]{1,0:T(8,128)(2,1)} %collective-permute-done.11.refs_0_), channel_id=1, source_target_pairs={{0,2},{2,4},{4,6},{6,7},{7,5},{5,3},{3,1},{1,0},{8,9},{10,8},{12,1... | collective-permute-start | bytes 1376264 | tf_op jit(solution)/shard_map/ppermute | solution.py:201
  52.8 2.4 %shard_map.90 = (f32[256,512]{1,0:T(8,128)S(1)}, bf16[1792,512]{1,0:T(8,128)(2,1)S(1)}) custom-call(s32[16]{0:T(128)S(1)} %dynamic-slice_bitcast_fusion.rows_ref, bf16[256,896]{1,0:T(8,128)(2,1)S(1)} %collective-permute-done.9.refs_0_, bf16[256,896]{1,0:T(8,128)(2,1)S(1)} %collective-permute-done.8.refs_1_, f32[256,512]{1,0:T(8,128)S(1)} %get-tuple-element.116.refs_2_, ...), custom_call_target="tpu_custom_call" | custom-call | tf_op jit(solution)/shard_map/pallas_call | solution.py:75
  55.2 0.4 collective-permute-done.10.refs_1_
  55.6 2.1 %collective-permute-start.17 = (bf16[256,896]{1,0:T(8,128)(2,1)}, bf16[256,896]{1,0:T(8,128)(2,1)}, u32[]{:S(2)}, u32[]{:S(2)}) collective-permute-start(bf16[256,896]{1,0:T(8,128)(2,1)} %collective-permute-done.10.refs_1_), channel_id=1, source_target_pairs={{0,2},{2,4},{4,6},{6,7},{7,5},{5,3},{3,1},{1,0},{8,9},{10,8},{12,1... | collective-permute-start | bytes 1376264 | tf_op jit(solution)/shard_map/ppermute | solution.py:201
  57.7 0.0 collective-permute-start.12
  57.7 0.5 collective-permute-start.14
  58.2 0.0 collective-permute-start.13
  58.2 0.1 copy.26.span_ref
  58.3 0.7 collective-permute-done.12.refs_3_
  59.0 0.2 collective-permute-done.14.refs_5_
  59.2 0.3 collective-permute-done.13.refs_4_
  59.5 0.7 shard_map.91
  60.2 0.3 collective-permute-done.15.refs_0_
  60.5 2.1 %collective-permute-start.16 = (bf16[256,896]{1,0:T(8,128)(2,1)}, bf16[256,896]{1,0:T(8,128)(2,1)S(1)}, u32[]{:S(2)}, u32[]{:S(2)}) collective-permute-start(bf16[256,896]{1,0:T(8,128)(2,1)} %collective-permute-done.15.refs_0_), channel_id=1, source_target_pairs={{0,2},{2,4},{4,6},{6,7},{7,5},{5,3},{3,1},{1,0},{8,9},{10,8},{12,1... | collective-permute-start | bytes 1376264 | tf_op jit(solution)/shard_map/ppermute | solution.py:201
  62.6 3.1 %shard_map.92 = (f32[256,512]{1,0:T(8,128)S(1)}, bf16[1792,512]{1,0:T(8,128)(2,1)S(1)}) custom-call(s32[16]{0:T(128)S(1)} %dynamic-slice_bitcast_fusion.rows_ref, bf16[256,896]{1,0:T(8,128)(2,1)} %collective-permute-done.11.refs_0_, bf16[256,896]{1,0:T(8,128)(2,1)} %collective-permute-done.10.refs_1_, f32[256,512]{1,0:T(8,128)S(1)} %get-tuple-element.135.refs_2_, ...), custom_call_target="tpu_custom_call" | custom-call | tf_op jit(solution)/shard_map/pallas_call | solution.py:75
  65.7 0.0 collective-permute-done.17.refs_1_
  65.7 1.8 %collective-permute-start.18 = (bf16[256,896]{1,0:T(8,128)(2,1)}, bf16[256,896]{1,0:T(8,128)(2,1)S(1)}, u32[]{:S(2)}, u32[]{:S(2)}) collective-permute-start(bf16[256,896]{1,0:T(8,128)(2,1)} %collective-permute-done.17.refs_1_), channel_id=1, source_target_pairs={{0,2},{2,4},{4,6},{6,7},{7,5},{5,3},{3,1},{1,0},{8,9},{10,8},{12,1... | collective-permute-start | bytes 1376264 | tf_op jit(solution)/shard_map/ppermute | solution.py:201
  67.5 3.1 %shard_map.93 = (f32[256,512]{1,0:T(8,128)S(1)}, bf16[1792,512]{1,0:T(8,128)(2,1)S(1)}) custom-call(s32[16]{0:T(128)S(1)} %dynamic-slice_bitcast_fusion.rows_ref, bf16[256,896]{1,0:T(8,128)(2,1)} %collective-permute-done.15.refs_0_, bf16[256,896]{1,0:T(8,128)(2,1)} %collective-permute-done.17.refs_1_, f32[256,512]{1,0:T(8,128)S(1)} %get-tuple-element.140.refs_2_, ...), custom_call_target="tpu_custom_call" | custom-call | tf_op jit(solution)/shard_map/pallas_call | solution.py:75
  70.6 0.0 collective-permute-done.16.refs_0_
  70.6 4.6 %collective-permute-done.18.refs_1_ = bf16[256,896]{1,0:T(8,128)(2,1)S(1)} collective-permute-done((bf16[256,896]{1,0:T(8,128)(2,1)}, bf16[256,896]{1,0:T(8,128)(2,1)S(1)}, u32[]{:S(2)}, u32[]{:S(2)}) %collective-permute-start.18) | collective-permute-done | bytes 458784 | tf_op jit(solution)/shard_map/ppermute | solution.py:201
  75.2 1.2 %shard_map.94.own_ref = bf16[256,512]{1,0:T(8,128)(2,1)S(1)} custom-call(s32[16]{0:T(128)S(1)} %dynamic-slice_bitcast_fusion.rows_ref, bf16[256,896]{1,0:T(8,128)(2,1)S(1)} %collective-permute-done.16.refs_0_, bf16[256,896]{1,0:T(8,128)(2,1)S(1)} %collective-permute-done.18.refs_1_, f32[256,512]{1,0:T(8,128)S(1)} %get-tuple-element.148.refs_2_, ...), custom_call_target="tpu_custom_call" | custom-call | tf_op jit(solution)/shard_map/pallas_call | solution.py:75
  76.4 0.1 collective-permute-start.19
  76.5 1.5 %collective-permute-done.19.far_ref = bf16[256,512]{1,0:T(8,128)(2,1)S(1)} collective-permute-done((bf16[256,512]{1,0:T(8,128)(2,1)S(1)}, bf16[256,512]{1,0:T(8,128)(2,1)S(1)}, u32[]{:S(2)}, u32[]{:S(2)}) %collective-permute-start.19) | collective-permute-done | bytes 262176 | tf_op jit(solution)/shard_map/ppermute | solution.py:260
  78.0 1.2 %shard_map.95 = bf16[16,4,256]{2,1,0:T(4,128)(2,1)} custom-call(bf16[64,768]{1,0:T(8,128)(2,1)S(1)} %get-tuple-element.129.fresh_ref, bf16[256,512]{1,0:T(8,128)(2,1)S(1)} %shard_map.94.own_ref, bf16[256,512]{1,0:T(8,128)(2,1)S(1)} %collective-permute-done.19.far_ref, f32[2,64,576]{2,1,0:T(8,128)S(1)} %get-tuple-element.150.bias_ref), custom_call_target="tpu_custom_call" | custom-call | tf_op jit(solution)/shard_map/pallas_call | solution.py:261
  (19 shorter events, 0.1 us)
Async XLA Ops:
  0.0 6.4 %copy-start.1 = (bf16[32,4,7168]{2,1,0:T(4,128)(2,1)S(1)}, bf16[32,4,7168]{2,1,0:T(4,128)(2,1)}, u32[]{:S(2)}) copy-start(bf16[32,4,7168]{2,1,0:T(4,128)(2,1)} %rows_ref.3) | copy-start | bytes 5505028
  0.0 21.2 %collective-permute-start.4 = (bf16[7168,256]{1,0:T(8,128)(2,1)}, bf16[7168,256]{1,0:T(8,128)(2,1)}, u32[]{:S(2)}, u32[]{:S(2)}) collective-permute-start(bf16[7168,256]{1,0:T(8,128)(2,1)} %refs_4_.6), channel_id=1, source_target_pairs={{0,8},{8,0},{1,9},{9,1},{2,10},{10,2},{3,11},{11,3},{4,12},{12,4},... | collective-permute-start | bytes 11010056 | tf_op jit(solution)/shard_map/ppermute | solution.py:204
  0.5 20.8 %collective-permute-start.5 = (bf16[7168,256]{1,0:T(8,128)(2,1)}, bf16[7168,256]{1,0:T(8,128)(2,1)}, u32[]{:S(2)}, u32[]{:S(2)}) collective-permute-start(bf16[7168,256]{1,0:T(8,128)(2,1)} %refs_5_.6), channel_id=1, source_target_pairs={{0,8},{8,0},{1,9},{9,1},{2,10},{10,2},{3,11},{11,3},{4,12},{12,4},... | collective-permute-start | bytes 11010056 | tf_op jit(solution)/shard_map/ppermute | solution.py:204
  1.8 9.5 %collective-permute-start.1 = (bf16[256,896]{1,0:T(8,128)(2,1)S(1)}, bf16[256,896]{1,0:T(8,128)(2,1)S(1)}, u32[]{:S(2)}, u32[]{:S(2)}) collective-permute-start(bf16[256,896]{1,0:T(8,128)(2,1)S(1)} %get-tuple-element.151.refs_0_), channel_id=1, source_target_pairs={{0,2},{2,4},{4,6},{6,7},{7,5},{5,3},{3,1},{1,0},{8,9},{10,8},{12,1... | collective-permute-start | bytes 1376264 | tf_op jit(solution)/shard_map/ppermute | solution.py:201
  4.9 11.4 %collective-permute-start = (bf16[256,896]{1,0:T(8,128)(2,1)S(1)}, bf16[256,896]{1,0:T(8,128)(2,1)}, u32[]{:S(2)}, u32[]{:S(2)}) collective-permute-start(bf16[256,896]{1,0:T(8,128)(2,1)S(1)} %get-tuple-element.152.refs_1_), channel_id=1, source_target_pairs={{0,2},{2,4},{4,6},{6,7},{7,5},{5,3},{3,1},{1,0},{8,9},{10,8},{12,1... | collective-permute-start | bytes 1376264 | tf_op jit(solution)/shard_map/ppermute | solution.py:201
  6.4 4.8 %copy-start.4 = (s32[1,16]{1,0:T(1,128)S(1)}, s32[1,16]{1,0:T(1,128)}, u32[]{:S(2)}) copy-start(s32[1,16]{1,0:T(1,128)} %param.10) | copy-start | bytes 196
  6.4 7.1 %copy-start.5 = (s32[512]{0:T(512)S(1)}, s32[512]{0:T(512)}, u32[]{:S(2)}) copy-start(s32[512]{0:T(512)} %param.9) | copy-start | bytes 6148
  11.3 9.8 %copy-start.2 = (bf16[256,896]{1,0:T(8,128)(2,1)}, bf16[256,896]{1,0:T(8,128)(2,1)S(1)}, u32[]{:S(2)}) copy-start(bf16[256,896]{1,0:T(8,128)(2,1)S(1)} %collective-permute-done.1.refs_0_) | copy-start | bytes 1376260
  11.5 9.7 %collective-permute-start.3 = (bf16[256,896]{1,0:T(8,128)(2,1)S(1)}, bf16[256,896]{1,0:T(8,128)(2,1)}, u32[]{:S(2)}, u32[]{:S(2)}) collective-permute-start(bf16[256,896]{1,0:T(8,128)(2,1)S(1)} %collective-permute-done.1.refs_0_), channel_id=1, source_target_pairs={{0,2},{2,4},{4,6},{6,7},{7,5},{5,3},{3,1},{1,0},{8,9},{10,8},{12,1... | collective-permute-start | bytes 1376264 | tf_op jit(solution)/shard_map/ppermute | solution.py:201
  16.3 7.0 %copy-start = (bf16[7168,256]{1,0:T(8,128)(2,1)S(1)}, bf16[7168,256]{1,0:T(8,128)(2,1)}, u32[]{:S(2)}) copy-start(bf16[7168,256]{1,0:T(8,128)(2,1)} %refs_4_.6) | copy-start | bytes 11010052
  16.3 9.7 %collective-permute-start.2 = (bf16[256,896]{1,0:T(8,128)(2,1)}, bf16[256,896]{1,0:T(8,128)(2,1)S(1)}, u32[]{:S(2)}, u32[]{:S(2)}) collective-permute-start(bf16[256,896]{1,0:T(8,128)(2,1)} %collective-permute-done.refs_1_), channel_id=1, source_target_pairs={{0,2},{2,4},{4,6},{6,7},{7,5},{5,3},{3,1},{1,0},{8,9},{10,8},{12,1... | collective-permute-start | bytes 1376264 | tf_op jit(solution)/shard_map/ppermute | solution.py:201
  21.2 9.7 %collective-permute-start.7 = (bf16[256,896]{1,0:T(8,128)(2,1)}, bf16[256,896]{1,0:T(8,128)(2,1)S(1)}, u32[]{:S(2)}, u32[]{:S(2)}) collective-permute-start(bf16[256,896]{1,0:T(8,128)(2,1)} %collective-permute-done.3.refs_0_), channel_id=1, source_target_pairs={{0,2},{2,4},{4,6},{6,7},{7,5},{5,3},{3,1},{1,0},{8,9},{10,8},{12,1... | collective-permute-start | bytes 1376264 | tf_op jit(solution)/shard_map/ppermute | solution.py:201
  26.0 9.8 %collective-permute-start.6 = (bf16[256,896]{1,0:T(8,128)(2,1)S(1)}, bf16[256,896]{1,0:T(8,128)(2,1)S(1)}, u32[]{:S(2)}, u32[]{:S(2)}) collective-permute-start(bf16[256,896]{1,0:T(8,128)(2,1)S(1)} %collective-permute-done.2.refs_1_), channel_id=1, source_target_pairs={{0,2},{2,4},{4,6},{6,7},{7,5},{5,3},{3,1},{1,0},{8,9},{10,8},{12,1... | collective-permute-start | bytes 1376264 | tf_op jit(solution)/shard_map/ppermute | solution.py:201
  30.9 9.9 %collective-permute-start.9 = (bf16[256,896]{1,0:T(8,128)(2,1)S(1)}, bf16[256,896]{1,0:T(8,128)(2,1)S(1)}, u32[]{:S(2)}, u32[]{:S(2)}) collective-permute-start(bf16[256,896]{1,0:T(8,128)(2,1)S(1)} %collective-permute-done.7.refs_0_), channel_id=1, source_target_pairs={{0,2},{2,4},{4,6},{6,7},{7,5},{5,3},{3,1},{1,0},{8,9},{10,8},{12,1... | collective-permute-start | bytes 1376264 | tf_op jit(solution)/shard_map/ppermute | solution.py:201
  33.0 4.9 %copy-start.3 = (bf16[256,896]{1,0:T(8,128)(2,1)S(1)}, bf16[256,896]{1,0:T(8,128)(2,1)}, u32[]{:S(2)}) copy-start(bf16[256,896]{1,0:T(8,128)(2,1)} %copy-done.2) | copy-start | bytes 1376260
  35.8 9.9 %collective-permute-start.8 = (bf16[256,896]{1,0:T(8,128)(2,1)S(1)}, bf16[256,896]{1,0:T(8,128)(2,1)S(1)}, u32[]{:S(2)}, u32[]{:S(2)}) collective-permute-start(bf16[256,896]{1,0:T(8,128)(2,1)S(1)} %collective-permute-done.6.refs_1_), channel_id=1, source_target_pairs={{0,2},{2,4},{4,6},{6,7},{7,5},{5,3},{3,1},{1,0},{8,9},{10,8},{12,1... | collective-permute-start | bytes 1376264 | tf_op jit(solution)/shard_map/ppermute | solution.py:201
  40.9 9.8 %collective-permute-start.11 = (bf16[256,896]{1,0:T(8,128)(2,1)S(1)}, bf16[256,896]{1,0:T(8,128)(2,1)}, u32[]{:S(2)}, u32[]{:S(2)}) collective-permute-start(bf16[256,896]{1,0:T(8,128)(2,1)S(1)} %collective-permute-done.9.refs_0_), channel_id=1, source_target_pairs={{0,2},{2,4},{4,6},{6,7},{7,5},{5,3},{3,1},{1,0},{8,9},{10,8},{12,1... | collective-permute-start | bytes 1376264 | tf_op jit(solution)/shard_map/ppermute | solution.py:201
  45.8 9.8 %collective-permute-start.10 = (bf16[256,896]{1,0:T(8,128)(2,1)S(1)}, bf16[256,896]{1,0:T(8,128)(2,1)}, u32[]{:S(2)}, u32[]{:S(2)}) collective-permute-start(bf16[256,896]{1,0:T(8,128)(2,1)S(1)} %collective-permute-done.8.refs_1_), channel_id=1, source_target_pairs={{0,2},{2,4},{4,6},{6,7},{7,5},{5,3},{3,1},{1,0},{8,9},{10,8},{12,1... | collective-permute-start | bytes 1376264 | tf_op jit(solution)/shard_map/ppermute | solution.py:201
  50.7 9.8 %collective-permute-start.15 = (bf16[256,896]{1,0:T(8,128)(2,1)}, bf16[256,896]{1,0:T(8,128)(2,1)}, u32[]{:S(2)}, u32[]{:S(2)}) collective-permute-start(bf16[256,896]{1,0:T(8,128)(2,1)} %collective-permute-done.11.refs_0_), channel_id=1, source_target_pairs={{0,2},{2,4},{4,6},{6,7},{7,5},{5,3},{3,1},{1,0},{8,9},{10,8},{12,1... | collective-permute-start | bytes 1376264 | tf_op jit(solution)/shard_map/ppermute | solution.py:201
  55.6 10.1 %collective-permute-start.17 = (bf16[256,896]{1,0:T(8,128)(2,1)}, bf16[256,896]{1,0:T(8,128)(2,1)}, u32[]{:S(2)}, u32[]{:S(2)}) collective-permute-start(bf16[256,896]{1,0:T(8,128)(2,1)} %collective-permute-done.10.refs_1_), channel_id=1, source_target_pairs={{0,2},{2,4},{4,6},{6,7},{7,5},{5,3},{3,1},{1,0},{8,9},{10,8},{12,1... | collective-permute-start | bytes 1376264 | tf_op jit(solution)/shard_map/ppermute | solution.py:201
  57.7 1.3 %collective-permute-start.12 = (f32[128,256]{1,0:T(8,128)S(1)}, f32[128,256]{1,0:T(8,128)S(1)}, u32[]{:S(2)}, u32[]{:S(2)}) collective-permute-start(f32[128,256]{1,0:T(8,128)S(1)} %shard_map.82.refs_0_), channel_id=1, source_target_pairs={{0,8},{8,0},{1,9},{9,1},{2,10},{10,2},{3,11},{11,3},{4,12},{12,4},... | collective-permute-start | bytes 393224 | tf_op jit(solution)/shard_map/ppermute | solution.py:240
  57.7 1.5 %collective-permute-start.14 = (f32[128,256]{1,0:T(8,128)S(1)}, f32[128,256]{1,0:T(8,128)S(1)}, u32[]{:S(2)}, u32[]{:S(2)}) collective-permute-start(f32[128,256]{1,0:T(8,128)S(1)} %shard_map.85.refs_2_), channel_id=1, source_target_pairs={{0,8},{8,0},{1,9},{9,1},{2,10},{10,2},{3,11},{11,3},{4,12},{12,4},... | collective-permute-start | bytes 393224 | tf_op jit(solution)/shard_map/ppermute | solution.py:240
  58.2 1.3 %collective-permute-start.13 = (f32[128,256]{1,0:T(8,128)S(1)}, f32[128,256]{1,0:T(8,128)S(1)}, u32[]{:S(2)}, u32[]{:S(2)}) collective-permute-start(f32[128,256]{1,0:T(8,128)S(1)} %shard_map.83.refs_1_), channel_id=1, source_target_pairs={{0,8},{8,0},{1,9},{9,1},{2,10},{10,2},{3,11},{11,3},{4,12},{12,4},... | collective-permute-start | bytes 393224 | tf_op jit(solution)/shard_map/ppermute | solution.py:240
  60.5 10.1 %collective-permute-start.16 = (bf16[256,896]{1,0:T(8,128)(2,1)}, bf16[256,896]{1,0:T(8,128)(2,1)S(1)}, u32[]{:S(2)}, u32[]{:S(2)}) collective-permute-start(bf16[256,896]{1,0:T(8,128)(2,1)} %collective-permute-done.15.refs_0_), channel_id=1, source_target_pairs={{0,2},{2,4},{4,6},{6,7},{7,5},{5,3},{3,1},{1,0},{8,9},{10,8},{12,1... | collective-permute-start | bytes 1376264 | tf_op jit(solution)/shard_map/ppermute | solution.py:201
  65.7 9.5 %collective-permute-start.18 = (bf16[256,896]{1,0:T(8,128)(2,1)}, bf16[256,896]{1,0:T(8,128)(2,1)S(1)}, u32[]{:S(2)}, u32[]{:S(2)}) collective-permute-start(bf16[256,896]{1,0:T(8,128)(2,1)} %collective-permute-done.17.refs_1_), channel_id=1, source_target_pairs={{0,2},{2,4},{4,6},{6,7},{7,5},{5,3},{3,1},{1,0},{8,9},{10,8},{12,1... | collective-permute-start | bytes 1376264 | tf_op jit(solution)/shard_map/ppermute | solution.py:201
  76.4 1.6 %collective-permute-start.19 = (bf16[256,512]{1,0:T(8,128)(2,1)S(1)}, bf16[256,512]{1,0:T(8,128)(2,1)S(1)}, u32[]{:S(2)}, u32[]{:S(2)}) collective-permute-start(bf16[256,512]{1,0:T(8,128)(2,1)S(1)} %shard_map.94.own_ref), channel_id=1, source_target_pairs={{0,8},{8,0},{1,9},{9,1},{2,10},{10,2},{3,11},{11,3},{4,12},{12,4},... | collective-permute-start | bytes 786440 | tf_op jit(solution)/shard_map/ppermute | solution.py:260

commit v5 on v4

--- a/solution.py
+++ b/solution.py
@@ -140,33 +140,47 @@
         bias_ref[head, :, slots:] = jnp.where(near_ok, -(slope_ref[head] * near_dist), -1e30)
 
 
-def attend_kernel(steps, fresh_ref, own_ref, far_ref, bias_ref, out_ref):
+def last_kernel(parts, at, *refs):
+    items, (acc_ref, now_ref, out_ref) = refs[: len(parts)], refs[len(parts) :]
+    cols = slice(at, at + out_ref.shape[1])
+    total = acc_ref[:, cols]
+    for item, start in zip(items, parts):
+        rows = now_ref[start : start + item.shape[1], cols]
+        total = total + jnp.dot(item[...], rows, preferred_element_type=jnp.float32)
+    out_ref[...] = total.astype(out_ref.dtype)
+
+
+def weight_kernel(fresh_ref, own_ref, far_ref, bias_ref, out_ref):
+    cols = own_ref.shape[1]
+    nt = (((1,), (1,)), ((), ()))
+    for head in range(cols // HS):
+        at = slice(head * HS, (head + 1) * HS)
+        key = fresh_ref[:, cols + head * HS : cols + (head + 1) * HS]
+        scores, start = [], 0
+        for part in (own_ref[:, at], far_ref[:, at], key):
+            score = lax.dot_general(fresh_ref[:, at], part, nt, preferred_element_type=jnp.float32)
+            stop = start + score.shape[1]
+            scores.append(score * (1.0 / HS**0.5) + bias_ref[head, :, start:stop])
+            start = stop
+        top = functools.reduce(jnp.maximum, [jnp.max(s, axis=1, keepdims=True) for s in scores])
+        exps = [jnp.exp(s - top) for s in scores]
+        total = 1.0 / sum(jnp.sum(e, axis=1, keepdims=True) for e in exps)
+        start = 0
+        for e in exps:
+            out_ref[head, :, start : start + e.shape[1]] = (e * total).astype(out_ref.dtype)
+            start += e.shape[1]
+
+
+def value_kernel(steps, weight_ref, fresh_ref, own_ref, far_ref, out_ref):
     rows = fresh_ref.shape[0]
-    cols = fresh_ref.shape[1] // 3
-    scale = 1.0 / HS**0.5
-    nt = (((1,), (1,)), ((), ()))
-    heads = range(cols // HS)
-    fresh = fresh_ref[:, cols:]
-    scores, out = [], []
-    for head in heads:
-        query = fresh_ref[:, head * HS : (head + 1) * HS]
-        at, here = 0, []
-        for part in (own_ref, far_ref, fresh):
-            key = part[:, head * HS : (head + 1) * HS]
-            score = lax.dot_general(query, key, nt, preferred_element_type=jnp.float32) * scale
-            here.append(score + bias_ref[head, :, at : at + score.shape[1]])
-            at += score.shape[1]
-        scores.append(here)
-    for head in heads:
-        top = functools.reduce(jnp.maximum, [jnp.max(s, axis=1, keepdims=True) for s in scores[head]])
-        exps = [jnp.exp(s - top) for s in scores[head]]
-        total = 1.0 / sum(jnp.sum(e, axis=1, keepdims=True) for e in exps)
-        weights = [(e * total).astype(jnp.bfloat16) for e in exps]
-        values = [part[:, cols + head * HS : cols + (head + 1) * HS] for part in (own_ref, far_ref, fresh)]
-        out.append(sum(jnp.dot(w, v, preferred_element_type=jnp.float32) for w, v in zip(weights, values)))
-    for head in heads:
-        for r in range(rows // steps):
-            out_ref[r, :, head * HS : (head + 1) * HS] = out[head][r * steps : (r + 1) * steps].astype(out_ref.dtype)
+    tok, cols = own_ref.shape
+    for head in range(cols // HS):
+        at = slice(head * HS, (head + 1) * HS)
+        fresh = fresh_ref[:, 2 * cols + head * HS : 2 * cols + (head + 1) * HS]
+        out = jnp.dot(weight_ref[head, :, :tok], own_ref[:, at], preferred_element_type=jnp.float32)
+        out += jnp.dot(weight_ref[head, :, tok : 2 * tok], far_ref[:, at], preferred_element_type=jnp.float32)
+        out += jnp.dot(weight_ref[head, :, 2 * tok :], fresh, preferred_element_type=jnp.float32)
+        out_ref[:, :, at] = out.reshape(rows // steps, steps, HS).astype(out_ref.dtype)
 
 
 def on_device(hidden, slot_tokens, lengths, decode_rows, query_weight, key_weight, value_weight):
@@ -256,15 +270,35 @@
                 cost_estimate=pl.CostEstimate(flops=0, bytes_accessed=0, transcendentals=0),
             )(owner[None], slope, where, span, *sums, *sums_far)
             acc, fresh, bias = tie((acc, fresh, bias))
-    (acc,) = step(moving[-2:], parts, acc, now, rows_of, None, weights, width, jnp.bfloat16)
-    far = lax.ppermute(acc, "pre", swap)
+    limit = pltpu.CompilerParams(vmem_limit_bytes=16 * 1024 * 1024)
+    cost = pl.CostEstimate(flops=0, bytes_accessed=0, transcendentals=0)
+    near = [
+        pl.pallas_call(
+            functools.partial(last_kernel, parts, at),
+            out_shape=jax.ShapeDtypeStruct((own_tok, cols), jnp.bfloat16),
+            in_specs=[vmem] * 4,
+            out_specs=vmem,
+            compiler_params=limit,
+            cost_estimate=cost,
+        )(*moving[-2:], acc, now)
+        for at in (0, cols)
+    ]
+    far = [lax.ppermute(part, "pre", swap) for part in near]
+    soft = pl.pallas_call(
+        weight_kernel,
+        out_shape=jax.ShapeDtypeStruct((heads_dev, rows_dev, 2 * own_tok + rows_dev), jnp.bfloat16),
+        in_specs=[vmem] * 4,
+        out_specs=vmem,
+        compiler_params=limit,
+        cost_estimate=cost,
+    )(fresh, near[0], far[0], bias)
     return pl.pallas_call(
-        functools.partial(attend_kernel, steps),
+        functools.partial(value_kernel, steps),
         out_shape=jax.ShapeDtypeStruct((req_dev, steps, cols), jnp.bfloat16),
         in_specs=[vmem] * 4,
         out_specs=vmem,
-        compiler_params=pltpu.CompilerParams(vmem_limit_bytes=16 * 1024 * 1024),
-    )(fresh, acc, far, bias)
+        compiler_params=limit,
+    )(soft, fresh, near[1], far[1])
 
 
 def solution(mesh):

time: 79.8 us -> 79 us (0.990)
  waiting for transfers between devices: 13.6 us -> 12.7 us
    pallas_call x9 -> x8, Pallas kernels: 22.4 us -> 21.2 us  [step(): pl.pallas_call(functools.partial(step_kernel, parts, block), out_shape=sh...]
    ppermute x1 -> x2, waiting for transfers between devices: 1.52 us -> 0.57 us  [on_device(): far = [lax.ppermute(part, 'pre', swap) for part in near]]
    pallas_call x1 -> x4, Pallas kernels: 1.17 us -> 2.08 us  [the longest x2 0.85 us: on_device(): pl.pallas_call(functools.partial(last_kernel, parts, at), out_shape=jax.S...]
  transfers between devices with their start and end apart: 20 -> 21, of which waited for: 14 -> 15; matrix products, arithmetic and copies ran while one was open for 3% -> 3% of each run, Pallas kernels for 38% -> 39%
where the time goes in v5:
time: 79 us; the launch traced here: 78.5 us
  Pallas kernels  32.1 us (41%)
  starting transfers between devices  30.8 us (39%)
  waiting for transfers between devices  12.7 us (16%)
  local copies, waits for them, and re-layouts  2.48 us (3%)
    ppermute x14, starting transfers between devices, send(): return lax.ppermute(item, ('pre', 'head'), around)  29.1 us
    pallas_call x8, Pallas kernels, step(): pl.pallas_call(functools.partial(step_kernel, parts, block), out_shape=sh...  21.2 us
    ppermute x14, waiting for transfers between devices, send(): return lax.ppermute(item, ('pre', 'head'), around)  10.9 us
    pallas_call x3, Pallas kernels, decode(): pl.pallas_call(decode_kernel, out_shape=jax.ShapeDtypeStruct((count * ste...  8.16 us
  transfers between devices with their start and end apart: 21, of which 15 were waited for; matrix products, arithmetic and copies ran while one was open for 3% of the time, Pallas kernels for 39%

profile of v5, /device:TPU:0, one launch (start us, length us, event | category | flops | bytes accessed | tf_op | source)
XLA Modules:
  0.0 78.5 jit_solution(2487277839613857567)
XLA Ops:
  0.0 0.5 collective-permute-start.4
  0.5 0.1 collective-permute-start.5
  0.5 1.3 %fusion.1 = (bf16[256,896]{1,0:T(8,128)(2,1)S(1)}, bf16[256,896]{1,0:T(8,128)(2,1)S(1)}) fusion(bf16[256,1792]{1,0:T(8,128)(2,1)} %param.8), kind=kLoop, calls=%fused_computation.10 | loop fusion | bytes 1835008 | tf_op jit(solution)/shard_map/slice | solution.py:212
  1.8 3.1 %collective-permute-start.1 = (bf16[256,896]{1,0:T(8,128)(2,1)S(1)}, bf16[256,896]{1,0:T(8,128)(2,1)S(1)}, u32[]{:S(2)}, u32[]{:S(2)}) collective-permute-start(bf16[256,896]{1,0:T(8,128)(2,1)S(1)} %get-tuple-element.151.refs_0_), channel_id=1, source_target_pairs={{0,2},{2,4},{4,6},{6,7},{7,5},{5,3},{3,1},{1,0},{8,9},{10,8},{12,1... | collective-permute-start | bytes 1376264 | tf_op jit(solution)/shard_map/ppermute | solution.py:215
  4.9 1.6 %collective-permute-start = (bf16[256,896]{1,0:T(8,128)(2,1)S(1)}, bf16[256,896]{1,0:T(8,128)(2,1)}, u32[]{:S(2)}, u32[]{:S(2)}) collective-permute-start(bf16[256,896]{1,0:T(8,128)(2,1)S(1)} %get-tuple-element.152.refs_1_), channel_id=1, source_target_pairs={{0,2},{2,4},{4,6},{6,7},{7,5},{5,3},{3,1},{1,0},{8,9},{10,8},{12,1... | collective-permute-start | bytes 1376264 | tf_op jit(solution)/shard_map/ppermute | solution.py:215
  6.4 2.7 %shard_map.82.refs_0_ = f32[128,256]{1,0:T(8,128)S(1)} custom-call(bf16[32,4,7168]{2,1,0:T(4,128)(2,1)S(1)} %copy-done.1, bf16[7168,256]{1,0:T(8,128)(2,1)} %weight_ref.3), custom_call_target="tpu_custom_call" | custom-call | tf_op jit(solution)/shard_map/pallas_call | solution.py:105
  9.2 0.7 dynamic-slice_bitcast_fusion.rows_ref
  9.9 1.4 %collective-permute-done.1.refs_0_ = bf16[256,896]{1,0:T(8,128)(2,1)S(1)} collective-permute-done((bf16[256,896]{1,0:T(8,128)(2,1)S(1)}, bf16[256,896]{1,0:T(8,128)(2,1)S(1)}, u32[]{:S(2)}, u32[]{:S(2)}) %collective-permute-start.1) | collective-permute-done | bytes 458784 | tf_op jit(solution)/shard_map/ppermute | solution.py:215
  11.3 0.1 copy.23
  11.4 0.1 copy.25
  11.5 2.1 %collective-permute-start.3 = (bf16[256,896]{1,0:T(8,128)(2,1)S(1)}, bf16[256,896]{1,0:T(8,128)(2,1)}, u32[]{:S(2)}, u32[]{:S(2)}) collective-permute-start(bf16[256,896]{1,0:T(8,128)(2,1)S(1)} %collective-permute-done.1.refs_0_), channel_id=1, source_target_pairs={{0,2},{2,4},{4,6},{6,7},{7,5},{5,3},{3,1},{1,0},{8,9},{10,8},{12,1... | collective-permute-start | bytes 1376264 | tf_op jit(solution)/shard_map/ppermute | solution.py:215
  13.6 0.1 dynamic_slice.6
  13.6 0.1 select_reduce_fusion
  13.8 0.1 broadcast_in_dim.32
  13.9 0.1 reshape.64
  14.0 2.3 %collective-permute-done.refs_1_ = bf16[256,896]{1,0:T(8,128)(2,1)} collective-permute-done((bf16[256,896]{1,0:T(8,128)(2,1)S(1)}, bf16[256,896]{1,0:T(8,128)(2,1)}, u32[]{:S(2)}, u32[]{:S(2)}) %collective-permute-start) | collective-permute-done | bytes 458784 | tf_op jit(solution)/shard_map/ppermute | solution.py:215
  16.3 2.1 %collective-permute-start.2 = (bf16[256,896]{1,0:T(8,128)(2,1)}, bf16[256,896]{1,0:T(8,128)(2,1)S(1)}, u32[]{:S(2)}, u32[]{:S(2)}) collective-permute-start(bf16[256,896]{1,0:T(8,128)(2,1)} %collective-permute-done.refs_1_), channel_id=1, source_target_pairs={{0,2},{2,4},{4,6},{6,7},{7,5},{5,3},{3,1},{1,0},{8,9},{10,8},{12,1... | collective-permute-start | bytes 1376264 | tf_op jit(solution)/shard_map/ppermute | solution.py:215
  18.4 2.7 %shard_map.83.refs_1_ = f32[128,256]{1,0:T(8,128)S(1)} custom-call(bf16[32,4,7168]{2,1,0:T(4,128)(2,1)S(1)} %copy-done.1, bf16[7168,256]{1,0:T(8,128)(2,1)} %refs_4_.6), custom_call_target="tpu_custom_call" | custom-call | tf_op jit(solution)/shard_map/pallas_call | solution.py:105
  21.1 0.1 collective-permute-done.3.refs_0_
  21.2 0.0 collective-permute-done.4.refs_2_.refs_6_
  21.2 0.0 collective-permute-done.5.refs_3_.refs_7_
  21.2 2.1 %collective-permute-start.7 = (bf16[256,896]{1,0:T(8,128)(2,1)}, bf16[256,896]{1,0:T(8,128)(2,1)S(1)}, u32[]{:S(2)}, u32[]{:S(2)}) collective-permute-start(bf16[256,896]{1,0:T(8,128)(2,1)} %collective-permute-done.3.refs_0_), channel_id=1, source_target_pairs={{0,2},{2,4},{4,6},{6,7},{7,5},{5,3},{3,1},{1,0},{8,9},{10,8},{12,1... | collective-permute-start | bytes 1376264 | tf_op jit(solution)/shard_map/ppermute | solution.py:215
  23.3 1.8 %shard_map.84.refs_3_ = bf16[1792,512]{1,0:T(8,128)(2,1)S(1)} custom-call(s32[16]{0:T(128)S(1)} %dynamic-slice_bitcast_fusion.rows_ref, bf16[7168,256]{1,0:T(8,128)(2,1)S(1)} %copy-done, bf16[7168,256]{1,0:T(8,128)(2,1)} %refs_5_.6, bf16[7168,256]{1,0:T(8,128)(2,1)} %collective-permute-done.4.refs_2_.refs_6_, ...), custom_call_target="tpu_custom_call" | custom-call | tf_op jit(solution)/shard_map/pallas_call | solution.py:75
  25.1 0.9 %collective-permute-done.2.refs_1_ = bf16[256,896]{1,0:T(8,128)(2,1)S(1)} collective-permute-done((bf16[256,896]{1,0:T(8,128)(2,1)}, bf16[256,896]{1,0:T(8,128)(2,1)S(1)}, u32[]{:S(2)}, u32[]{:S(2)}) %collective-permute-start.2) | collective-permute-done | bytes 458784 | tf_op jit(solution)/shard_map/ppermute | solution.py:215
  26.0 2.1 %collective-permute-start.6 = (bf16[256,896]{1,0:T(8,128)(2,1)S(1)}, bf16[256,896]{1,0:T(8,128)(2,1)S(1)}, u32[]{:S(2)}, u32[]{:S(2)}) collective-permute-start(bf16[256,896]{1,0:T(8,128)(2,1)S(1)} %collective-permute-done.2.refs_1_), channel_id=1, source_target_pairs={{0,2},{2,4},{4,6},{6,7},{7,5},{5,3},{3,1},{1,0},{8,9},{10,8},{12,1... | collective-permute-start | bytes 1376264 | tf_op jit(solution)/shard_map/ppermute | solution.py:215
  28.1 2.7 %shard_map.85.refs_2_ = f32[128,256]{1,0:T(8,128)S(1)} custom-call(bf16[32,4,7168]{2,1,0:T(4,128)(2,1)S(1)} %copy-done.1, bf16[7168,256]{1,0:T(8,128)(2,1)} %refs_5_.6), custom_call_target="tpu_custom_call" | custom-call | tf_op jit(solution)/shard_map/pallas_call | solution.py:105
  30.8 0.1 collective-permute-done.7.refs_0_
  30.9 2.1 %collective-permute-start.9 = (bf16[256,896]{1,0:T(8,128)(2,1)S(1)}, bf16[256,896]{1,0:T(8,128)(2,1)S(1)}, u32[]{:S(2)}, u32[]{:S(2)}) collective-permute-start(bf16[256,896]{1,0:T(8,128)(2,1)S(1)} %collective-permute-done.7.refs_0_), channel_id=1, source_target_pairs={{0,2},{2,4},{4,6},{6,7},{7,5},{5,3},{3,1},{1,0},{8,9},{10,8},{12,1... | collective-permute-start | bytes 1376264 | tf_op jit(solution)/shard_map/ppermute | solution.py:215
  33.0 2.5 %shard_map.86 = (f32[256,512]{1,0:T(8,128)S(1)}, bf16[1792,512]{1,0:T(8,128)(2,1)S(1)}) custom-call(s32[16]{0:T(128)S(1)} %dynamic-slice_bitcast_fusion.rows_ref, bf16[256,896]{1,0:T(8,128)(2,1)S(1)} %get-tuple-element.151.refs_0_, bf16[256,896]{1,0:T(8,128)(2,1)S(1)} %get-tuple-element.152.refs_1_, f32[8,128]{1,0:T(8,128)S(1)} %broadcast_in_dim.33.refs_2_, ...), custom_call_target="tpu_custom_call" | custom-call | tf_op jit(solution)/shard_map/pallas_call | solution.py:75
  35.5 0.3 collective-permute-done.6.refs_1_
  35.8 2.1 %collective-permute-start.8 = (bf16[256,896]{1,0:T(8,128)(2,1)S(1)}, bf16[256,896]{1,0:T(8,128)(2,1)S(1)}, u32[]{:S(2)}, u32[]{:S(2)}) collective-permute-start(bf16[256,896]{1,0:T(8,128)(2,1)S(1)} %collective-permute-done.6.refs_1_), channel_id=1, source_target_pairs={{0,2},{2,4},{4,6},{6,7},{7,5},{5,3},{3,1},{1,0},{8,9},{10,8},{12,1... | collective-permute-start | bytes 1376264 | tf_op jit(solution)/shard_map/ppermute | solution.py:215
  37.9 2.9 %shard_map.87 = (f32[256,512]{1,0:T(8,128)S(1)}, bf16[1792,512]{1,0:T(8,128)(2,1)S(1)}) custom-call(s32[16]{0:T(128)S(1)} %dynamic-slice_bitcast_fusion.rows_ref, bf16[256,896]{1,0:T(8,128)(2,1)S(1)} %copy-done.3, bf16[256,896]{1,0:T(8,128)(2,1)} %collective-permute-done.refs_1_, f32[256,512]{1,0:T(8,128)S(1)} %get-tuple-element.102.refs_2_, ...), custom_call_target="tpu_custom_call" | custom-call | tf_op jit(solution)/shard_map/pallas_call | solution.py:75
  40.9 0.0 collective-permute-done.9.refs_0_
  40.9 2.0 %collective-permute-start.11 = (bf16[256,896]{1,0:T(8,128)(2,1)S(1)}, bf16[256,896]{1,0:T(8,128)(2,1)}, u32[]{:S(2)}, u32[]{:S(2)}) collective-permute-start(bf16[256,896]{1,0:T(8,128)(2,1)S(1)} %collective-permute-done.9.refs_0_), channel_id=1, source_target_pairs={{0,2},{2,4},{4,6},{6,7},{7,5},{5,3},{3,1},{1,0},{8,9},{10,8},{12,1... | collective-permute-start | bytes 1376264 | tf_op jit(solution)/shard_map/ppermute | solution.py:215
  42.8 2.9 %shard_map.88 = (f32[256,512]{1,0:T(8,128)S(1)}, bf16[1792,512]{1,0:T(8,128)(2,1)S(1)}) custom-call(s32[16]{0:T(128)S(1)} %dynamic-slice_bitcast_fusion.rows_ref, bf16[256,896]{1,0:T(8,128)(2,1)} %collective-permute-done.3.refs_0_, bf16[256,896]{1,0:T(8,128)(2,1)S(1)} %collective-permute-done.2.refs_1_, f32[256,512]{1,0:T(8,128)S(1)} %get-tuple-element.106.refs_2_, ...), custom_call_target="tpu_custom_call" | custom-call | tf_op jit(solution)/shard_map/pallas_call | solution.py:75
  45.8 0.0 collective-permute-done.8.refs_1_
  45.8 2.0 %collective-permute-start.10 = (bf16[256,896]{1,0:T(8,128)(2,1)S(1)}, bf16[256,896]{1,0:T(8,128)(2,1)}, u32[]{:S(2)}, u32[]{:S(2)}) collective-permute-start(bf16[256,896]{1,0:T(8,128)(2,1)S(1)} %collective-permute-done.8.refs_1_), channel_id=1, source_target_pairs={{0,2},{2,4},{4,6},{6,7},{7,5},{5,3},{3,1},{1,0},{8,9},{10,8},{12,1... | collective-permute-start | bytes 1376264 | tf_op jit(solution)/shard_map/ppermute | solution.py:215
  47.7 2.4 %shard_map.89 = (f32[256,512]{1,0:T(8,128)S(1)}, bf16[1792,512]{1,0:T(8,128)(2,1)S(1)}) custom-call(s32[16]{0:T(128)S(1)} %dynamic-slice_bitcast_fusion.rows_ref, bf16[256,896]{1,0:T(8,128)(2,1)S(1)} %collective-permute-done.7.refs_0_, bf16[256,896]{1,0:T(8,128)(2,1)S(1)} %collective-permute-done.6.refs_1_, f32[256,512]{1,0:T(8,128)S(1)} %get-tuple-element.112.refs_2_, ...), custom_call_target="tpu_custom_call" | custom-call | tf_op jit(solution)/shard_map/pallas_call | solution.py:75
  50.2 0.5 collective-permute-done.11.refs_0_
  50.7 2.1 %collective-permute-start.15 = (bf16[256,896]{1,0:T(8,128)(2,1)}, bf16[256,896]{1,0:T(8,128)(2,1)}, u32[]{:S(2)}, u32[]{:S(2)}) collective-permute-start(bf16[256,896]{1,0:T(8,128)(2,1)} %collective-permute-done.11.refs_0_), channel_id=1, source_target_pairs={{0,2},{2,4},{4,6},{6,7},{7,5},{5,3},{3,1},{1,0},{8,9},{10,8},{12,1... | collective-permute-start | bytes 1376264 | tf_op jit(solution)/shard_map/ppermute | solution.py:215
  52.8 2.4 %shard_map.90 = (f32[256,512]{1,0:T(8,128)S(1)}, bf16[1792,512]{1,0:T(8,128)(2,1)S(1)}) custom-call(s32[16]{0:T(128)S(1)} %dynamic-slice_bitcast_fusion.rows_ref, bf16[256,896]{1,0:T(8,128)(2,1)S(1)} %collective-permute-done.9.refs_0_, bf16[256,896]{1,0:T(8,128)(2,1)S(1)} %collective-permute-done.8.refs_1_, f32[256,512]{1,0:T(8,128)S(1)} %get-tuple-element.116.refs_2_, ...), custom_call_target="tpu_custom_call" | custom-call | tf_op jit(solution)/shard_map/pallas_call | solution.py:75
  55.2 0.4 collective-permute-done.10.refs_1_
  55.6 2.1 %collective-permute-start.17 = (bf16[256,896]{1,0:T(8,128)(2,1)}, bf16[256,896]{1,0:T(8,128)(2,1)}, u32[]{:S(2)}, u32[]{:S(2)}) collective-permute-start(bf16[256,896]{1,0:T(8,128)(2,1)} %collective-permute-done.10.refs_1_), channel_id=1, source_target_pairs={{0,2},{2,4},{4,6},{6,7},{7,5},{5,3},{3,1},{1,0},{8,9},{10,8},{12,1... | collective-permute-start | bytes 1376264 | tf_op jit(solution)/shard_map/ppermute | solution.py:215
  57.7 0.5 collective-permute-start.14
  58.2 0.0 collective-permute-start.13
  58.2 0.1 copy.26.span_ref
  58.3 0.7 collective-permute-done.12.refs_3_
  59.0 0.2 collective-permute-done.14.refs_5_
  59.2 0.3 collective-permute-done.13.refs_4_
  59.5 0.7 shard_map.91
  60.2 0.3 collective-permute-done.15.refs_0_
  60.5 2.1 %collective-permute-start.16 = (bf16[256,896]{1,0:T(8,128)(2,1)}, bf16[256,896]{1,0:T(8,128)(2,1)S(1)}, u32[]{:S(2)}, u32[]{:S(2)}) collective-permute-start(bf16[256,896]{1,0:T(8,128)(2,1)} %collective-permute-done.15.refs_0_), channel_id=1, source_target_pairs={{0,2},{2,4},{4,6},{6,7},{7,5},{5,3},{3,1},{1,0},{8,9},{10,8},{12,1... | collective-permute-start | bytes 1376264 | tf_op jit(solution)/shard_map/ppermute | solution.py:215
  62.6 3.1 %shard_map.92 = (f32[256,512]{1,0:T(8,128)S(1)}, bf16[1792,512]{1,0:T(8,128)(2,1)S(1)}) custom-call(s32[16]{0:T(128)S(1)} %dynamic-slice_bitcast_fusion.rows_ref, bf16[256,896]{1,0:T(8,128)(2,1)} %collective-permute-done.11.refs_0_, bf16[256,896]{1,0:T(8,128)(2,1)} %collective-permute-done.10.refs_1_, f32[256,512]{1,0:T(8,128)S(1)} %get-tuple-element.135.refs_2_, ...), custom_call_target="tpu_custom_call" | custom-call | tf_op jit(solution)/shard_map/pallas_call | solution.py:75
  65.7 1.8 %collective-permute-start.18 = (bf16[256,896]{1,0:T(8,128)(2,1)}, bf16[256,896]{1,0:T(8,128)(2,1)S(1)}, u32[]{:S(2)}, u32[]{:S(2)}) collective-permute-start(bf16[256,896]{1,0:T(8,128)(2,1)} %collective-permute-done.17.refs_1_), channel_id=1, source_target_pairs={{0,2},{2,4},{4,6},{6,7},{7,5},{5,3},{3,1},{1,0},{8,9},{10,8},{12,1... | collective-permute-start | bytes 1376264 | tf_op jit(solution)/shard_map/ppermute | solution.py:215
  67.5 3.1 %shard_map.93 = (f32[256,512]{1,0:T(8,128)S(1)}, bf16[1792,512]{1,0:T(8,128)(2,1)S(1)}) custom-call(s32[16]{0:T(128)S(1)} %dynamic-slice_bitcast_fusion.rows_ref, bf16[256,896]{1,0:T(8,128)(2,1)} %collective-permute-done.15.refs_0_, bf16[256,896]{1,0:T(8,128)(2,1)} %collective-permute-done.17.refs_1_, f32[256,512]{1,0:T(8,128)S(1)} %get-tuple-element.140.refs_2_, ...), custom_call_target="tpu_custom_call" | custom-call | tf_op jit(solution)/shard_map/pallas_call | solution.py:75
  70.6 4.6 %collective-permute-done.18.refs_1_ = bf16[256,896]{1,0:T(8,128)(2,1)S(1)} collective-permute-done((bf16[256,896]{1,0:T(8,128)(2,1)}, bf16[256,896]{1,0:T(8,128)(2,1)S(1)}, u32[]{:S(2)}, u32[]{:S(2)}) %collective-permute-start.18) | collective-permute-done | bytes 458784 | tf_op jit(solution)/shard_map/ppermute | solution.py:215
  75.2 0.4 shard_map.94.own_ref
  75.6 0.1 collective-permute-start.19
  75.7 0.4 shard_map.96.own_ref
  76.1 0.6 collective-permute-start.20
  76.7 0.3 collective-permute-done.19.far_ref
  77.0 0.4 shard_map.95.weight_ref
  77.4 0.2 collective-permute-done.20.far_ref
  77.7 0.8 %shard_map.97 = bf16[16,4,256]{2,1,0:T(4,128)(2,1)} custom-call(bf16[2,64,576]{2,1,0:T(8,128)(2,1)S(1)} %shard_map.95.weight_ref, bf16[64,768]{1,0:T(8,128)(2,1)S(1)} %get-tuple-element.129.fresh_ref, bf16[256,256]{1,0:T(8,128)(2,1)S(1)} %shard_map.96.own_ref, bf16[256,256]{1,0:T(8,128)(2,1)S(1)} %collective-permute-done.20.far_ref), custom_call_target="tpu_custom_call" | custom-call | tf_op jit(solution)/shard_map/pallas_call | solution.py:295
  (23 shorter events, 0.1 us)
Async XLA Ops:
  0.0 6.4 %copy-start.1 = (bf16[32,4,7168]{2,1,0:T(4,128)(2,1)S(1)}, bf16[32,4,7168]{2,1,0:T(4,128)(2,1)}, u32[]{:S(2)}) copy-start(bf16[32,4,7168]{2,1,0:T(4,128)(2,1)} %rows_ref.3) | copy-start | bytes 5505028
  0.0 21.2 %collective-permute-start.4 = (bf16[7168,256]{1,0:T(8,128)(2,1)}, bf16[7168,256]{1,0:T(8,128)(2,1)}, u32[]{:S(2)}, u32[]{:S(2)}) collective-permute-start(bf16[7168,256]{1,0:T(8,128)(2,1)} %refs_4_.6), channel_id=1, source_target_pairs={{0,8},{8,0},{1,9},{9,1},{2,10},{10,2},{3,11},{11,3},{4,12},{12,4},... | collective-permute-start | bytes 11010056 | tf_op jit(solution)/shard_map/ppermute | solution.py:218
  0.5 20.8 %collective-permute-start.5 = (bf16[7168,256]{1,0:T(8,128)(2,1)}, bf16[7168,256]{1,0:T(8,128)(2,1)}, u32[]{:S(2)}, u32[]{:S(2)}) collective-permute-start(bf16[7168,256]{1,0:T(8,128)(2,1)} %refs_5_.6), channel_id=1, source_target_pairs={{0,8},{8,0},{1,9},{9,1},{2,10},{10,2},{3,11},{11,3},{4,12},{12,4},... | collective-permute-start | bytes 11010056 | tf_op jit(solution)/shard_map/ppermute | solution.py:218
  1.8 9.5 %collective-permute-start.1 = (bf16[256,896]{1,0:T(8,128)(2,1)S(1)}, bf16[256,896]{1,0:T(8,128)(2,1)S(1)}, u32[]{:S(2)}, u32[]{:S(2)}) collective-permute-start(bf16[256,896]{1,0:T(8,128)(2,1)S(1)} %get-tuple-element.151.refs_0_), channel_id=1, source_target_pairs={{0,2},{2,4},{4,6},{6,7},{7,5},{5,3},{3,1},{1,0},{8,9},{10,8},{12,1... | collective-permute-start | bytes 1376264 | tf_op jit(solution)/shard_map/ppermute | solution.py:215
  4.9 11.4 %collective-permute-start = (bf16[256,896]{1,0:T(8,128)(2,1)S(1)}, bf16[256,896]{1,0:T(8,128)(2,1)}, u32[]{:S(2)}, u32[]{:S(2)}) collective-permute-start(bf16[256,896]{1,0:T(8,128)(2,1)S(1)} %get-tuple-element.152.refs_1_), channel_id=1, source_target_pairs={{0,2},{2,4},{4,6},{6,7},{7,5},{5,3},{3,1},{1,0},{8,9},{10,8},{12,1... | collective-permute-start | bytes 1376264 | tf_op jit(solution)/shard_map/ppermute | solution.py:215
  6.4 4.8 %copy-start.4 = (s32[1,16]{1,0:T(1,128)S(1)}, s32[1,16]{1,0:T(1,128)}, u32[]{:S(2)}) copy-start(s32[1,16]{1,0:T(1,128)} %param.10) | copy-start | bytes 196
  6.4 7.1 %copy-start.5 = (s32[512]{0:T(512)S(1)}, s32[512]{0:T(512)}, u32[]{:S(2)}) copy-start(s32[512]{0:T(512)} %param.9) | copy-start | bytes 6148
  11.3 9.8 %copy-start.2 = (bf16[256,896]{1,0:T(8,128)(2,1)}, bf16[256,896]{1,0:T(8,128)(2,1)S(1)}, u32[]{:S(2)}) copy-start(bf16[256,896]{1,0:T(8,128)(2,1)S(1)} %collective-permute-done.1.refs_0_) | copy-start | bytes 1376260
  11.5 9.7 %collective-permute-start.3 = (bf16[256,896]{1,0:T(8,128)(2,1)S(1)}, bf16[256,896]{1,0:T(8,128)(2,1)}, u32[]{:S(2)}, u32[]{:S(2)}) collective-permute-start(bf16[256,896]{1,0:T(8,128)(2,1)S(1)} %collective-permute-done.1.refs_0_), channel_id=1, source_target_pairs={{0,2},{2,4},{4,6},{6,7},{7,5},{5,3},{3,1},{1,0},{8,9},{10,8},{12,1... | collective-permute-start | bytes 1376264 | tf_op jit(solution)/shard_map/ppermute | solution.py:215
  16.3 7.0 %copy-start = (bf16[7168,256]{1,0:T(8,128)(2,1)S(1)}, bf16[7168,256]{1,0:T(8,128)(2,1)}, u32[]{:S(2)}) copy-start(bf16[7168,256]{1,0:T(8,128)(2,1)} %refs_4_.6) | copy-start | bytes 11010052
  16.3 9.7 %collective-permute-start.2 = (bf16[256,896]{1,0:T(8,128)(2,1)}, bf16[256,896]{1,0:T(8,128)(2,1)S(1)}, u32[]{:S(2)}, u32[]{:S(2)}) collective-permute-start(bf16[256,896]{1,0:T(8,128)(2,1)} %collective-permute-done.refs_1_), channel_id=1, source_target_pairs={{0,2},{2,4},{4,6},{6,7},{7,5},{5,3},{3,1},{1,0},{8,9},{10,8},{12,1... | collective-permute-start | bytes 1376264 | tf_op jit(solution)/shard_map/ppermute | solution.py:215
  21.2 9.7 %collective-permute-start.7 = (bf16[256,896]{1,0:T(8,128)(2,1)}, bf16[256,896]{1,0:T(8,128)(2,1)S(1)}, u32[]{:S(2)}, u32[]{:S(2)}) collective-permute-start(bf16[256,896]{1,0:T(8,128)(2,1)} %collective-permute-done.3.refs_0_), channel_id=1, source_target_pairs={{0,2},{2,4},{4,6},{6,7},{7,5},{5,3},{3,1},{1,0},{8,9},{10,8},{12,1... | collective-permute-start | bytes 1376264 | tf_op jit(solution)/shard_map/ppermute | solution.py:215
  26.0 9.8 %collective-permute-start.6 = (bf16[256,896]{1,0:T(8,128)(2,1)S(1)}, bf16[256,896]{1,0:T(8,128)(2,1)S(1)}, u32[]{:S(2)}, u32[]{:S(2)}) collective-permute-start(bf16[256,896]{1,0:T(8,128)(2,1)S(1)} %collective-permute-done.2.refs_1_), channel_id=1, source_target_pairs={{0,2},{2,4},{4,6},{6,7},{7,5},{5,3},{3,1},{1,0},{8,9},{10,8},{12,1... | collective-permute-start | bytes 1376264 | tf_op jit(solution)/shard_map/ppermute | solution.py:215
  30.9 9.9 %collective-permute-start.9 = (bf16[256,896]{1,0:T(8,128)(2,1)S(1)}, bf16[256,896]{1,0:T(8,128)(2,1)S(1)}, u32[]{:S(2)}, u32[]{:S(2)}) collective-permute-start(bf16[256,896]{1,0:T(8,128)(2,1)S(1)} %collective-permute-done.7.refs_0_), channel_id=1, source_target_pairs={{0,2},{2,4},{4,6},{6,7},{7,5},{5,3},{3,1},{1,0},{8,9},{10,8},{12,1... | collective-permute-start | bytes 1376264 | tf_op jit(solution)/shard_map/ppermute | solution.py:215
  33.0 4.9 %copy-start.3 = (bf16[256,896]{1,0:T(8,128)(2,1)S(1)}, bf16[256,896]{1,0:T(8,128)(2,1)}, u32[]{:S(2)}) copy-start(bf16[256,896]{1,0:T(8,128)(2,1)} %copy-done.2) | copy-start | bytes 1376260
  35.8 9.9 %collective-permute-start.8 = (bf16[256,896]{1,0:T(8,128)(2,1)S(1)}, bf16[256,896]{1,0:T(8,128)(2,1)S(1)}, u32[]{:S(2)}, u32[]{:S(2)}) collective-permute-start(bf16[256,896]{1,0:T(8,128)(2,1)S(1)} %collective-permute-done.6.refs_1_), channel_id=1, source_target_pairs={{0,2},{2,4},{4,6},{6,7},{7,5},{5,3},{3,1},{1,0},{8,9},{10,8},{12,1... | collective-permute-start | bytes 1376264 | tf_op jit(solution)/shard_map/ppermute | solution.py:215
  40.9 9.8 %collective-permute-start.11 = (bf16[256,896]{1,0:T(8,128)(2,1)S(1)}, bf16[256,896]{1,0:T(8,128)(2,1)}, u32[]{:S(2)}, u32[]{:S(2)}) collective-permute-start(bf16[256,896]{1,0:T(8,128)(2,1)S(1)} %collective-permute-done.9.refs_0_), channel_id=1, source_target_pairs={{0,2},{2,4},{4,6},{6,7},{7,5},{5,3},{3,1},{1,0},{8,9},{10,8},{12,1... | collective-permute-start | bytes 1376264 | tf_op jit(solution)/shard_map/ppermute | solution.py:215
  45.8 9.8 %collective-permute-start.10 = (bf16[256,896]{1,0:T(8,128)(2,1)S(1)}, bf16[256,896]{1,0:T(8,128)(2,1)}, u32[]{:S(2)}, u32[]{:S(2)}) collective-permute-start(bf16[256,896]{1,0:T(8,128)(2,1)S(1)} %collective-permute-done.8.refs_1_), channel_id=1, source_target_pairs={{0,2},{2,4},{4,6},{6,7},{7,5},{5,3},{3,1},{1,0},{8,9},{10,8},{12,1... | collective-permute-start | bytes 1376264 | tf_op jit(solution)/shard_map/ppermute | solution.py:215
  50.7 9.8 %collective-permute-start.15 = (bf16[256,896]{1,0:T(8,128)(2,1)}, bf16[256,896]{1,0:T(8,128)(2,1)}, u32[]{:S(2)}, u32[]{:S(2)}) collective-permute-start(bf16[256,896]{1,0:T(8,128)(2,1)} %collective-permute-done.11.refs_0_), channel_id=1, source_target_pairs={{0,2},{2,4},{4,6},{6,7},{7,5},{5,3},{3,1},{1,0},{8,9},{10,8},{12,1... | collective-permute-start | bytes 1376264 | tf_op jit(solution)/shard_map/ppermute | solution.py:215
  55.6 10.1 %collective-permute-start.17 = (bf16[256,896]{1,0:T(8,128)(2,1)}, bf16[256,896]{1,0:T(8,128)(2,1)}, u32[]{:S(2)}, u32[]{:S(2)}) collective-permute-start(bf16[256,896]{1,0:T(8,128)(2,1)} %collective-permute-done.10.refs_1_), channel_id=1, source_target_pairs={{0,2},{2,4},{4,6},{6,7},{7,5},{5,3},{3,1},{1,0},{8,9},{10,8},{12,1... | collective-permute-start | bytes 1376264 | tf_op jit(solution)/shard_map/ppermute | solution.py:215
  57.7 1.3 %collective-permute-start.12 = (f32[128,256]{1,0:T(8,128)S(1)}, f32[128,256]{1,0:T(8,128)S(1)}, u32[]{:S(2)}, u32[]{:S(2)}) collective-permute-start(f32[128,256]{1,0:T(8,128)S(1)} %shard_map.82.refs_0_), channel_id=1, source_target_pairs={{0,8},{8,0},{1,9},{9,1},{2,10},{10,2},{3,11},{11,3},{4,12},{12,4},... | collective-permute-start | bytes 393224 | tf_op jit(solution)/shard_map/ppermute | solution.py:254
  57.7 1.5 %collective-permute-start.14 = (f32[128,256]{1,0:T(8,128)S(1)}, f32[128,256]{1,0:T(8,128)S(1)}, u32[]{:S(2)}, u32[]{:S(2)}) collective-permute-start(f32[128,256]{1,0:T(8,128)S(1)} %shard_map.85.refs_2_), channel_id=1, source_target_pairs={{0,8},{8,0},{1,9},{9,1},{2,10},{10,2},{3,11},{11,3},{4,12},{12,4},... | collective-permute-start | bytes 393224 | tf_op jit(solution)/shard_map/ppermute | solution.py:254
  58.2 1.3 %collective-permute-start.13 = (f32[128,256]{1,0:T(8,128)S(1)}, f32[128,256]{1,0:T(8,128)S(1)}, u32[]{:S(2)}, u32[]{:S(2)}) collective-permute-start(f32[128,256]{1,0:T(8,128)S(1)} %shard_map.83.refs_1_), channel_id=1, source_target_pairs={{0,8},{8,0},{1,9},{9,1},{2,10},{10,2},{3,11},{11,3},{4,12},{12,4},... | collective-permute-start | bytes 393224 | tf_op jit(solution)/shard_map/ppermute | solution.py:254
  60.5 10.1 %collective-permute-start.16 = (bf16[256,896]{1,0:T(8,128)(2,1)}, bf16[256,896]{1,0:T(8,128)(2,1)S(1)}, u32[]{:S(2)}, u32[]{:S(2)}) collective-permute-start(bf16[256,896]{1,0:T(8,128)(2,1)} %collective-permute-done.15.refs_0_), channel_id=1, source_target_pairs={{0,2},{2,4},{4,6},{6,7},{7,5},{5,3},{3,1},{1,0},{8,9},{10,8},{12,1... | collective-permute-start | bytes 1376264 | tf_op jit(solution)/shard_map/ppermute | solution.py:215
  65.7 9.5 %collective-permute-start.18 = (bf16[256,896]{1,0:T(8,128)(2,1)}, bf16[256,896]{1,0:T(8,128)(2,1)S(1)}, u32[]{:S(2)}, u32[]{:S(2)}) collective-permute-start(bf16[256,896]{1,0:T(8,128)(2,1)} %collective-permute-done.17.refs_1_), channel_id=1, source_target_pairs={{0,2},{2,4},{4,6},{6,7},{7,5},{5,3},{3,1},{1,0},{8,9},{10,8},{12,1... | collective-permute-start | bytes 1376264 | tf_op jit(solution)/shard_map/ppermute | solution.py:215
  75.6 1.4 %collective-permute-start.19 = (bf16[256,256]{1,0:T(8,128)(2,1)S(1)}, bf16[256,256]{1,0:T(8,128)(2,1)S(1)}, u32[]{:S(2)}, u32[]{:S(2)}) collective-permute-start(bf16[256,256]{1,0:T(8,128)(2,1)S(1)} %shard_map.94.own_ref), channel_id=1, source_target_pairs={{0,8},{8,0},{1,9},{9,1},{2,10},{10,2},{3,11},{11,3},{4,12},{12,4},... | collective-permute-start | bytes 393224 | tf_op jit(solution)/shard_map/ppermute | solution.py:286
  76.1 1.5 %collective-permute-start.20 = (bf16[256,256]{1,0:T(8,128)(2,1)S(1)}, bf16[256,256]{1,0:T(8,128)(2,1)S(1)}, u32[]{:S(2)}, u32[]{:S(2)}) collective-permute-start(bf16[256,256]{1,0:T(8,128)(2,1)S(1)} %shard_map.96.own_ref), channel_id=1, source_target_pairs={{0,8},{8,0},{1,9},{9,1},{2,10},{10,2},{3,11},{11,3},{4,12},{12,4},... | collective-permute-start | bytes 393224 | tf_op jit(solution)/shard_map/ppermute | solution.py:286
